TPU v7x, 128 devices: a whole 4x4x4 slice. The times are simulated.
128 devices in a mesh: dom: 16 (over z, y_lo, core), bead: 8 (over y_hi, x).
Axes of the slice: x: 4, y: 4 (y_hi: 2, y_lo: 2; y = y_hi * 2 + y_lo), z: 4, core: 2. Of those that a mesh axis runs over, the one named last changes fastest.
Arguments:
- positions: float32 [8, 3, 8192], P('bead', None, 'dom'), may hold values from -6 to 6
- velocities: float32 [8, 3, 8192], P('bead', None, 'dom'), may hold values from -6 to 6
- species: int32 [8192], P('dom'), may hold values from 0 to 1
- neighbours: int32 [32, 8192], P(None, 'dom'), may hold values from 0 to 767
- neighbour_count: int32 [8192], P('dom'), may hold values from 16 to 32, as said below
- send_lists: int32 [2, 2048], P(None, 'dom'), may hold values from 0 to 511
- projection: float32 [2, 3, 512], replicated, may hold values from -4 to 4
- phase_shift: float32 [2, 512], replicated, may hold values from -3.140625 to 3.140625
- points: bfloat16 [2, 2000, 512], P(None, 'bead'), may hold values from -0.25 to 0.25
- point_weights: bfloat16 [2, 2000], P(None, 'bead'), may hold values from -0.125 to 0.125
Outputs:
- new_positions: float32 [8, 3, 8192], P('bead', None, 'dom')
- new_velocities: float32 [8, 3, 8192], P('bead', None, 'dom')
Inputs may be any that keep to these rules, and one draw needn't show every extreme that they name: `neighbours`: slots below 512 are atoms of the domain itself, the next 128 the atoms received from the domain below, the last 128 those from the domain above; domains form a closed loop; entries past an atom's count are padding. `neighbour_count`: every domain has an atom with all 32 slots valid. `send_lists`: local atom numbers of the sending domain; an atom may be listed more than once.
All inputs are finite; a program needn't handle non-finite values.
Results may differ from a plain program's by a relative error of at most 0.019.
Values may be sent and summed in bfloat16 or wider, within the bound.
No kernel may reach another device: no remote copies, remote signals or barrier semaphores. Data moves between devices by JAX's collectives and lax.ppermute only.
A program may use at most 128 MiB of HBM per device.

v0:
```python
import jax
import jax.numpy as jnp
from jax import lax
from jax.sharding import PartitionSpec as P

NEIGH = 32
STEPS = 2


WIDTH = 1.5
DT = 0.1
KAPPA = 0.5
SLOT_BLOCK = 8


def passed_along(block, axis, distance):
    devices = range(lax.axis_size(axis))
    route = [((i - distance) % len(devices), i) for i in devices]
    return lax.ppermute(block, axis, route)


def pair_geometry(position, near, species_near, valid, projection, phase_shift):
    offset = near - position[:, None, :]
    weight = valid * jnp.exp(
        -(offset[0] ** 2 + offset[1] ** 2 + offset[2] ** 2) / (2.0 * WIDTH * WIDTH)
    )
    change = projection[1] - projection[0]
    phase = (
        phase_shift[0][None, :, None]
        + species_near[:, None, :] * (phase_shift[1] - phase_shift[0])[None, :, None]
    )
    coeffs = []
    for axis_id in range(3):
        coeff = (
            projection[0][axis_id][None, :, None]
            + species_near[:, None, :] * change[axis_id][None, :, None]
        )
        phase = phase + coeff * offset[axis_id][:, None, :]
        coeffs.append(coeff)
    return (offset, weight, phase, coeffs)


def kernel_gradient(q_low, species, kernel_points, kernel_weights):
    count = kernel_points.shape[1]
    flat = kernel_points.reshape(2 * count, kernel_points.shape[2])
    u = jnp.dot(flat, q_low, preferred_element_type=jnp.float32)
    row_species = jnp.arange(2 * count, dtype=jnp.int32) // count
    scale = 2.0 * kernel_weights.reshape(2 * count).astype(jnp.float32)
    coefficient = jnp.where(
        row_species[:, None] == species[None, :], scale[:, None] * u, 0.0
    ).astype(jnp.bfloat16)
    return lax.dot_general(
        flat, coefficient, (((0,), (0,)), ((), ())), preferred_element_type=jnp.float32
    )


def ghost_rows(packed, send_lists):
    going_down = jnp.take(packed, send_lists[0], axis=1)
    going_up = jnp.take(packed, send_lists[1], axis=1)
    from_lower = passed_along(going_up, "dom", 1)
    from_upper = passed_along(going_down, "dom", -1)
    return (from_lower, from_upper)


def ghost_return(force_all, send_lists, atoms):
    ghosts = send_lists.shape[1]
    lower_back = force_all[:, atoms : atoms + ghosts]
    upper_back = force_all[:, atoms + ghosts :]
    back_from_lower = passed_along(upper_back, "dom", 1)
    back_from_upper = passed_along(lower_back, "dom", -1)
    own = force_all[:, :atoms]
    own = own.at[:, send_lists[0]].add(back_from_lower)
    return own.at[:, send_lists[1]].add(back_from_upper)


def chain_difference(position):
    before = passed_along(position, "bead", 1)
    after = passed_along(position, "bead", -1)
    return 2.0 * position - before - after


def shards(
    positions,
    velocities,
    species,
    neighbours,
    neighbour_count,
    send_lists,
    projection,
    phase_shift,
    points,
    point_weights,
):
    position = positions[0]
    velocity = velocities[0]
    atoms = position.shape[1]
    features = points.shape[2]
    species_value = species.astype(jnp.float32)
    mass = jnp.where(species == 0, 16.0, 1.0).astype(jnp.float32)
    slots = jnp.arange(NEIGH, dtype=jnp.int32)
    full_points, full_weights = (
        lax.all_gather(points, "bead", axis=1, tiled=True),
        lax.all_gather(point_weights, "bead", axis=1, tiled=True),
    )
    for step in range(STEPS):
        packed = jnp.concatenate([position, species_value[None]], axis=0)
        from_lower, from_upper = ghost_rows(packed, send_lists)
        near_all = jnp.concatenate([packed, from_lower, from_upper], axis=1)
        descriptor = jnp.zeros((features, atoms), jnp.float32)
        for start in range(0, NEIGH, SLOT_BLOCK):
            index = neighbours[start : start + SLOT_BLOCK]
            valid = (slots[start : start + SLOT_BLOCK][:, None] < neighbour_count[None, :]).astype(
                jnp.float32
            )
            near = jnp.take(near_all, index, axis=1)
            offset, weight, phase, coeffs = pair_geometry(
                position, near[:3], near[3], valid, projection, phase_shift
            )
            descriptor = descriptor + jnp.sum(weight[:, None, :] * jnp.cos(phase), axis=0)
        q_low = descriptor.astype(jnp.bfloat16)
        gradient = kernel_gradient(q_low, species, full_points, full_weights)
        force_all = jnp.zeros((3, near_all.shape[1]), jnp.float32)
        for start in range(0, NEIGH, SLOT_BLOCK):
            index = neighbours[start : start + SLOT_BLOCK]
            valid = (slots[start : start + SLOT_BLOCK][:, None] < neighbour_count[None, :]).astype(
                jnp.float32
            )
            near = jnp.take(near_all, index, axis=1)
            offset, weight, phase, coeffs = pair_geometry(
                position, near[:3], near[3], valid, projection, phase_shift
            )
            with_sin = gradient[None] * jnp.sin(phase)
            along = jnp.sum(gradient[None] * jnp.cos(phase), axis=1)
            pair_terms = jnp.stack(
                [
                    -weight
                    * (jnp.sum(with_sin * coeffs[a], axis=1) + along * offset[a] / (WIDTH * WIDTH))
                    for a in range(3)
                ]
            )
            force_all = force_all.at[:, :atoms].add(jnp.sum(pair_terms, axis=1))
            force_all = force_all.at[:, index].add(-pair_terms)
        potential = ghost_return(force_all, send_lists, atoms)
        total = potential - KAPPA * mass * chain_difference(position)
        velocity = velocity + DT * (total / mass)
        position = position + DT * velocity
    return (position[None], velocity[None])


def solution(mesh):
    placed = (
        P("bead", None, "dom"),
        P("bead", None, "dom"),
        P("dom"),
        P(None, "dom"),
        P("dom"),
        P(None, "dom"),
        P(),
        P(),
        P(None, "bead", None),
        P(None, "bead"),
    )
    return jax.shard_map(
        shards,
        mesh=mesh,
        in_specs=placed,
        out_specs=(P("bead", None, "dom"), P("bead", None, "dom")),
        check_vma=False,
    )
```

profile of v0, /device:TPU:6, one launch (start us, length us, event | category | flops | bytes accessed | tf_op | source)
XLA Modules:
  0.0 999.1 jit_solution(3469277847476804373)
XLA Ops:
  9.3 4.8 collective-permute-start.4
  17.8 4.0 collective-permute-start.1
  25.7 18.1 %all-gather = bf16[8,250,2]{1,2,0:T(2,128)(2,1)S(1)} all-gather(bf16[1,250,2]{1,2,0:T(2,128)(2,1)} %bitcast.579), channel_id=1, replica_groups=mesh['dom'=16,'bead'=8] {'bead'}, dimensions={0}, use_global_device_ids=true | all-gather | bytes 9000 | tf_op jit(solution)/shard_map/all_gather | solution.py:103
  49.9 10.8 %gather_fusion.4 = f32[4096,4]{1,0:T(8,128)S(1)} fusion(f32[4,768]{0,1:T(8,128)S(1)} %copy.195, s32[4096]{0:T(1024)S(1)} %broadcast_clamp_fusion.1), kind=kCustom, calls=%fused_computation.6.clone | custom fusion | bytes 147456 | tf_op jit(solution)/shard_map/jit(_take)/gather | solution.py:115
  61.3 10.8 %gather_fusion.5 = f32[4096,4]{1,0:T(8,128)S(1)} fusion(f32[4,768]{0,1:T(8,128)S(1)} %copy.195, s32[4096]{0:T(1024)S(1)} %broadcast_clamp_fusion), kind=kCustom, calls=%fused_computation.7.clone | custom fusion | bytes 147456 | tf_op jit(solution)/shard_map/jit(_take)/gather | solution.py:115
  72.7 10.8 %gather_fusion.3 = f32[4096,4]{1,0:T(8,128)S(1)} fusion(f32[4,768]{0,1:T(8,128)S(1)} %copy.195, s32[4096]{0:T(1024)S(1)} %broadcast_clamp_fusion.2), kind=kCustom, calls=%fused_computation.5.clone | custom fusion | bytes 147456 | tf_op jit(solution)/shard_map/jit(_take)/gather | solution.py:115
  84.2 10.8 %gather_fusion.2 = f32[4096,4]{1,0:T(8,128)S(1)} fusion(f32[4,768]{0,1:T(8,128)S(1)} %copy.195, s32[4096]{0:T(1024)S(1)} %broadcast_clamp_fusion.3), kind=kCustom, calls=%fused_computation.1.clone | custom fusion | bytes 147456 | tf_op jit(solution)/shard_map/jit(_take)/gather | solution.py:128
  96.6 63.9 %multiply_reduce_fusion.39 = (f32[512,512]{1,0:T(8,128)S(1)}, f32[512,512]{1,0:T(8,128)}) fusion(f32[8,512]{1,0:T(8,128)S(1)} %get-tuple-element.291, f32[8,512]{1,0:T(8,128)S(1)} %get-tuple-element.256, f32[512]{0:T(512)S(1)} %bitcast.563, f32[512]{0:T(512)S(1)} %bitcast.539, f32[8,512]{1,0:T(8,128)S(1)} %get-tuple-element.257, f32[512]{0:T(512)S(1)} %bitcast.571, ...), kind=kLoop, calls=%fused_computation.101 | loop fusion | flops 66584576 | bytes 2277376 | tf_op jit(solution)/shard_map/reduce_sum | solution.py:119
  160.5 64.6 %multiply_reduce_fusion.38 = (f32[512,512]{1,0:T(8,128)}, f32[512,512]{1,0:T(8,128)}) fusion(f32[8,512]{1,0:T(8,128)S(1)} %get-tuple-element.289, f32[8,512]{1,0:T(8,128)S(1)} %get-tuple-element.250, f32[512]{0:T(512)S(1)} %bitcast.564, f32[512]{0:T(512)S(1)} %bitcast.540, f32[8,512]{1,0:T(8,128)S(1)} %get-tuple-element.251, f32[512]{0:T(512)S(1)} %bitcast.572, ...), kind=kLoop, calls=%fused_computation.96 | loop fusion | flops 66584576 | bytes 2277376 | tf_op jit(solution)/shard_map/reduce_sum | solution.py:119
  225.2 4.7 copy.204
  229.9 9.1 fusion.12
  239.4 72.0 %multiply_reduce_fusion.27 = (f32[8,512]{1,0:T(8,128)S(1)}, f32[8,512]{1,0:T(8,128)S(1)}, f32[8,512]{1,0:T(8,128)S(1)}, f32[8,512]{1,0:T(8,128)S(1)}, f32[8,512]...) fusion(f32[512,512]{1,0:T(8,128)S(1)} %copy.205, ...), kind=kLoop, calls=%fused_computation.74 | loop fusion | flops 96436224 | bytes 1327104 | tf_op jit(solution)/shard_map/reduce_sum | solution.py:137
  311.5 85.4 %multiply_reduce_fusion.23 = (f32[8,512]{1,0:T(8,128)S(1)}, f32[8,512]{1,0:T(8,128)S(1)}, f32[8,512]{1,0:T(8,128)S(1)}, f32[8,512]{1,0:T(8,128)}, f32[8,512]{1,0...) fusion(f32[512,512]{1,0:T(8,128)S(1)} %copy.205, ...), kind=kLoop, calls=%fused_computation.69 | loop fusion | flops 96436224 | bytes 1327104 | tf_op jit(solution)/shard_map/reduce_sum | solution.py:137
  405.3 22.7 %scatter_fusion = f32[3,768]{0,1:T(8,128)S(1)} fusion(f32[3,768]{0,1:T(8,128)S(1)} %scatter-add.124, s32[4096]{0:T(1024)} %bitcast.509, f32[4096,3]{1,0:T(8,128)S(1)} %bitcast.492), kind=kCustom, calls=%fused_computation.12 | custom fusion | flops 12288 | bytes 163840 | tf_op jit(solution)/shard_map/scatter-add | solution.py:142
  428.8 22.8 %scatter_fusion.1 = f32[3,768]{0,1:T(8,128)S(1)} fusion(f32[3,768]{0,1:T(8,128)S(1)} %fusion.14, s32[4096]{0:T(1024)} %bitcast.506, f32[4096,3]{1,0:T(8,128)} %bitcast.493), kind=kCustom, calls=%fused_computation.13 | custom fusion | flops 12288 | bytes 163840 | tf_op jit(solution)/shard_map/scatter-add | solution.py:142
  452.4 22.8 %scatter_fusion.2 = f32[3,768]{0,1:T(8,128)S(1)} fusion(f32[3,768]{0,1:T(8,128)S(1)} %fusion.15, s32[4096]{0:T(1024)} %bitcast.503, f32[4096,3]{1,0:T(8,128)} %bitcast.495), kind=kCustom, calls=%fused_computation.14 | custom fusion | flops 12288 | bytes 163840 | tf_op jit(solution)/shard_map/scatter-add | solution.py:142
  476.1 22.8 %scatter_fusion.3 = f32[3,768]{0,1:T(8,128)S(1)} fusion(f32[3,768]{0,1:T(8,128)S(1)} %fusion.16, s32[4096]{0:T(1024)S(1)} %bitcast.500, f32[4096,3]{1,0:T(8,128)} %bitcast.498), kind=kCustom, calls=%fused_computation.15 | custom fusion | flops 12288 | bytes 163840 | tf_op jit(solution)/shard_map/scatter-add | solution.py:142
  516.9 4.4 collective-permute-start.10
  522.2 10.8 %gather_fusion.9 = f32[4096,4]{1,0:T(8,128)S(1)} fusion(f32[4,768]{0,1:T(8,128)S(1)} %copy.219, s32[4096]{0:T(1024)S(1)} %copy-done.12), kind=kCustom, calls=%fused_computation.9.clone | custom fusion | bytes 147456 | tf_op jit(solution)/shard_map/jit(_take)/gather | solution.py:115
  533.0 14.1 %gather_fusion.8 = f32[4096,4]{1,0:T(8,128)} fusion(f32[4,768]{0,1:T(8,128)S(1)} %copy.219, s32[4096]{0:T(1024)S(1)} %copy-done.14), kind=kCustom, calls=%fused_computation.8.clone | custom fusion | bytes 147456 | tf_op jit(solution)/shard_map/jit(_take)/gather | solution.py:128
  547.1 14.1 %gather_fusion.11 = f32[4096,4]{1,0:T(8,128)} fusion(f32[4,768]{0,1:T(8,128)S(1)} %copy.219, s32[4096]{0:T(1024)S(1)} %copy-done.10), kind=kCustom, calls=%fused_computation.11.clone | custom fusion | bytes 147456 | tf_op jit(solution)/shard_map/jit(_take)/gather | solution.py:115
  561.2 14.1 %gather_fusion.10 = f32[4096,4]{1,0:T(8,128)} fusion(f32[4,768]{0,1:T(8,128)S(1)} %copy.219, s32[4096]{0:T(1024)S(1)} %copy-done.8), kind=kCustom, calls=%fused_computation.10.clone | custom fusion | bytes 147456 | tf_op jit(solution)/shard_map/jit(_take)/gather | solution.py:115
  581.7 63.9 %multiply_reduce_fusion.17 = (f32[512,512]{1,0:T(8,128)S(1)}, f32[512,512]{1,0:T(8,128)}) fusion(f32[8,512]{1,0:T(8,128)S(1)} %get-tuple-element.280, f32[8,512]{1,0:T(8,128)S(1)} %get-tuple-element.236, f32[512]{0:T(512)S(1)} %bitcast.567, f32[512]{0:T(512)S(1)} %bitcast.543, f32[8,512]{1,0:T(8,128)S(1)} %get-tuple-element.237, f32[512]{0:T(512)S(1)} %bitcast.575, ...), kind=kLoop, calls=%fused_computation.51 | loop fusion | flops 66584576 | bytes 2277376 | tf_op jit(solution)/shard_map/reduce_sum | solution.py:119
  645.6 64.7 %multiply_reduce_fusion.18 = (f32[512,512]{1,0:T(8,128)}, f32[512,512]{1,0:T(8,128)}) fusion(f32[8,512]{1,0:T(8,128)S(1)} %get-tuple-element.281, f32[8,512]{1,0:T(8,128)S(1)} %get-tuple-element.230, f32[512]{0:T(512)S(1)} %bitcast.568, f32[512]{0:T(512)S(1)} %bitcast.544, f32[8,512]{1,0:T(8,128)S(1)} %get-tuple-element.231, f32[512]{0:T(512)S(1)} %bitcast.576, ...), kind=kLoop, calls=%fused_computation.56 | loop fusion | flops 66584576 | bytes 2277376 | tf_op jit(solution)/shard_map/reduce_sum | solution.py:119
  710.4 9.2 fusion.13
  719.9 73.9 %multiply_reduce_fusion.7 = (f32[8,512]{1,0:T(8,128)S(1)}, f32[8,512]{1,0:T(8,128)S(1)}, f32[8,512]{1,0:T(8,128)S(1)}, f32[8,512]{1,0:T(8,128)S(1)}, f32[8,512]{...) fusion(f32[512,512]{1,0:T(8,128)S(1)} %copy.227, ...), kind=kLoop, calls=%fused_computation.34 | loop fusion | flops 96436224 | bytes 1327104 | tf_op jit(solution)/shard_map/reduce_sum | solution.py:137
  793.8 85.1 %multiply_reduce_fusion.3 = (f32[8,512]{1,0:T(8,128)S(1)}, f32[8,512]{1,0:T(8,128)S(1)}, f32[8,512]{1,0:T(8,128)S(1)}, f32[8,512]{1,0:T(8,128)S(1)}, f32[8,512]{...) fusion(f32[512,512]{1,0:T(8,128)S(1)} %copy.227, ...), kind=kLoop, calls=%fused_computation.29 | loop fusion | flops 96436224 | bytes 1327104 | tf_op jit(solution)/shard_map/reduce_sum | solution.py:137
  887.1 22.5 %scatter_fusion.4 = f32[3,768]{0,1:T(8,128)S(1)} fusion(f32[3,768]{0,1:T(8,128)S(1)} %scatter-add.134, s32[4096]{0:T(1024)S(1)} %bitcast.510, f32[4096,3]{1,0:T(8,128)S(1)} %bitcast.491), kind=kCustom, calls=%fused_computation.18 | custom fusion | flops 12288 | bytes 163840 | tf_op jit(solution)/shard_map/scatter-add | solution.py:142
  910.5 22.8 %scatter_fusion.5 = f32[3,768]{0,1:T(8,128)S(1)} fusion(f32[3,768]{0,1:T(8,128)S(1)} %fusion.17, s32[4096]{0:T(1024)S(1)} %bitcast.507, f32[4096,3]{1,0:T(8,128)} %bitcast.494), kind=kCustom, calls=%fused_computation.19 | custom fusion | flops 12288 | bytes 163840 | tf_op jit(solution)/shard_map/scatter-add | solution.py:142
  934.1 22.8 %scatter_fusion.6 = f32[3,768]{0,1:T(8,128)S(1)} fusion(f32[3,768]{0,1:T(8,128)S(1)} %fusion.18, s32[4096]{0:T(1024)S(1)} %bitcast.504, f32[4096,3]{1,0:T(8,128)} %bitcast.496), kind=kCustom, calls=%fused_computation.20 | custom fusion | flops 12288 | bytes 163840 | tf_op jit(solution)/shard_map/scatter-add | solution.py:142
  957.7 22.8 %scatter_fusion.7 = f32[3,768]{0,1:T(8,128)S(1)} fusion(f32[3,768]{0,1:T(8,128)S(1)} %fusion.19, s32[4096]{0:T(1024)S(1)} %bitcast.501, f32[4096,3]{1,0:T(8,128)} %bitcast.497), kind=kCustom, calls=%fused_computation.21 | custom fusion | flops 12288 | bytes 163840 | tf_op jit(solution)/shard_map/scatter-add | solution.py:142
  980.7 3.8 collective-permute-start.9
  (305 shorter events, 73.3 us)
Async XLA Ops:
  7.2 218.0 %all-gather.3.cloned.1.call-start = ((), (), s32[]{:S(2)}) async-start(), calls=%async_computation | async-start | bytes 4608000 | tf_op jit(solution)/shard_map/all_gather | solution.py:102
  8.5 499.7 %collective-permute-start.5 = (f32[3,512]{1,0:T(4,128)}, f32[3,512]{1,0:T(4,128)}, u32[]{:S(2)}, u32[]{:S(2)}) collective-permute-start(f32[3,512]{1,0:T(4,128)} %bitcast.479), channel_id=1, source_target_pairs={{1,0},{2,1},{3,2},{4,3},{5,4},{6,5},{7,6},{0,7},{9,8},{10,9},{11,1... | collective-permute-start | bytes 18440 | tf_op jit(solution)/shard_map/ppermute | solution.py:19
  9.3 498.8 %collective-permute-start.4 = (f32[3,512]{1,0:T(4,128)}, f32[3,512]{1,0:T(4,128)}, u32[]{:S(2)}, u32[]{:S(2)}) collective-permute-start(f32[3,512]{1,0:T(4,128)} %bitcast.479), channel_id=1, source_target_pairs={{7,0},{0,1},{1,2},{2,3},{3,4},{4,5},{5,6},{6,7},{15,8},{8,9},{9,10... | collective-permute-start | bytes 18440 | tf_op jit(solution)/shard_map/ppermute | solution.py:19
  17.8 31.1 %collective-permute-start.1 = (f32[4,128]{1,0:T(4,128)S(1)}, f32[4,128]{1,0:T(4,128)S(1)}, u32[]{:S(2)}, u32[]{:S(2)}) collective-permute-start(f32[4,128]{1,0:T(4,128)S(1)} %select_bitcast_fusion.10), channel_id=1, source_target_pairs={{8,0},{16,8},{24,16},{32,24},{40,32},{48,40},{56,48},{64,56},{72,6... | collective-permute-start | bytes 6152 | tf_op jit(solution)/shard_map/ppermute | solution.py:19
  22.5 26.4 %collective-permute-start = (f32[4,128]{1,0:T(4,128)S(1)}, f32[4,128]{1,0:T(4,128)S(1)}, u32[]{:S(2)}, u32[]{:S(2)}) collective-permute-start(f32[4,128]{1,0:T(4,128)S(1)} %select_bitcast_fusion.11), channel_id=1, source_target_pairs={{120,0},{0,8},{8,16},{16,24},{24,32},{32,40},{40,48},{48,56},{56,6... | collective-permute-start | bytes 6152 | tf_op jit(solution)/shard_map/ppermute | solution.py:19
  25.7 285.7 %copy-start.52 = (f32[1,1,512]{2,0,1:T(1,128)}, f32[1,1,512]{2,0,1:T(1,128)S(1)}, u32[]{:S(2)}) copy-start(f32[1,1,512]{2,0,1:T(1,128)S(1)} %get-tuple-element.258) | copy-start | bytes 6148
  25.7 285.7 %copy-start.54 = (f32[1,1,512]{2,0,1:T(1,128)}, f32[1,1,512]{2,0,1:T(1,128)S(1)}, u32[]{:S(2)}) copy-start(f32[1,1,512]{2,0,1:T(1,128)S(1)} %get-tuple-element.259) | copy-start | bytes 6148
  25.7 285.7 %copy-start.56 = (f32[1,1,512]{2,0,1:T(1,128)}, f32[1,1,512]{2,0,1:T(1,128)S(1)}, u32[]{:S(2)}) copy-start(f32[1,1,512]{2,0,1:T(1,128)S(1)} %get-tuple-element.260) | copy-start | bytes 6148
  45.7 265.7 %copy-start.58 = (f32[1,1,512]{2,0,1:T(1,128)}, f32[1,1,512]{2,0,1:T(1,128)S(1)}, u32[]{:S(2)}) copy-start(f32[1,1,512]{2,0,1:T(1,128)S(1)} %get-tuple-element.269) | copy-start | bytes 6148
  45.7 265.7 %copy-start.60 = (f32[1,1,512]{2,0,1:T(1,128)}, f32[1,1,512]{2,0,1:T(1,128)S(1)}, u32[]{:S(2)}) copy-start(f32[1,1,512]{2,0,1:T(1,128)S(1)} %get-tuple-element.270) | copy-start | bytes 6148
  45.7 265.7 %copy-start.62 = (f32[1,1,512]{2,0,1:T(1,128)}, f32[1,1,512]{2,0,1:T(1,128)S(1)}, u32[]{:S(2)}) copy-start(f32[1,1,512]{2,0,1:T(1,128)S(1)} %get-tuple-element.271) | copy-start | bytes 6148
  46.5 265.0 %copy-start.44 = (f32[1,512]{1,0:T(1,128)}, f32[1,512]{1,0:T(1,128)S(1)}, u32[]{:S(2)}) copy-start(f32[1,512]{1,0:T(1,128)S(1)} %get-tuple-element.272) | copy-start | bytes 6148
  47.8 182.1 %copy-start.29 = (s32[4000]{0:T(1024)}, s32[4000]{0:T(1024)S(1)}, u32[]{:S(2)}) copy-start(s32[4000]{0:T(1024)S(1)} %add_select_fusion.6) | copy-start | bytes 48004
  48.0 181.9 %copy-start.31 = (f32[4000]{0:T(1024)}, f32[4000]{0:T(1024)S(1)}, u32[]{:S(2)}) copy-start(f32[4000]{0:T(1024)S(1)} %mul.541) | copy-start | bytes 48004
  48.1 349.8 %copy-start.34 = (s32[8]{0:T(128)}, s32[8]{0:T(128)S(1)}, u32[]{:S(2)}) copy-start(s32[8]{0:T(128)S(1)} %slice.321) | copy-start | bytes 100
  48.1 349.8 %copy-start.36 = (s32[8]{0:T(128)}, s32[8]{0:T(128)S(1)}, u32[]{:S(2)}) copy-start(s32[8]{0:T(128)S(1)} %slice.314) | copy-start | bytes 100
  48.2 349.7 %copy-start.38 = (s32[8]{0:T(128)}, s32[8]{0:T(128)S(1)}, u32[]{:S(2)}) copy-start(s32[8]{0:T(128)S(1)} %slice.328) | copy-start | bytes 100
  48.2 263.3 %copy-start.50 = (f32[512]{0:T(512)}, f32[512]{0:T(512)S(1)}, u32[]{:S(2)}) copy-start(f32[512]{0:T(512)S(1)} %sub.52) | copy-start | bytes 6148
  96.5 300.4 %copy-start.40 = (s32[32]{0:T(128)}, s32[32]{0:T(128)S(1)}, u32[]{:S(2)}) copy-start(s32[32]{0:T(128)S(1)} %iota.27) | copy-start | bytes 388
  405.3 116.9 %copy-start.12 = (s32[4096]{0:T(1024)S(1)}, s32[4096]{0:T(1024)}, u32[]{:S(2)}) copy-start(s32[4096]{0:T(1024)} %copy-done.11) | copy-start | bytes 49156
  428.0 105.0 %copy-start.14 = (s32[4096]{0:T(1024)S(1)}, s32[4096]{0:T(1024)}, u32[]{:S(2)}) copy-start(s32[4096]{0:T(1024)} %copy-done.13) | copy-start | bytes 49156
  428.8 118.3 %copy-start.10 = (s32[4096]{0:T(1024)S(1)}, s32[4096]{0:T(1024)}, u32[]{:S(2)}) copy-start(s32[4096]{0:T(1024)} %copy-done.9) | copy-start | bytes 49156
  451.6 109.6 %copy-start.8 = (s32[4096]{0:T(1024)S(1)}, s32[4096]{0:T(1024)}, u32[]{:S(2)}) copy-start(s32[4096]{0:T(1024)} %copy-done.7) | copy-start | bytes 49156
  498.9 6.4 collective-permute-start.2
  499.0 7.7 collective-permute-start.3
  512.6 8.7 collective-permute-start.7
  515.3 6.0 collective-permute-start.6
  515.3 474.7 %collective-permute-start.11 = (f32[3,512]{1,0:T(4,128)S(1)}, f32[3,512]{1,0:T(4,128)}, u32[]{:S(2)}, u32[]{:S(2)}) collective-permute-start(f32[3,512]{1,0:T(4,128)S(1)} %get-tuple-element.176), channel_id=1, source_target_pairs={{1,0},{2,1},{3,2},{4,3},{5,4},{6,5},{7,6},{0,7},{9,8},{10,9},{11,1... | collective-permute-start | bytes 18440 | tf_op jit(solution)/shard_map/ppermute | solution.py:19
  516.9 473.1 %collective-permute-start.10 = (f32[3,512]{1,0:T(4,128)S(1)}, f32[3,512]{1,0:T(4,128)}, u32[]{:S(2)}, u32[]{:S(2)}) collective-permute-start(f32[3,512]{1,0:T(4,128)S(1)} %get-tuple-element.176), channel_id=1, source_target_pairs={{7,0},{0,1},{1,2},{2,3},{3,4},{4,5},{5,6},{6,7},{15,8},{8,9},{9,10... | collective-permute-start | bytes 18440 | tf_op jit(solution)/shard_map/ppermute | solution.py:19
  887.1 103.0 %copy-start.28 = (f32[512]{0:T(512)S(1)}, f32[512]{0:T(512)}, u32[]{:S(2)}) copy-start(f32[512]{0:T(512)} %get-tuple-element.283) | copy-start | bytes 6148
  980.6 6.4 collective-permute-start.8
  980.7 7.8 collective-permute-start.9
  (47 other events, 1331.6 us)
Sparse Core Ops, SparseCore 0:
  14.3 70.9 all-gather.2
where the time goes:
time: 1010 us; the launch traced here: 999 us
  other arithmetic  782 us (77%)
  local copies, waits for them, and re-layouts  135 us (13%)
  starting transfers between devices  25.4 us (3%)
  matrix products  18.3 us (2%)
  blocking collectives  18.1 us (2%)
  between operations  15.7 us (2%)
    reduce_sum x4, other arithmetic, shards(): jnp.sum(with_sin * coeffs[a], axis=1) + along * offset[a] / (WIDTH * WIDTH)  316 us
    reduce_sum x4, other arithmetic, shards(): jnp.sum(weight[:, None, :] * jnp.cos(phase), axis=0)  257 us
    scatter-add x8, other arithmetic, shards(): force_all = force_all.at[:, index].add(-pair_terms)  182 us
    gather x16, local copies, waits for them, and re-layouts, shards(): near = jnp.take(near_all, index, axis=1)  105 us
    ppermute x12, starting transfers between devices, passed_along(): return lax.ppermute(block, axis, route)  25.4 us
  transfers between devices with their start and end apart: 13, of which 2 were waited for; matrix products, arithmetic and copies ran while one was open for 93% of the time, Pallas kernels for 0%

commit v1 on v0

v1 whole, which is shorter than its diff:
```python
import functools

import jax
import jax.numpy as jnp
from jax import lax
from jax.experimental import pallas as pl
from jax.experimental.pallas import tpu as pltpu
from jax.sharding import PartitionSpec as P

NEIGH = 32
STEPS = 2

WIDTH = 1.5
DT = 0.1
KAPPA = 0.5

F32, BF16 = jnp.float32, jnp.bfloat16
LANES = 128
ROWS = 16
FB = 256
TURN = 0.15915494309189535
SIN = (3.1415927410125732, -5.167710304260254, 2.550077438354492, -0.5982903838157654, 0.07765591144561768)
COS = (0.9999999403953552, -4.934792995452881, 4.05841064453125, -1.3318729400634766, 0.21968242526054382)
VMEM = pl.BlockSpec(memory_space=pltpu.VMEM)
PARAMS = pltpu.CompilerParams(vmem_limit_bytes=60 * 1024 * 1024)


def call(body, outs, scratch=()):
    return pl.pallas_call(
        body,
        out_shape=outs,
        out_specs=jax.tree.map(lambda _: VMEM, outs),
        scratch_shapes=scratch,
        compiler_params=PARAMS,
    )


def cos_sin(turns):
    f = turns - jnp.round(turns)
    g = f * f
    s, c = SIN[-1], COS[-1]
    for low in SIN[-2::-1]:
        s = s * g + low
    for low in COS[-2::-1]:
        c = c * g + low
    s = s * f
    twice = s + s
    return 1.0 - twice * s, twice * c


def count_kernel(neighbours_ref, count_ref, number_ref, named):
    slot = lax.broadcasted_iota(jnp.int32, neighbours_ref.shape, 0)
    named[...] = jnp.where(slot < count_ref[...], neighbours_ref[...], -1)
    rows = 32
    atoms = neighbours_ref.shape[1]

    def chunk(c, carry):
        first = pl.multiple_of(c * rows, rows)
        local = lax.broadcasted_iota(jnp.int32, (rows, atoms), 0) + first
        total = jnp.zeros((rows, atoms), F32)
        for k in range(NEIGH):
            total = total + jnp.where(local == named[k : k + 1, :], 1.0, 0.0)
        number_ref[pl.ds(first, rows), :] = total
        return carry

    lax.fori_loop(0, number_ref.shape[0] // rows, chunk, 0)


def gather_rows(columns, list_row, count):
    atoms, listed = columns.shape[0], list_row.shape[1]
    hit = lax.broadcasted_iota(jnp.int32, (atoms, listed), 0) == list_row
    return [
        jnp.sum(jnp.where(hit, columns[:, a : a + 1], 0.0), axis=0, keepdims=True)
        for a in range(count)
    ]


def send_rows(position_rows, species_row, lists_ref, down_ref, up_ref, wide):
    wide[...] = jnp.zeros_like(wide)
    for a in range(3):
        wide[a : a + 1, :] = position_rows[a]
    wide[3:4, :] = species_row
    columns = wide[...].T
    for out, which in ((down_ref, 0), (up_ref, 1)):
        for a, row in enumerate(gather_rows(columns, lists_ref[which : which + 1, :], 4)):
            out[a : a + 1, :] = row


def first_kernel(position_ref, species_ref, lists_ref, down_ref, up_ref, wide):
    rows = [position_ref[0, a : a + 1, :] for a in range(3)]
    send_rows(rows, species_ref[...].astype(F32), lists_ref, down_ref, up_ref, wide)


def update_kernel(
    last,
    force_ref,
    back_lower_ref,
    back_upper_ref,
    lists_ref,
    position_ref,
    velocity_ref,
    before_ref,
    after_ref,
    species_ref,
    new_position_ref,
    new_velocity_ref,
    *rest,
):
    atoms = position_ref.shape[2]
    listed = lists_ref.shape[1]
    wide = rest[-1]
    extra = [0.0, 0.0, 0.0]
    back = rest[-2]
    for which, ref in ((0, back_lower_ref), (1, back_upper_ref)):
        back[...] = jnp.zeros_like(back)
        back[0:3, :] = ref[...]
        values = back[...].T
        back[0:1, :] = lists_ref[which : which + 1, :].astype(F32)
        names = back[...].T[:, 0:1]
        hit = lax.broadcasted_iota(jnp.int32, (listed, atoms), 1).astype(F32) == names
        for a in range(3):
            extra[a] = extra[a] + jnp.sum(
                jnp.where(hit, values[:, a : a + 1], 0.0), axis=0, keepdims=True
            )
    species = species_ref[...]
    mass = jnp.where(species == 0, 16.0, 1.0)
    rows = []
    for a in range(3):
        here = position_ref[0, a : a + 1, :]
        chain = 2.0 * here - before_ref[0, a : a + 1, :] - after_ref[0, a : a + 1, :]
        total = force_ref[a : a + 1, 0:atoms] + extra[a] - KAPPA * mass * chain
        velocity = velocity_ref[0, a : a + 1, :] + DT * (total / mass)
        place = here + DT * velocity
        new_velocity_ref[0, a : a + 1, :] = velocity
        new_position_ref[0, a : a + 1, :] = place
        rows.append(place)
    if not last:
        send_rows(rows, species.astype(F32), lists_ref, rest[0], rest[1], wide)


def force_kernel(
    position_ref,
    species_ref,
    lower_ref,
    upper_ref,
    number_ref,
    projection_ref,
    shift_ref,
    matrix_ref,
    force_ref,
    near,
    cols,
    weight,
    weight_low,
    weight_turned,
    waves,
    turned,
    sums,
    sines,
    low,
    grad,
    spread,
    product,
    back,
    parts,
):
    own = position_ref.shape[2]
    ghosts = lower_ref.shape[1]
    everyone = own + 2 * ghosts
    features = projection_ref.shape[2]
    blocks = features // FB

    near[...] = jnp.zeros_like(near)
    near[0:3, 0:own] = position_ref[0]
    near[3:4, 0:own] = species_ref[...].astype(F32)
    near[0:4, own : own + ghosts] = lower_ref[...]
    near[0:4, own + ghosts : everyone] = upper_ref[...]
    cols[...] = near[...].T

    here = [near[a : a + 1, 0:own] for a in range(3)]

    def weigh(c, carry):
        rows = pl.ds(pl.multiple_of(c * ROWS, ROWS), ROWS)
        there = cols[rows, :]
        square = 0.0
        for a in range(3):
            d = there[:, a : a + 1] - here[a]
            square = square + d * d
        w = number_ref[rows, :] * jnp.exp(square * (-1.0 / (2.0 * WIDTH * WIDTH)))
        weight[rows, :] = w
        weight_low[rows, :] = w.astype(BF16)
        return carry

    lax.fori_loop(0, everyone // ROWS, weigh, 0, unroll=2)
    weight_turned[...] = weight[...].T.astype(BF16)

    shift_cos, shift_sin = cos_sin(shift_ref[...] * TURN)

    for block in range(blocks):
        mine = slice(block * FB, (block + 1) * FB)
        base = block * 4 * FB
        wave = [
            [projection_ref[s, a : a + 1, mine] * TURN for a in range(3)] for s in range(2)
        ]
        turn_cos = [shift_cos[s : s + 1, mine] for s in range(2)]
        turn_sin = [shift_sin[s : s + 1, mine] for s in range(2)]

        def own_waves(c, carry):
            rows = pl.ds(pl.multiple_of(c * ROWS, ROWS), ROWS)
            there = cols[rows, :]
            x, y, z = (jnp.broadcast_to(there[:, a : a + 1], (ROWS, FB)) for a in range(3))
            second = jnp.broadcast_to(there[:, 3:4], (ROWS, FB)) > 0.5
            for s in range(2):
                cos, sin = cos_sin(x * wave[s][0] + y * wave[s][1] + z * wave[s][2])
                at = base + s * 2 * FB
                turned[rows, at : at + FB] = turn_cos[s] * cos + turn_sin[s] * sin
                turned[rows, at + FB : at + 2 * FB] = turn_sin[s] * cos - turn_cos[s] * sin
                if s == 0:
                    cos, sin = jnp.where(second, 0.0, cos), jnp.where(second, 0.0, sin)
                else:
                    cos, sin = jnp.where(second, cos, 0.0), jnp.where(second, sin, 0.0)
                waves[rows, at : at + FB] = cos.astype(BF16)
                waves[rows, at + FB : at + 2 * FB] = sin.astype(BF16)
            return carry

        lax.fori_loop(0, own // ROWS, own_waves, 0)

        def ghost_waves(c, carry):
            rows = pl.ds(pl.multiple_of(own + c * ROWS, ROWS), ROWS)
            there = cols[rows, :]
            x, y, z = (jnp.broadcast_to(there[:, a : a + 1], (ROWS, FB)) for a in range(3))
            second = jnp.broadcast_to(there[:, 3:4], (ROWS, FB)) > 0.5
            px, py, pz = (jnp.where(second, wave[1][a], wave[0][a]) for a in range(3))
            cos, sin = cos_sin(x * px + y * py + z * pz)
            for s in range(2):
                at = base + s * 2 * FB
                for k, part in enumerate((cos, sin)):
                    if s == 0:
                        part = jnp.where(second, 0.0, part)
                    else:
                        part = jnp.where(second, part, 0.0)
                    waves[rows, at + k * FB : at + (k + 1) * FB] = part.astype(BF16)
            return carry

        lax.fori_loop(0, 2 * ghosts // ROWS, ghost_waves, 0)

        sums[...] = jnp.dot(
            weight_turned[...], waves[:, base : base + 4 * FB], preferred_element_type=F32
        )

        def describe(c, carry):
            rows = pl.ds(pl.multiple_of(c * ROWS, ROWS), ROWS)
            total = 0.0
            for s in range(2):
                at = base + s * 2 * FB
                tr, ti = turned[rows, at : at + FB], turned[rows, at + FB : at + 2 * FB]
                ur = sums[rows, s * 2 * FB : s * 2 * FB + FB]
                ui = sums[rows, s * 2 * FB + FB : s * 2 * FB + 2 * FB]
                total = total + (tr * ur - ti * ui)
                first = s * features + block * FB
                sines[rows, first : first + FB] = tr * ui + ti * ur
            low[rows, mine] = total.astype(BF16)
            return carry

        lax.fori_loop(0, own // ROWS, describe, 0)

    species = cols[0:own, 3:4]
    grad[...] = jnp.where(
        species > 0.5,
        jnp.dot(low[...], matrix_ref[features : 2 * features, :], preferred_element_type=F32),
        jnp.dot(low[...], matrix_ref[0:features, :], preferred_element_type=F32),
    )

    parts[...] = jnp.zeros_like(parts)

    def fold(value):
        total = value[:, 0:LANES]
        for k in range(1, value.shape[1] // LANES):
            total = total + value[:, k * LANES : (k + 1) * LANES]
        return total

    for block in range(blocks):
        mine = slice(block * FB, (block + 1) * FB)
        base = block * 4 * FB
        raw = [[projection_ref[s, a : a + 1, mine] for a in range(3)] for s in range(2)]

        def spread_out(c, carry):
            rows = pl.ds(pl.multiple_of(c * ROWS, ROWS), ROWS)
            g = grad[rows, mine]
            first = block * FB
            t0 = g * sines[rows, first : first + FB]
            t1 = g * sines[rows, features + first : features + first + FB]
            for a in range(3):
                parts[a, rows, :] = parts[a, rows, :] - fold(t0 * raw[0][a] + t1 * raw[1][a])
            for s in range(2):
                at = base + s * 2 * FB
                spread[rows, at : at + FB] = (g * turned[rows, at : at + FB]).astype(BF16)
                spread[rows, at + FB : at + 2 * FB] = (
                    -g * turned[rows, at + FB : at + 2 * FB]
                ).astype(BF16)
            return carry

        lax.fori_loop(0, own // ROWS, spread_out, 0)
        back[...] = jnp.dot(
            weight_low[...], spread[:, base : base + 4 * FB], preferred_element_type=F32
        )

        def pull(c, carry):
            rows = pl.ds(pl.multiple_of(c * ROWS, ROWS), ROWS)
            second = jnp.broadcast_to(cols[rows, 3:4], (ROWS, FB)) > 0.5
            total = 0.0
            for s in range(2):
                at = base + s * 2 * FB
                er = waves[rows, at : at + FB].astype(F32)
                ei = waves[rows, at + FB : at + 2 * FB].astype(F32)
                vr = back[rows, s * 2 * FB : s * 2 * FB + FB]
                vi = back[rows, s * 2 * FB + FB : s * 2 * FB + 2 * FB]
                total = total + (ei * vr - er * vi)
            for a in range(3):
                coeff = jnp.where(second, raw[1][a], raw[0][a])
                parts[a, rows, :] = parts[a, rows, :] + fold(total * coeff)
            return carry

        lax.fori_loop(0, everyone // ROWS, pull, 0)

    product[...] = lax.dot_general(
        waves[...], spread[...], (((1,), (1,)), ((), ())), preferred_element_type=F32
    )

    def along(c, carry):
        rows = pl.ds(pl.multiple_of(c * ROWS, ROWS), ROWS)
        there = cols[rows, :]
        z = weight[rows, :] * product[rows, :] * (1.0 / (WIDTH * WIDTH))
        out = []
        for a in range(3):
            pull_a = z * (there[:, a : a + 1] - here[a])
            parts[a, rows, :] = parts[a, rows, :] + fold(pull_a)
            total = pull_a[0:8]
            for k in range(1, ROWS // 8):
                total = total + pull_a[8 * k : 8 * k + 8]
            out.append(carry[a] + total)
        return tuple(out)

    centre = lax.fori_loop(
        0,
        everyone // ROWS,
        along,
        tuple(jnp.zeros((8, own), F32) for _ in range(3)),
    )
    for a in range(3):
        row = jnp.sum(parts[a].T, axis=0, keepdims=True)
        force_ref[a : a + 1, 0:own] = row[:, 0:own] - jnp.sum(centre[a], axis=0, keepdims=True)
        force_ref[a : a + 1, own:everyone] = row[:, own:everyone]


def passed_along(block, axis, distance):
    devices = range(lax.axis_size(axis))
    route = [((i - distance) % len(devices), i) for i in devices]
    return lax.ppermute(block, axis, route)


def routed(block, axis, source):
    return lax.ppermute(block, axis, [(source(i), i) for i in range(lax.axis_size(axis))])


def kernel_matrix(points, point_weights):
    features = points.shape[2]
    dom, bead = lax.axis_index("dom"), lax.axis_index("bead")
    place = dom % 2 * 8 + dom // 4 * 2 + dom // 2 % 2
    which, height = place // 8, features // 8
    p = lax.dynamic_index_in_dim(points, which, 0, keepdims=False).astype(F32)
    w = lax.dynamic_index_in_dim(point_weights, which, 0, keepdims=False).astype(F32)
    left = lax.dynamic_slice_in_dim(p, place % 8 * height, height, axis=1)
    part = lax.dot_general(
        left * (2.0 * w)[:, None],
        p,
        (((0,), (0,)), ((), ())),
        precision=lax.Precision.HIGHEST,
        preferred_element_type=F32,
    )
    other = routed(part.astype(BF16), "bead", lambda i: i ^ 4)
    part = part + other.astype(F32)
    sent = part.astype(BF16)
    for k in (1, 2, 3):
        part = part + routed(sent, "bead", lambda i: i // 4 * 4 + (i - k) % 4).astype(F32)
    held = part.astype(BF16)
    other = routed(held, "dom", lambda i: i ^ 2)
    upper = dom // 2 % 2 == 1
    held = jnp.where(upper, jnp.concatenate([other, held]), jnp.concatenate([held, other]))
    rows = held.shape[0]
    pieces = [routed(held, "dom", lambda i: (i - 4 * k) % 16) for k in (3, 2, 1)] + [held]
    held = lax.dynamic_slice_in_dim(
        jnp.concatenate(pieces + pieces), (3 - dom // 4) % 4 * rows, 4 * rows, axis=0
    )
    other = routed(held, "dom", lambda i: i ^ 1)
    return jnp.where(
        dom % 2 == 1, jnp.concatenate([other, held]), jnp.concatenate([held, other])
    )


def shards(
    positions,
    velocities,
    species,
    neighbours,
    neighbour_count,
    send_lists,
    projection,
    phase_shift,
    points,
    point_weights,
):
    own, ghosts = positions.shape[2], send_lists.shape[1]
    everyone = own + 2 * ghosts
    features = points.shape[2]
    shape = jax.ShapeDtypeStruct
    species = species.reshape(1, own)
    sent = (shape((4, ghosts), F32),) * 2
    wide = pltpu.VMEM((LANES, own), F32)

    going_down, going_up = call(first_kernel, sent, [wide])(positions, species, send_lists)
    number = call(
        count_kernel, shape((everyone, own), F32), [pltpu.VMEM((NEIGH, own), jnp.int32)]
    )(neighbours, neighbour_count.reshape(1, own))
    matrix = kernel_matrix(points, point_weights)

    force_call = call(
        force_kernel,
        shape((3, everyone), F32),
        [
            pltpu.VMEM((LANES, everyone), F32),
            pltpu.VMEM((everyone, LANES), F32),
            pltpu.VMEM((everyone, own), F32),
            pltpu.VMEM((everyone, own), BF16),
            pltpu.VMEM((own, everyone), BF16),
            pltpu.VMEM((everyone, 4 * features), BF16),
            pltpu.VMEM((own, 4 * features), F32),
            pltpu.VMEM((own, 4 * FB), F32),
            pltpu.VMEM((own, 2 * features), F32),
            pltpu.VMEM((own, features), BF16),
            pltpu.VMEM((own, features), F32),
            pltpu.VMEM((own, 4 * features), BF16),
            pltpu.VMEM((everyone, own), F32),
            pltpu.VMEM((everyone, 4 * FB), F32),
            pltpu.VMEM((3, everyone, LANES), F32),
        ],
    )
    for step in range(STEPS):
        from_lower = passed_along(going_up, "dom", 1)
        from_upper = passed_along(going_down, "dom", -1)
        before = passed_along(positions, "bead", 1)
        after = passed_along(positions, "bead", -1)
        force = force_call(
            positions, species, from_lower, from_upper, number, projection, phase_shift, matrix
        )
        back_from_lower = passed_along(force[:, own + ghosts :], "dom", 1)
        back_from_upper = passed_along(force[:, own : own + ghosts], "dom", -1)
        last = step == STEPS - 1
        moved = shape(positions.shape, F32)
        positions, velocities, *sends = call(
            functools.partial(update_kernel, last),
            (moved, moved) + (() if last else sent),
            [pltpu.VMEM((LANES, ghosts), F32), wide],
        )(
            force,
            back_from_lower,
            back_from_upper,
            send_lists,
            positions,
            velocities,
            before,
            after,
            species,
        )
        if not last:
            going_down, going_up = sends
    return (positions, velocities)


def solution(mesh):
    placed = (
        P("bead", None, "dom"),
        P("bead", None, "dom"),
        P("dom"),
        P(None, "dom"),
        P("dom"),
        P(None, "dom"),
        P(),
        P(),
        P(None, "bead", None),
        P(None, "bead"),
    )
    return jax.shard_map(
        shards,
        mesh=mesh,
        in_specs=placed,
        out_specs=(P("bead", None, "dom"), P("bead", None, "dom")),
        check_vma=False,
    )
```

time: 1010 us -> 157 us (0.16); the launches traced: 999 us -> 157 us
  other arithmetic: 782 us -> 2.27 us
  local copies, waits for them, and re-layouts: 135 us -> 9.55 us
  Pallas kernels: 0 us -> 86 us
  waiting for transfers between devices: 4.15 us -> 23.2 us
  blocking collectives: 18.1 us -> 0 us
  matrix products: 18.3 us -> 0.37 us
  between operations: 15.7 us -> 0.93 us
    reduce_sum x8 -> x0, other arithmetic: 574 us -> none  [the longest x4 316 us: shards(): jnp.sum(with_sin * coeffs[a], axis=1) + along * offset[a] / (WIDTH * WIDTH)]
    scatter-add x18 -> x0, other arithmetic: 193 us -> none  [the longest x8 182 us: shards(): force_all = force_all.at[:, index].add(-pair_terms)]
    gather x24 -> x0, local copies, waits for them, and re-layouts: 108 us -> none  [the longest x16 105 us: shards(): near = jnp.take(near_all, index, axis=1)]
    pallas_call x0 -> x6, Pallas kernels: none -> 86 us  [the longest x2 72.7 us: shards(): force_call(positions, species, from_lower, from_upper, number, projection...]
    all_gather x1 -> x0, blocking collectives: 18.1 us -> none  [shards(): lax.all_gather(point_weights, 'bead', axis=1, tiled=True)]
    dot_general x2 -> x1, matrix products: 18.3 us -> 0.37 us  [kernel_matrix(): lax.dot_general(left * (2.0 * w)[:, None], p, (((0,), (0,)), ((), ())), p...]
    ppermute x0 -> x9, waiting for transfers between devices: none -> 14.6 us  [routed(): lax.ppermute(block, axis, [(source(i), i) for i in range(lax.axis_size(ax...]
    ppermute x0 -> x9, starting transfers between devices: none -> 14.5 us  [routed(): lax.ppermute(block, axis, [(source(i), i) for i in range(lax.axis_size(ax...]
  transfers between devices with their start and end apart: 13 -> 21, of which waited for: 2 -> 12; matrix products, arithmetic and copies ran while one was open for 93% -> 3% of each run, Pallas kernels for 0% -> 52%
where the time goes in v1:
time: 157 us
  Pallas kernels  86 us (55%)
  starting transfers between devices  34.6 us (22%)
  waiting for transfers between devices  23.2 us (15%)
  local copies, waits for them, and re-layouts  9.55 us (6%)
  other arithmetic  2.27 us (1%)
    pallas_call x2, Pallas kernels, shards(): force_call(positions, species, from_lower, from_upper, number, projection...  72.7 us
    ppermute x12, starting transfers between devices, passed_along(): return lax.ppermute(block, axis, route)  20.1 us
    ppermute x9, waiting for transfers between devices, routed(): lax.ppermute(block, axis, [(source(i), i) for i in range(lax.axis_size(ax...  14.6 us
    ppermute x9, starting transfers between devices, routed(): lax.ppermute(block, axis, [(source(i), i) for i in range(lax.axis_size(ax...  14.5 us
    ppermute x12, waiting for transfers between devices, passed_along(): return lax.ppermute(block, axis, route)  8.63 us
    pallas_call x1, Pallas kernels, shards(): call(count_kernel, shape((everyone, own), F32), [pltpu.VMEM((NEIGH, own),...  7.39 us
    unnamed x45, local copies, waits for them, and re-layouts  5.02 us
    pallas_call x2, Pallas kernels, shards(): call(functools.partial(update_kernel, last), (moved, moved) + (() if last...  4.06 us
  transfers between devices with their start and end apart: 21, of which 12 were waited for; matrix products, arithmetic and copies ran while one was open for 3% of the time, Pallas kernels for 52%

profile of v1, /device:TPU:6, one launch (start us, length us, event | category | flops | bytes accessed | tf_op | source)
XLA Modules:
  0.0 156.8 jit_solution(5357466595628099975)
XLA Ops:
  0.7 0.7 convert_multiply_fusion
  2.7 3.3 %collective-permute-start.2 = (bf16[64,512]{1,0:T(8,128)(2,1)S(1)}, bf16[64,512]{1,0:T(8,128)(2,1)S(1)}, u32[]{:S(2)}, u32[]{:S(2)}) collective-permute-start(bf16[64,512]{1,0:T(8,128)(2,1)S(1)} %get-tuple-element.22), channel_id=1, source_target_pairs={{4,0},{5,1},{6,2},{7,3},{0,4},{1,5},{2,6},{3,7},{12,8},{13,9},{14,... | collective-permute-start | bytes 196616 | tf_op jit(solution)/shard_map/ppermute | solution.py:363
  5.9 2.6 %collective-permute-done.2 = bf16[64,512]{1,0:T(8,128)(2,1)S(1)} collective-permute-done((bf16[64,512]{1,0:T(8,128)(2,1)S(1)}, bf16[64,512]{1,0:T(8,128)(2,1)S(1)}, u32[]{:S(2)}, u32[]{:S(2)}) %collective-permute-start.2) | collective-permute-done | bytes 65568 | tf_op jit(solution)/shard_map/ppermute | solution.py:363
  8.5 0.9 collective-permute-start.5
  9.4 1.0 collective-permute-start.4
  10.4 2.2 %collective-permute-start.3 = (bf16[64,512]{1,0:T(8,128)(2,1)S(1)}, bf16[64,512]{1,0:T(8,128)(2,1)S(1)}, u32[]{:S(2)}, u32[]{:S(2)}) collective-permute-start(bf16[64,512]{1,0:T(8,128)(2,1)S(1)} %fusion.3), channel_id=1, source_target_pairs={{3,0},{0,1},{1,2},{2,3},{7,4},{4,5},{5,6},{6,7},{11,8},{8,9},{9,10... | collective-permute-start | bytes 196616 | tf_op jit(solution)/shard_map/ppermute | solution.py:363
  12.6 1.4 collective-permute-done.5
  14.1 1.1 collective-permute-done.4
  15.7 1.7 %collective-permute-start.6 = (bf16[64,512]{1,0:T(8,128)(2,1)S(1)}, bf16[64,512]{1,0:T(8,128)(2,1)S(1)}, u32[]{:S(2)}, u32[]{:S(2)}) collective-permute-start(bf16[64,512]{1,0:T(8,128)(2,1)S(1)} %add_convert_fusion), channel_id=1, source_target_pairs={{16,0},{24,8},{0,16},{8,24},{48,32},{56,40},{32,48},{40,56},{80,64... | collective-permute-start | bytes 196616 | tf_op jit(solution)/shard_map/ppermute | solution.py:363
  17.3 2.7 %collective-permute-done.6 = bf16[64,512]{1,0:T(8,128)(2,1)S(1)} collective-permute-done((bf16[64,512]{1,0:T(8,128)(2,1)S(1)}, bf16[64,512]{1,0:T(8,128)(2,1)S(1)}, u32[]{:S(2)}, u32[]{:S(2)}) %collective-permute-start.6) | collective-permute-done | bytes 65568 | tf_op jit(solution)/shard_map/ppermute | solution.py:363
  20.0 4.1 %collective-permute-start.7 = (bf16[128,512]{1,0:T(8,128)(2,1)S(1)}, bf16[128,512]{1,0:T(8,128)(2,1)S(1)}, u32[]{:S(2)}, u32[]{:S(2)}) collective-permute-start(bf16[128,512]{1,0:T(8,128)(2,1)S(1)} %maximum_select_fusion.1), channel_id=1, source_target_pairs={{32,0},{40,8},{48,16},{56,24},{64,32},{72,40},{80,48},{88,56},{96,... | collective-permute-start | bytes 393224 | tf_op jit(solution)/shard_map/ppermute | solution.py:363
  24.2 1.3 collective-permute-start.9
  25.4 2.7 %collective-permute-done.7 = bf16[128,512]{1,0:T(8,128)(2,1)S(1)} collective-permute-done((bf16[128,512]{1,0:T(8,128)(2,1)S(1)}, bf16[128,512]{1,0:T(8,128)(2,1)S(1)}, u32[]{:S(2)}, u32[]{:S(2)}) %collective-permute-start.7) | collective-permute-done | bytes 131104 | tf_op jit(solution)/shard_map/ppermute | solution.py:363
  28.1 2.6 %collective-permute-done.8 = bf16[128,512]{1,0:T(8,128)(2,1)S(1)} collective-permute-done((bf16[128,512]{1,0:T(8,128)(2,1)S(1)}, bf16[128,512]{1,0:T(8,128)(2,1)S(1)}, u32[]{:S(2)}, u32[]{:S(2)}) %collective-permute-start.8) | collective-permute-done | bytes 131104 | tf_op jit(solution)/shard_map/ppermute | solution.py:363
  30.7 1.0 collective-permute-done.9
  32.0 1.4 collective-permute-start.14
  33.4 4.3 %collective-permute-start.13 = (f32[1,3,512]{2,1,0:T(4,128)S(1)}, f32[1,3,512]{2,1,0:T(4,128)S(1)}, u32[]{:S(2)}, u32[]{:S(2)}) collective-permute-start(f32[1,3,512]{2,1,0:T(4,128)S(1)} %copy.24.position_ref), channel_id=1, source_target_pairs={{7,0},{0,1},{1,2},{2,3},{3,4},{4,5},{5,6},{6,7},{15,8},{8,9},{9,10... | collective-permute-start | bytes 18440 | tf_op jit(solution)/shard_map/ppermute | solution.py:359
  37.7 1.8 %shard_map.113 = (f32[4,128]{1,0:T(4,128)}, f32[4,128]{1,0:T(4,128)}) custom-call(f32[1,3,512]{2,1,0:T(4,128)} %copy-done.1, s32[1,512]{1,0:T(1,128)} %bitcast.8, s32[2,128]{1,0:T(2,128)} %lists_ref.5), custom_call_target="tpu_custom_call" | custom-call | tf_op jit(solution)/shard_map/pallas_call | solution.py:421
  39.5 3.9 %collective-permute-start.1 = (f32[4,128]{1,0:T(4,128)}, f32[4,128]{1,0:T(4,128)S(1)}, u32[]{:S(2)}, u32[]{:S(2)}) collective-permute-start(f32[4,128]{1,0:T(4,128)} %get-tuple-element.9), channel_id=1, source_target_pairs={{8,0},{16,8},{24,16},{32,24},{40,32},{48,40},{56,48},{64,56},{72,6... | collective-permute-start | bytes 6152 | tf_op jit(solution)/shard_map/ppermute | solution.py:359
  44.0 7.4 %shard_map.114.number_ref = f32[768,512]{1,0:T(8,128)} custom-call(s32[32,512]{1,0:T(8,128)} %neighbours_ref.1, s32[1,512]{1,0:T(1,128)} %bitcast.14), custom_call_target="tpu_custom_call" | custom-call | tf_op jit(solution)/shard_map/pallas_call | solution.py:422
  51.4 1.4 maximum_select_fusion.matrix_ref
  54.0 36.4 %shard_map.115.force_ref = f32[3,768]{1,0:T(4,128)} custom-call(f32[1,3,512]{2,1,0:T(4,128)} %copy-done.1, s32[1,512]{1,0:T(1,128)} %bitcast.9, f32[4,128]{1,0:T(4,128)} %copy-done.9, f32[4,128]{1,0:T(4,128)} %copy-done.11, f32[768,512]{1,0:T(8,128)} %shard_map.114.number_ref, f32[2,3,512]{2,1,0:T(4,128)} %copy.25.projection_ref, f32[2,512]{1,0:T(2,128)} %shift_ref.3, ...), custom_call_target="tpu_custom_call" | custom-call | tf_op jit(solution)/shard_map/pallas_call | solution.py:453
  92.3 3.8 %collective-permute-done.11.back_lower_ref = f32[3,128]{1,0:T(4,128)S(1)} collective-permute-done((f32[3,128]{1,0:T(4,128)S(1)}, f32[3,128]{1,0:T(4,128)S(1)}, u32[]{:S(2)}, u32[]{:S(2)}) %collective-permute-start.11) | collective-permute-done | bytes 1568 | tf_op jit(solution)/shard_map/ppermute | solution.py:359
  96.7 2.3 %shard_map.116 = (f32[1,3,512]{2,1,0:T(4,128)}, f32[1,3,512]{2,1,0:T(4,128)}, f32[4,128]{1,0:T(4,128)}, f32[4,128]{1,0:T(4,128)}) custom-call(f32[3,768]{1,0:T(4,128)} %shard_map.115.force_ref, f32[3,128]{1,0:T(4,128)} %copy-done.15, f32[3,128]{1,0:T(4,128)} %copy-done.13, s32[2,128]{1,0:T(2,128)} %lists_ref.5, f32[1,3,512]{2,1,0:T(4,128)} %copy-done.1, ...), custom_call_target="tpu_custom_call" | custom-call | tf_op jit(solution)/shard_map/pallas_call | solution.py:460
  99.0 3.9 %collective-permute-start.16 = (f32[4,128]{1,0:T(4,128)}, f32[4,128]{1,0:T(4,128)S(1)}, u32[]{:S(2)}, u32[]{:S(2)}) collective-permute-start(f32[4,128]{1,0:T(4,128)} %get-tuple-element.12), channel_id=1, source_target_pairs={{8,0},{16,8},{24,16},{32,24},{40,32},{48,40},{56,48},{64,56},{72,6... | collective-permute-start | bytes 6152 | tf_op jit(solution)/shard_map/ppermute | solution.py:359
  102.8 5.6 %collective-permute-start.19 = (f32[1,3,512]{2,1,0:T(4,128)}, f32[1,3,512]{2,1,0:T(4,128)S(1)}, u32[]{:S(2)}, u32[]{:S(2)}) collective-permute-start(f32[1,3,512]{2,1,0:T(4,128)} %get-tuple-element.10.position_ref), channel_id=1, source_target_pairs={{7,0},{0,1},{1,2},{2,3},{3,4},{4,5},{5,6},{6,7},{15,8},{8,9},{9,10... | collective-permute-start | bytes 18440 | tf_op jit(solution)/shard_map/ppermute | solution.py:359
  109.6 36.4 %shard_map.117.force_ref = f32[3,768]{1,0:T(4,128)} custom-call(f32[1,3,512]{2,1,0:T(4,128)} %get-tuple-element.10.position_ref, s32[1,512]{1,0:T(1,128)} %bitcast.11, f32[4,128]{1,0:T(4,128)} %copy-done.10, f32[4,128]{1,0:T(4,128)} %copy-done.12, f32[768,512]{1,0:T(8,128)} %shard_map.114.number_ref, f32[2,3,512]{2,1,0:T(4,128)} %copy.25.projection_ref, ...), custom_call_target="tpu_custom_call" | custom-call | tf_op jit(solution)/shard_map/pallas_call | solution.py:453
  147.2 0.8 collective-permute-done.18.back_upper_ref
  148.0 3.8 %collective-permute-done.17.back_lower_ref = f32[3,128]{1,0:T(4,128)S(1)} collective-permute-done((f32[3,128]{1,0:T(4,128)S(1)}, f32[3,128]{1,0:T(4,128)S(1)}, u32[]{:S(2)}, u32[]{:S(2)}) %collective-permute-start.17) | collective-permute-done | bytes 1568 | tf_op jit(solution)/shard_map/ppermute | solution.py:359
  152.4 1.8 %shard_map.118 = (f32[1,3,512]{2,1,0:T(4,128)}, f32[1,3,512]{2,1,0:T(4,128)}) custom-call(f32[3,768]{1,0:T(4,128)} %shard_map.117.force_ref, f32[3,128]{1,0:T(4,128)} %copy-done.16, f32[3,128]{1,0:T(4,128)} %copy-done.14, s32[2,128]{1,0:T(2,128)} %lists_ref.5, f32[1,3,512]{2,1,0:T(4,128)} %get-tuple-element.10.position_ref, ...), custom_call_target="tpu_custom_call" | custom-call | tf_op jit(solution)/shard_map/pallas_call | solution.py:460
  154.2 1.3 copy.31
  155.5 1.3 copy.32
  (74 shorter events, 9.2 us)
Async XLA Ops:
  0.6 1.1 copy-start
  2.7 5.8 %collective-permute-start.2 = (bf16[64,512]{1,0:T(8,128)(2,1)S(1)}, bf16[64,512]{1,0:T(8,128)(2,1)S(1)}, u32[]{:S(2)}, u32[]{:S(2)}) collective-permute-start(bf16[64,512]{1,0:T(8,128)(2,1)S(1)} %get-tuple-element.22), channel_id=1, source_target_pairs={{4,0},{5,1},{6,2},{7,3},{0,4},{1,5},{2,6},{3,7},{12,8},{13,9},{14,... | collective-permute-start | bytes 196616 | tf_op jit(solution)/shard_map/ppermute | solution.py:363
  8.5 5.5 %collective-permute-start.5 = (bf16[64,512]{1,0:T(8,128)(2,1)S(1)}, bf16[64,512]{1,0:T(8,128)(2,1)S(1)}, u32[]{:S(2)}, u32[]{:S(2)}) collective-permute-start(bf16[64,512]{1,0:T(8,128)(2,1)S(1)} %fusion.3), channel_id=1, source_target_pairs={{1,0},{2,1},{3,2},{0,3},{5,4},{6,5},{7,6},{4,7},{9,8},{10,9},{11,1... | collective-permute-start | bytes 196616 | tf_op jit(solution)/shard_map/ppermute | solution.py:363
  9.4 5.8 %collective-permute-start.4 = (bf16[64,512]{1,0:T(8,128)(2,1)S(1)}, bf16[64,512]{1,0:T(8,128)(2,1)S(1)}, u32[]{:S(2)}, u32[]{:S(2)}) collective-permute-start(bf16[64,512]{1,0:T(8,128)(2,1)S(1)} %fusion.3), channel_id=1, source_target_pairs={{2,0},{3,1},{0,2},{1,3},{6,4},{7,5},{4,6},{5,7},{10,8},{11,9},{8,1... | collective-permute-start | bytes 196616 | tf_op jit(solution)/shard_map/ppermute | solution.py:363
  10.4 5.2 %collective-permute-start.3 = (bf16[64,512]{1,0:T(8,128)(2,1)S(1)}, bf16[64,512]{1,0:T(8,128)(2,1)S(1)}, u32[]{:S(2)}, u32[]{:S(2)}) collective-permute-start(bf16[64,512]{1,0:T(8,128)(2,1)S(1)} %fusion.3), channel_id=1, source_target_pairs={{3,0},{0,1},{1,2},{2,3},{7,4},{4,5},{5,6},{6,7},{11,8},{8,9},{9,10... | collective-permute-start | bytes 196616 | tf_op jit(solution)/shard_map/ppermute | solution.py:363
  15.7 4.3 %collective-permute-start.6 = (bf16[64,512]{1,0:T(8,128)(2,1)S(1)}, bf16[64,512]{1,0:T(8,128)(2,1)S(1)}, u32[]{:S(2)}, u32[]{:S(2)}) collective-permute-start(bf16[64,512]{1,0:T(8,128)(2,1)S(1)} %add_convert_fusion), channel_id=1, source_target_pairs={{16,0},{24,8},{0,16},{8,24},{48,32},{56,40},{32,48},{40,56},{80,64... | collective-permute-start | bytes 196616 | tf_op jit(solution)/shard_map/ppermute | solution.py:363
  20.0 8.0 %collective-permute-start.7 = (bf16[128,512]{1,0:T(8,128)(2,1)S(1)}, bf16[128,512]{1,0:T(8,128)(2,1)S(1)}, u32[]{:S(2)}, u32[]{:S(2)}) collective-permute-start(bf16[128,512]{1,0:T(8,128)(2,1)S(1)} %maximum_select_fusion.1), channel_id=1, source_target_pairs={{32,0},{40,8},{48,16},{56,24},{64,32},{72,40},{80,48},{88,56},{96,... | collective-permute-start | bytes 393224 | tf_op jit(solution)/shard_map/ppermute | solution.py:363
  24.2 6.6 %collective-permute-start.8 = (bf16[128,512]{1,0:T(8,128)(2,1)S(1)}, bf16[128,512]{1,0:T(8,128)(2,1)S(1)}, u32[]{:S(2)}, u32[]{:S(2)}) collective-permute-start(bf16[128,512]{1,0:T(8,128)(2,1)S(1)} %maximum_select_fusion.1), channel_id=1, source_target_pairs={{64,0},{72,8},{80,16},{88,24},{96,32},{104,40},{112,48},{120,56},{... | collective-permute-start | bytes 393224 | tf_op jit(solution)/shard_map/ppermute | solution.py:363
  24.2 7.8 %copy-start.7 = (f32[1,3,512]{2,0,1:T(1,128)S(1)}, f32[1,3,512]{2,0,1:T(1,128)}, u32[]{:S(2)}) copy-start(f32[1,3,512]{2,0,1:T(1,128)} %param.10) | copy-start | bytes 18436
  24.2 19.2 %copy-start.2 = (f32[2,3,512]{2,0,1:T(2,128)S(1)}, f32[2,3,512]{2,0,1:T(2,128)}, u32[]{:S(2)}) copy-start(f32[2,3,512]{2,0,1:T(2,128)} %param.16) | copy-start | bytes 36868
  24.2 7.6 %collective-permute-start.9 = (bf16[128,512]{1,0:T(8,128)(2,1)S(1)}, bf16[128,512]{1,0:T(8,128)(2,1)S(1)}, u32[]{:S(2)}, u32[]{:S(2)}) collective-permute-start(bf16[128,512]{1,0:T(8,128)(2,1)S(1)} %maximum_select_fusion.1), channel_id=1, source_target_pairs={{96,0},{104,8},{112,16},{120,24},{0,32},{8,40},{16,48},{24,56},{32... | collective-permute-start | bytes 393224 | tf_op jit(solution)/shard_map/ppermute | solution.py:363
  31.9 19.4 %collective-permute-start.10 = (bf16[512,512]{1,0:T(8,128)(2,1)S(1)}, bf16[512,512]{1,0:T(8,128)(2,1)S(1)}, u32[]{:S(2)}, u32[]{:S(2)}) collective-permute-start(bf16[512,512]{1,0:T(8,128)(2,1)S(1)} %constant_dynamic-slice_fusion), channel_id=1, source_target_pairs={{8,0},{0,8},{24,16},{16,24},{40,32},{32,40},{56,48},{48,56},{72,64... | collective-permute-start | bytes 1572872 | tf_op jit(solution)/shard_map/ppermute | solution.py:363
  32.0 5.7 %copy-start.1 = (f32[1,3,512]{2,1,0:T(4,128)}, f32[1,3,512]{2,1,0:T(4,128)S(1)}, u32[]{:S(2)}) copy-start(f32[1,3,512]{2,1,0:T(4,128)S(1)} %copy.24.position_ref) | copy-start | bytes 18436
  32.0 60.1 %collective-permute-start.14 = (f32[1,3,512]{2,1,0:T(4,128)S(1)}, f32[1,3,512]{2,1,0:T(4,128)S(1)}, u32[]{:S(2)}, u32[]{:S(2)}) collective-permute-start(f32[1,3,512]{2,1,0:T(4,128)S(1)} %copy.24.position_ref), channel_id=1, source_target_pairs={{1,0},{2,1},{3,2},{4,3},{5,4},{6,5},{7,6},{0,7},{9,8},{10,9},{11,1... | collective-permute-start | bytes 18440 | tf_op jit(solution)/shard_map/ppermute | solution.py:359
  33.4 58.7 %collective-permute-start.13 = (f32[1,3,512]{2,1,0:T(4,128)S(1)}, f32[1,3,512]{2,1,0:T(4,128)S(1)}, u32[]{:S(2)}, u32[]{:S(2)}) collective-permute-start(f32[1,3,512]{2,1,0:T(4,128)S(1)} %copy.24.position_ref), channel_id=1, source_target_pairs={{7,0},{0,1},{1,2},{2,3},{3,4},{4,5},{5,6},{6,7},{15,8},{8,9},{9,10... | collective-permute-start | bytes 18440 | tf_op jit(solution)/shard_map/ppermute | solution.py:359
  39.5 13.3 %collective-permute-start = (f32[4,128]{1,0:T(4,128)}, f32[4,128]{1,0:T(4,128)S(1)}, u32[]{:S(2)}, u32[]{:S(2)}) collective-permute-start(f32[4,128]{1,0:T(4,128)} %get-tuple-element.8), channel_id=1, source_target_pairs={{120,0},{0,8},{8,16},{16,24},{24,32},{32,40},{40,48},{48,56},{56,6... | collective-permute-start | bytes 6152 | tf_op jit(solution)/shard_map/ppermute | solution.py:359
  39.5 13.3 %collective-permute-start.1 = (f32[4,128]{1,0:T(4,128)}, f32[4,128]{1,0:T(4,128)S(1)}, u32[]{:S(2)}, u32[]{:S(2)}) collective-permute-start(f32[4,128]{1,0:T(4,128)} %get-tuple-element.9), channel_id=1, source_target_pairs={{8,0},{16,8},{24,16},{32,24},{40,32},{48,40},{56,48},{64,56},{72,6... | collective-permute-start | bytes 6152 | tf_op jit(solution)/shard_map/ppermute | solution.py:359
  52.8 38.7 %copy-start.8 = (f32[1,3,512]{2,0,1:T(1,128)S(1)}, f32[1,3,512]{2,0,1:T(1,128)}, u32[]{:S(2)}) copy-start(f32[1,3,512]{2,0,1:T(1,128)} %param.11) | copy-start | bytes 18436
  91.0 1.3 collective-permute-start.12
  91.0 5.1 %collective-permute-start.11 = (f32[3,128]{1,0:T(4,128)S(1)}, f32[3,128]{1,0:T(4,128)S(1)}, u32[]{:S(2)}, u32[]{:S(2)}) collective-permute-start(f32[3,128]{1,0:T(4,128)S(1)} %get-tuple-element.21), channel_id=1, source_target_pairs={{120,0},{0,8},{8,16},{16,24},{24,32},{32,40},{40,48},{48,56},{56,6... | collective-permute-start | bytes 4616 | tf_op jit(solution)/shard_map/ppermute | solution.py:359
  92.1 4.0 %copy-start.3 = (f32[1,3,512]{2,1,0:T(4,128)}, f32[1,3,512]{2,1,0:T(4,128)S(1)}, u32[]{:S(2)}) copy-start(f32[1,3,512]{2,1,0:T(4,128)S(1)} %collective-permute-done.14.after_ref) | copy-start | bytes 18436
  92.1 4.0 %copy-start.4 = (f32[1,3,512]{2,1,0:T(4,128)}, f32[1,3,512]{2,1,0:T(4,128)S(1)}, u32[]{:S(2)}) copy-start(f32[1,3,512]{2,1,0:T(4,128)S(1)} %collective-permute-done.13.before_ref) | copy-start | bytes 18436
  92.3 3.8 %copy-start.13 = (f32[3,128]{1,0:T(4,128)}, f32[3,128]{1,0:T(4,128)S(1)}, u32[]{:S(2)}) copy-start(f32[3,128]{1,0:T(4,128)S(1)} %collective-permute-done.12.back_upper_ref) | copy-start | bytes 4612
  99.0 9.5 %collective-permute-start.15 = (f32[4,128]{1,0:T(4,128)}, f32[4,128]{1,0:T(4,128)S(1)}, u32[]{:S(2)}, u32[]{:S(2)}) collective-permute-start(f32[4,128]{1,0:T(4,128)} %get-tuple-element.11), channel_id=1, source_target_pairs={{120,0},{0,8},{8,16},{16,24},{24,32},{32,40},{40,48},{48,56},{56,6... | collective-permute-start | bytes 6152 | tf_op jit(solution)/shard_map/ppermute | solution.py:359
  99.0 9.5 %collective-permute-start.16 = (f32[4,128]{1,0:T(4,128)}, f32[4,128]{1,0:T(4,128)S(1)}, u32[]{:S(2)}, u32[]{:S(2)}) collective-permute-start(f32[4,128]{1,0:T(4,128)} %get-tuple-element.12), channel_id=1, source_target_pairs={{8,0},{16,8},{24,16},{32,24},{40,32},{48,40},{56,48},{64,56},{72,6... | collective-permute-start | bytes 6152 | tf_op jit(solution)/shard_map/ppermute | solution.py:359
  102.8 49.0 %collective-permute-start.20 = (f32[1,3,512]{2,1,0:T(4,128)}, f32[1,3,512]{2,1,0:T(4,128)S(1)}, u32[]{:S(2)}, u32[]{:S(2)}) collective-permute-start(f32[1,3,512]{2,1,0:T(4,128)} %get-tuple-element.10.position_ref), channel_id=1, source_target_pairs={{1,0},{2,1},{3,2},{4,3},{5,4},{6,5},{7,6},{0,7},{9,8},{10,9},{11,1... | collective-permute-start | bytes 18440 | tf_op jit(solution)/shard_map/ppermute | solution.py:359
  102.8 49.0 %collective-permute-start.19 = (f32[1,3,512]{2,1,0:T(4,128)}, f32[1,3,512]{2,1,0:T(4,128)S(1)}, u32[]{:S(2)}, u32[]{:S(2)}) collective-permute-start(f32[1,3,512]{2,1,0:T(4,128)} %get-tuple-element.10.position_ref), channel_id=1, source_target_pairs={{7,0},{0,1},{1,2},{2,3},{3,4},{4,5},{5,6},{6,7},{15,8},{8,9},{9,10... | collective-permute-start | bytes 18440 | tf_op jit(solution)/shard_map/ppermute | solution.py:359
  146.7 1.3 collective-permute-start.18
  146.7 5.1 %collective-permute-start.17 = (f32[3,128]{1,0:T(4,128)S(1)}, f32[3,128]{1,0:T(4,128)S(1)}, u32[]{:S(2)}, u32[]{:S(2)}) collective-permute-start(f32[3,128]{1,0:T(4,128)S(1)} %get-tuple-element.19), channel_id=1, source_target_pairs={{120,0},{0,8},{8,16},{16,24},{24,32},{32,40},{40,48},{48,56},{56,6... | collective-permute-start | bytes 4616 | tf_op jit(solution)/shard_map/ppermute | solution.py:359
  148.0 3.8 %copy-start.14 = (f32[3,128]{1,0:T(4,128)}, f32[3,128]{1,0:T(4,128)S(1)}, u32[]{:S(2)}) copy-start(f32[3,128]{1,0:T(4,128)S(1)} %collective-permute-done.18.back_upper_ref) | copy-start | bytes 4612
  151.8 0.6 copy-start.5
  151.8 0.6 copy-start.6
  (6 other events, 3.5 us)

commit v2 on v1

v2 whole, which is shorter than its diff:
```python
import functools

import jax
import jax.numpy as jnp
from jax import lax
from jax.experimental import pallas as pl
from jax.experimental.pallas import tpu as pltpu
from jax.sharding import PartitionSpec as P

NEIGH = 32
STEPS = 2

WIDTH = 1.5
DT = 0.1
KAPPA = 0.5

F32, BF16 = jnp.float32, jnp.bfloat16
LANES = 128
ROWS = 32
FB = 256
TURN = 0.15915494309189535
SIN = (3.1415927410125732, -5.167710304260254, 2.550077438354492, -0.5982903838157654, 0.07765591144561768)
COS = (0.9999999403953552, -4.934792995452881, 4.05841064453125, -1.3318729400634766, 0.21968242526054382)
VMEM = pl.BlockSpec(memory_space=pltpu.VMEM)
MIB = 1024 * 1024
LIMIT = 16


def call(body, outs, scratch=(), limit=8):
    return pl.pallas_call(
        body,
        out_shape=outs,
        out_specs=jax.tree.map(lambda _: VMEM, outs),
        scratch_shapes=scratch,
        compiler_params=pltpu.CompilerParams(vmem_limit_bytes=limit * MIB),
    )


def cos_sin(turns):
    f = turns - jnp.round(turns)
    g = f * f
    s, c = SIN[-1], COS[-1]
    for low in SIN[-2::-1]:
        s = s * g + low
    for low in COS[-2::-1]:
        c = c * g + low
    s = s * f
    twice = s + s
    return 1.0 - twice * s, twice * c


def core_of():
    return lax.axis_index("dom") % 2


def count_kernel(part, neighbours_ref, count_ref, number_ref, named):
    slot = lax.broadcasted_iota(jnp.int32, neighbours_ref.shape, 0)
    named[...] = jnp.where(slot < count_ref[...], neighbours_ref[...], -1)
    rows, atoms = number_ref.shape
    ghosts = rows // 2
    core = core_of()

    def chunk(c, carry):
        start = pl.multiple_of(c * ROWS, ROWS)
        row = start + part * rows
        swap = jnp.where(core == 0, ghosts, 0)
        shift = jnp.where(row >= atoms + ghosts, -swap, jnp.where(row >= atoms, swap, 0))
        local = lax.broadcasted_iota(jnp.int32, (ROWS, atoms), 0) + (row + shift)
        total = jnp.zeros((ROWS, atoms), F32)
        for k in range(NEIGH):
            total = total + jnp.where(local == named[k : k + 1, :], 1.0, 0.0)
        number_ref[pl.ds(start, ROWS), :] = total
        return carry

    lax.fori_loop(0, rows // ROWS, chunk, 0)


def near_far_lists(lists_ref):
    core = core_of()
    return [lists_ref[pl.ds(1 - core, 1), :], lists_ref[pl.ds(core, 1), :]]


def gather_rows(columns, list_row, count):
    atoms, listed = columns.shape[0], list_row.shape[1]
    hit = lax.broadcasted_iota(jnp.int32, (atoms, listed), 0) == list_row
    return [
        jnp.sum(jnp.where(hit, columns[:, a : a + 1], 0.0), axis=0, keepdims=True)
        for a in range(count)
    ]


def send_rows(position_rows, species_row, lists, near_ref, far_ref, wide):
    wide[...] = jnp.zeros_like(wide)
    for a in range(3):
        wide[a : a + 1, :] = position_rows[a]
    wide[3:4, :] = species_row
    columns = wide[...].T
    for out, listed in zip((near_ref, far_ref), lists):
        for a, row in enumerate(gather_rows(columns, listed, 4)):
            out[a : a + 1, :] = row


def first_kernel(position_ref, species_ref, lists_ref, near_ref, far_ref, wide):
    rows = [position_ref[a] for a in range(3)]
    lists = near_far_lists(lists_ref)
    send_rows(rows, species_ref[...].astype(F32), lists, near_ref, far_ref, wide)


def update_kernel(
    last,
    force_ref,
    near_back_ref,
    far_back_ref,
    lists_ref,
    position_ref,
    velocity_ref,
    below_ref,
    above_ref,
    species_ref,
    new_position_ref,
    new_velocity_ref,
    *rest,
):
    atoms = position_ref.shape[2]
    listed = lists_ref.shape[1]
    wide = rest[-1]
    back = rest[-2]
    lists = near_far_lists(lists_ref)
    extra = [0.0, 0.0, 0.0]
    for names, ref in zip(lists, (near_back_ref, far_back_ref)):
        back[...] = jnp.zeros_like(back)
        back[0:3, :] = ref[...]
        back[3:4, :] = names.astype(F32)
        values = back[...].T
        hit = lax.broadcasted_iota(jnp.int32, (listed, atoms), 1).astype(F32) == values[:, 3:4]
        for a in range(3):
            extra[a] = extra[a] + jnp.sum(
                jnp.where(hit, values[:, a : a + 1], 0.0), axis=0, keepdims=True
            )
    species = species_ref[...]
    mass = jnp.where(species == 0, 16.0, 1.0)
    rows = []
    for a in range(3):
        here = position_ref[a]
        chain = 2.0 * here - below_ref[a] - above_ref[a]
        total = force_ref[a : a + 1, :] + extra[a] - KAPPA * mass * chain
        velocity = velocity_ref[a] + DT * (total / mass)
        place = here + DT * velocity
        new_velocity_ref[a] = velocity
        new_position_ref[a] = place
        rows.append(place)
    if not last:
        send_rows(rows, species.astype(F32), lists, rest[0], rest[1], wide)


def each(count, body, unroll=4, carry=0):
    return lax.fori_loop(0, count // ROWS, body, carry, unroll=min(unroll, count // ROWS))


def chunk_rows(c, first=0):
    return pl.ds(pl.multiple_of(first + c * ROWS, ROWS), ROWS)


def own_kernel(
    position_ref,
    species_ref,
    projection_ref,
    shift_ref,
    cols,
    waves,
    turned,
    rows_in,
):
    own = position_ref.shape[2]
    features = projection_ref.shape[2]
    rows_in[...] = jnp.zeros_like(rows_in)
    for a in range(3):
        rows_in[a : a + 1, :] = position_ref[a]
    rows_in[3:4, :] = species_ref[...].astype(F32)
    cols[...] = rows_in[...].T

    shift_cos, shift_sin = cos_sin(shift_ref[...] * TURN)
    for block in range(features // FB):
        mine = slice(block * FB, (block + 1) * FB)
        base = block * 4 * FB
        wave = [
            [projection_ref[a, s : s + 1, mine] * TURN for a in range(3)] for s in range(2)
        ]
        turn_cos = [shift_cos[s : s + 1, mine] for s in range(2)]
        turn_sin = [shift_sin[s : s + 1, mine] for s in range(2)]

        def own_waves(c, carry):
            rows = chunk_rows(c)
            there = cols[rows, :]
            x, y, z = (jnp.broadcast_to(there[:, a : a + 1], (ROWS, FB)) for a in range(3))
            second = jnp.broadcast_to(there[:, 3:4], (ROWS, FB)) > 0.5
            for s in range(2):
                cos, sin = cos_sin(x * wave[s][0] + y * wave[s][1] + z * wave[s][2])
                at = base + s * 2 * FB
                turned[rows, at : at + FB] = turn_cos[s] * cos + turn_sin[s] * sin
                turned[rows, at + FB : at + 2 * FB] = turn_sin[s] * cos - turn_cos[s] * sin
                if s == 0:
                    cos, sin = jnp.where(second, 0.0, cos), jnp.where(second, 0.0, sin)
                else:
                    cos, sin = jnp.where(second, cos, 0.0), jnp.where(second, sin, 0.0)
                waves[rows, at : at + FB] = cos.astype(BF16)
                waves[rows, at + FB : at + 2 * FB] = sin.astype(BF16)
            return carry

        each(own, own_waves)


def weigh_kernel(
    position_ref,
    near_ref,
    far_ref,
    own_cols,
    projection_ref,
    *rest,
):
    *numbers, ghost_cols, weight, weight_turned, waves, rows_in = rest
    own = position_ref.shape[2]
    sent = near_ref.shape[1]
    features = projection_ref.shape[2]

    rows_in[...] = jnp.zeros_like(rows_in)
    rows_in[0:4, 0:sent] = near_ref[...]
    rows_in[0:4, sent : 2 * sent] = far_ref[...]
    ghost_cols[...] = rows_in[...].T
    here = [position_ref[a] for a in range(3)]

    for k, number_ref in enumerate(numbers):
        first = k * number_ref.shape[0]
        cols, skip = (own_cols, first) if first < own else (ghost_cols, first - own)

        def weigh(c, carry):
            there = cols[chunk_rows(c, skip), :]
            square = 0.0
            for a in range(3):
                d = there[:, a : a + 1] - here[a]
                square = square + d * d
            weight[chunk_rows(c, first), :] = number_ref[chunk_rows(c), :] * jnp.exp(
                square * (-1.0 / (2.0 * WIDTH * WIDTH))
            )
            return carry

        each(number_ref.shape[0], weigh)
    weight_turned[...] = weight[...].T.astype(BF16)

    for block in range(features // FB):
        mine = slice(block * FB, (block + 1) * FB)
        base = block * 4 * FB
        wave = [
            [projection_ref[a, s : s + 1, mine] * TURN for a in range(3)] for s in range(2)
        ]

        def ghost_waves(c, carry):
            rows = chunk_rows(c)
            there = ghost_cols[rows, :]
            x, y, z = (jnp.broadcast_to(there[:, a : a + 1], (ROWS, FB)) for a in range(3))
            second = jnp.broadcast_to(there[:, 3:4], (ROWS, FB)) > 0.5
            px, py, pz = (jnp.where(second, wave[1][a], wave[0][a]) for a in range(3))
            cos, sin = cos_sin(x * px + y * py + z * pz)
            for s in range(2):
                at = base + s * 2 * FB
                for k, part in enumerate((cos, sin)):
                    if s == 0:
                        part = jnp.where(second, 0.0, part)
                    else:
                        part = jnp.where(second, part, 0.0)
                    waves[rows, at + k * FB : at + (k + 1) * FB] = part.astype(BF16)
            return carry

        each(2 * sent, ghost_waves)


def describe_kernel(
    weight_turned,
    own_waves,
    ghost_waves,
    turned,
    sines,
    low,
    sums,
):
    own = weight_turned.shape[0]
    features = low.shape[1]
    for block in range(features // FB):
        mine = slice(block * FB, (block + 1) * FB)
        base = block * 4 * FB
        sums[...] = jnp.dot(
            weight_turned[:, 0:own], own_waves[:, base : base + 4 * FB], preferred_element_type=F32
        ) + jnp.dot(
            weight_turned[:, own:], ghost_waves[:, base : base + 4 * FB], preferred_element_type=F32
        )

        def describe(c, carry):
            rows = chunk_rows(c)
            total = 0.0
            for s in range(2):
                at = base + s * 2 * FB
                tr, ti = turned[rows, at : at + FB], turned[rows, at + FB : at + 2 * FB]
                ur = sums[rows, s * 2 * FB : s * 2 * FB + FB]
                ui = sums[rows, s * 2 * FB + FB : s * 2 * FB + 2 * FB]
                total = total + (tr * ur - ti * ui)
                first = s * features + block * FB
                sines[rows, first : first + FB] = tr * ui + ti * ur
            low[rows, mine] = total.astype(BF16)
            return carry

        each(own, describe)


def fold(value):
    total = value[:, 0:LANES]
    for k in range(1, value.shape[1] // LANES):
        total = total + value[:, k * LANES : (k + 1) * LANES]
    return total


def pull_rows(first, cols, waves, weight, spread, projection_ref, here, parts, back, product):
    count = cols.shape[0]
    features = projection_ref.shape[2]
    held = weight[first : first + count, :].astype(BF16)
    for block in range(features // FB):
        mine = slice(block * FB, (block + 1) * FB)
        base = block * 4 * FB
        raw = [[projection_ref[a, s : s + 1, mine] for a in range(3)] for s in range(2)]
        back[...] = jnp.dot(held, spread[:, base : base + 4 * FB], preferred_element_type=F32)

        def pull(c, carry):
            rows = chunk_rows(c)
            second = jnp.broadcast_to(cols[rows, 3:4], (ROWS, FB)) > 0.5
            total = 0.0
            for s in range(2):
                at = base + s * 2 * FB
                er = waves[rows, at : at + FB].astype(F32)
                ei = waves[rows, at + FB : at + 2 * FB].astype(F32)
                vr = back[rows, s * 2 * FB : s * 2 * FB + FB]
                vi = back[rows, s * 2 * FB + FB : s * 2 * FB + 2 * FB]
                total = total + (ei * vr - er * vi)
            for a in range(3):
                coeff = jnp.where(second, raw[1][a], raw[0][a])
                parts[a, rows, :] = parts[a, rows, :] + fold(total * coeff)
            return carry

        each(count, pull)

    product[...] = lax.dot_general(
        waves[...], spread[...], (((1,), (1,)), ((), ())), preferred_element_type=F32
    )

    def along(c, carry):
        rows = chunk_rows(c)
        there = cols[rows, :]
        z = weight[chunk_rows(c, first), :] * product[rows, :] * (1.0 / (WIDTH * WIDTH))
        out = []
        for a in range(3):
            pull_a = z * (there[:, a : a + 1] - here[a])
            parts[a, rows, :] = parts[a, rows, :] + fold(pull_a)
            total = pull_a[0:8]
            for k in range(1, ROWS // 8):
                total = total + pull_a[8 * k : 8 * k + 8]
            out.append(carry[a] + total)
        return tuple(out)

    start = tuple(jnp.zeros((8, here[0].shape[1]), F32) for _ in range(3))
    return each(count, along, carry=start)


def ghost_force_kernel(
    low,
    half_ref,
    other_ref,
    own_cols,
    turned,
    weight,
    waves,
    cols,
    position_ref,
    projection_ref,
    grad,
    spread,
    centre_ref,
    near_ref,
    far_ref,
    back,
    product,
    parts,
):
    own, features = grad.shape
    sent = near_ref.shape[1]
    here = [position_ref[a] for a in range(3)]
    mine_is = core_of().astype(F32)
    grad[...] = jnp.where(
        own_cols[:, 3:4] == mine_is,
        jnp.dot(low[...], half_ref[...], preferred_element_type=F32),
        jnp.dot(low[...], other_ref[...], preferred_element_type=F32),
    )
    for block in range(features // FB):
        mine = slice(block * FB, (block + 1) * FB)
        base = block * 4 * FB

        def spread_out(c, carry):
            rows = chunk_rows(c)
            g = grad[rows, mine]
            for s in range(2):
                at = base + s * 2 * FB
                spread[rows, at : at + FB] = (g * turned[rows, at : at + FB]).astype(BF16)
                spread[rows, at + FB : at + 2 * FB] = (
                    -g * turned[rows, at + FB : at + 2 * FB]
                ).astype(BF16)
            return carry

        each(own, spread_out)

    parts[...] = jnp.zeros_like(parts)
    centre = pull_rows(
        own, cols, waves, weight, spread, projection_ref, here, parts, back, product
    )
    for a in range(3):
        row = jnp.sum(parts[a].T, axis=0, keepdims=True)
        centre_ref[a : a + 1, :] = jnp.sum(centre[a], axis=0, keepdims=True)
        near_ref[a : a + 1, :] = row[:, 0:sent]
        far_ref[a : a + 1, :] = row[:, sent:]


def own_force_kernel(
    grad,
    spread,
    sines,
    waves,
    weight,
    cols,
    position_ref,
    centre_ref,
    projection_ref,
    force_ref,
    back,
    product,
    parts,
):
    own, features = grad.shape
    here = [position_ref[a] for a in range(3)]
    raw = [[projection_ref[a, s : s + 1, :] for a in range(3)] for s in range(2)]

    def turn(c, carry):
        rows = chunk_rows(c)
        g = grad[rows, :]
        t0 = g * sines[rows, 0:features]
        t1 = g * sines[rows, features : 2 * features]
        for a in range(3):
            parts[a, rows, :] = -fold(t0 * raw[0][a] + t1 * raw[1][a])
        return carry

    each(own, turn, 2)
    centre = pull_rows(
        0, cols, waves, weight, spread, projection_ref, here, parts, back, product
    )
    for a in range(3):
        row = jnp.sum(parts[a].T, axis=0, keepdims=True)
        force_ref[a : a + 1, :] = (
            row - jnp.sum(centre[a], axis=0, keepdims=True) - centre_ref[a : a + 1, :]
        )


def passed_along(block, axis, distance):
    devices = range(lax.axis_size(axis))
    route = [((i - distance) % len(devices), i) for i in devices]
    return lax.ppermute(block, axis, route)


def routed(block, axis, source):
    return lax.ppermute(block, axis, [(source(i), i) for i in range(lax.axis_size(axis))])


def near_pair(block):
    return routed(block, "dom", lambda i: i ^ 1)


def far_pair(block):
    return routed(block, "dom", lambda i: (i - 1 + i % 2 * 2) % lax.axis_size("dom"))


def after(value, *others):
    return lax.optimization_barrier((value, others))[0]


def matrix_part(points, point_weights):
    dom = lax.axis_index("dom")
    which, height = dom % 2, points.shape[2] // 8
    p = lax.dynamic_index_in_dim(points, which, 0, keepdims=False).astype(F32)
    w = lax.dynamic_index_in_dim(point_weights, which, 0, keepdims=False).astype(F32)
    left = lax.dynamic_slice_in_dim(p, (dom // 4 * 2 + dom // 2 % 2) * height, height, axis=1)
    return lax.dot_general(
        left * (2.0 * w)[:, None],
        p,
        (((0,), (0,)), ((), ())),
        precision=lax.Precision.HIGHEST,
        preferred_element_type=F32,
    )


def add_kernel(part_ref, other_ref, *outs):
    total = part_ref[...] + other_ref[...].astype(F32)
    for out in outs:
        out[...] = total.astype(out.dtype)


def pair_kernel(held_ref, other_ref, out_ref):
    rows = held_ref.shape[0]
    bit = lax.axis_index("dom") // 2 % 2
    out_ref[pl.ds(pl.multiple_of(bit * rows, rows), rows), :] = held_ref[...]
    out_ref[pl.ds(pl.multiple_of((1 - bit) * rows, rows), rows), :] = other_ref[...]


def ring_kernel(*refs):
    *pieces, out_ref = refs
    rows = pieces[0].shape[0]
    height = lax.axis_index("dom") // 4
    for k, piece in enumerate(pieces):
        place = (height + 4 - k) % 4
        out_ref[pl.ds(pl.multiple_of(place * rows, rows), rows), :] = piece[...]


def shards(
    positions,
    velocities,
    species,
    neighbours,
    neighbour_count,
    send_lists,
    projection,
    phase_shift,
    points,
    point_weights,
):
    own, sent = positions.shape[2], send_lists.shape[1]
    ghosts = 2 * sent
    everyone = own + ghosts
    features = points.shape[2]
    shape = jax.ShapeDtypeStruct
    species = species.reshape(1, own)
    position, velocity = positions.transpose(1, 0, 2), velocities.transpose(1, 0, 2)
    projection = projection.transpose(1, 0, 2)
    sends = (shape((4, sent), F32),) * 2
    wide = pltpu.VMEM((LANES, own), F32)
    slab = (features // 8, features)
    counts = neighbour_count.reshape(1, own)

    def count(part, neighbours):
        return call(
            functools.partial(count_kernel, part),
            shape((ghosts, own), F32),
            [pltpu.VMEM((NEIGH, own), jnp.int32)],
        )(neighbours, counts)

    own_call = call(
        own_kernel,
        (
            shape((own, LANES), F32),
            shape((own, 4 * features), BF16),
            shape((own, 4 * features), F32),
        ),
        [wide],
        LIMIT,
    )
    weigh_call = call(
        weigh_kernel,
        (
            shape((ghosts, LANES), F32),
            shape((everyone, own), F32),
            shape((own, everyone), BF16),
            shape((ghosts, 4 * features), BF16),
        ),
        [pltpu.VMEM((LANES, ghosts), F32)],
        LIMIT,
    )
    describe_call = call(
        describe_kernel,
        (shape((own, 2 * features), F32), shape((own, features), BF16)),
        [pltpu.VMEM((own, 4 * FB), F32)],
        LIMIT,
    )
    ghost_force_call = call(
        ghost_force_kernel,
        (
            shape((own, features), F32),
            shape((own, 4 * features), BF16),
            shape((3, own), F32),
            shape((3, sent), F32),
            shape((3, sent), F32),
        ),
        [
            pltpu.VMEM((ghosts, 4 * FB), F32),
            pltpu.VMEM((ghosts, own), F32),
            pltpu.VMEM((3, ghosts, LANES), F32),
        ],
        LIMIT,
    )
    own_force_call = call(
        own_force_kernel,
        shape((3, own), F32),
        [
            pltpu.VMEM((own, 4 * FB), F32),
            pltpu.VMEM((own, own), F32),
            pltpu.VMEM((3, own, LANES), F32),
        ],
        LIMIT,
    )

    above = passed_along(position, "bead", -1)
    to_near, to_far = call(first_kernel, sends, [wide])(position, species, send_lists)
    part = after(matrix_part(points, point_weights), to_near, to_far)
    for step in range(STEPS):
        last = step == STEPS - 1
        if step == 0:
            other = routed(part, "bead", lambda i: i ^ 4)
            to_far = after(to_far, part)
        from_far = far_pair(to_far)
        from_near = near_pair(to_near)
        cols, waves, turned = own_call(position, species, projection, phase_shift)
        if step == 0:
            number = []
            part, held = call(add_kernel, (shape(slab, F32), shape(slab, BF16)))(
                part, after(other, cols, from_far, from_near)
            )
            other = routed(held, "bead", lambda i: i ^ 1)
            number.append(count(0, after(neighbours, held)))
            part, held = call(add_kernel, (shape(slab, F32), shape(slab, BF16)))(
                part, after(other, number[-1])
            )
            other = routed(held, "bead", lambda i: i ^ 2)
            number.append(count(1, after(neighbours, held)))
            held = call(add_kernel, (shape(slab, BF16),))(part, after(other, number[-1]))[0]
            other = routed(held, "dom", lambda i: i ^ 2)
            number.append(count(2, after(neighbours, held)))
            state = weigh_call(position, from_near, from_far, cols, projection, *number)
            ghost_cols, weight, weight_turned, ghost_waves = state
            held = call(pair_kernel, shape((2 * slab[0], features), BF16))(
                held, after(other, *state)
            )
            pieces = [held] + [routed(held, "dom", lambda i: (i - 4 * k) % 16) for k in (1, 2, 3)]
            sines, low = describe_call(after(weight_turned, held), waves, ghost_waves, turned)
            half = call(ring_kernel, shape((features, features), BF16))(
                pieces[0], *[after(piece, low) for piece in pieces[1:]]
            )
            other_half = near_pair(half)
            below = passed_along(after(position, other_half), "bead", 1)
        else:
            above = passed_along(after(position, cols, from_far, from_near), "bead", -1)
            ghost_cols, weight, weight_turned, ghost_waves = weigh_call(
                position, from_near, from_far, cols, projection, *number
            )
            sines, low = describe_call(weight_turned, waves, ghost_waves, turned)
            below = passed_along(after(position, low), "bead", 1)
        grad, spread, centre, near_force, far_force = ghost_force_call(
            low,
            half,
            other_half,
            cols,
            turned,
            weight,
            ghost_waves,
            ghost_cols,
            position,
            projection,
        )
        far_back = far_pair(far_force)
        near_back = near_pair(near_force)
        force = own_force_call(
            grad, spread, sines, waves, weight, cols, position, centre, projection
        )
        moved = shape(position.shape, F32)
        position, velocity, *rest = call(
            functools.partial(update_kernel, last),
            (moved, moved) + (() if last else sends),
            [pltpu.VMEM((LANES, sent), F32), wide],
        )(
            force,
            near_back,
            far_back,
            send_lists,
            position,
            velocity,
            below,
            above,
            species,
        )
        if not last:
            to_near, to_far = rest
    return (position.transpose(1, 0, 2), velocity.transpose(1, 0, 2))


def solution(mesh):
    placed = (
        P("bead", None, "dom"),
        P("bead", None, "dom"),
        P("dom"),
        P(None, "dom"),
        P("dom"),
        P(None, "dom"),
        P(),
        P(),
        P(None, "bead", None),
        P(None, "bead"),
    )
    return jax.shard_map(
        shards,
        mesh=mesh,
        in_specs=placed,
        out_specs=(P("bead", None, "dom"), P("bead", None, "dom")),
        check_vma=False,
    )
```

time: 157 us -> 85.4 us (0.54)
  Pallas kernels: 86 us -> 43.2 us
  waiting for transfers between devices: 23.2 us -> 7.94 us
  local copies, waits for them, and re-layouts: 9.55 us -> 1.52 us
  starting transfers between devices: 34.6 us -> 30.4 us
  other arithmetic: 2.27 us -> 0.69 us
    pallas_call x4 -> x19, Pallas kernels: 81.9 us -> 41.3 us  [the longest x2 10.6 us: shards(): own_force_call(grad, spread, sines, waves, weight, cols, position, centre...]
    ppermute x12 -> x4, starting transfers between devices: 20.1 us -> 10.5 us  [passed_along(): return lax.ppermute(block, axis, route)]
    ppermute x12 -> x4, waiting for transfers between devices: 8.63 us -> 0.01 us  [passed_along(): return lax.ppermute(block, axis, route)]
    ppermute x9 -> x16, waiting for transfers between devices: 14.6 us -> 7.93 us  [routed(): lax.ppermute(block, axis, [(source(i), i) for i in range(lax.axis_size(ax...]
    ppermute x9 -> x16, starting transfers between devices: 14.5 us -> 20 us  [routed(): lax.ppermute(block, axis, [(source(i), i) for i in range(lax.axis_size(ax...]
    unnamed x45 -> x19, local copies, waits for them, and re-layouts: 5.02 us -> 0.99 us
    pallas_call x2 -> x0, local copies, waits for them, and re-layouts: 2.59 us -> none  [shards(): call(functools.partial(update_kernel, last), (moved, moved) + (() if last...]
    pallas_call x2, Pallas kernels: 4.06 us -> 1.92 us  [shards(): call(functools.partial(update_kernel, last), (moved, moved) + (() if last...]
  transfers between devices with their start and end apart: 21 -> 20, of which waited for: 12 -> 5; matrix products, arithmetic and copies ran while one was open for 3% -> 0% of each run, Pallas kernels for 52% -> 48%
where the time goes in v2:
time: 85.4 us; the launch traced here: 85.2 us
  Pallas kernels  43.2 us (51%)
  starting transfers between devices  30.4 us (36%)
  waiting for transfers between devices  7.94 us (9%)
  local copies, waits for them, and re-layouts  1.52 us (2%)
  between operations  1.08 us (1%)
    ppermute x16, starting transfers between devices, routed(): lax.ppermute(block, axis, [(source(i), i) for i in range(lax.axis_size(ax...  20 us
    pallas_call x2, Pallas kernels, shards(): own_force_call(grad, spread, sines, waves, weight, cols, position, centre...  10.6 us
    ppermute x4, starting transfers between devices, passed_along(): return lax.ppermute(block, axis, route)  10.5 us
    ppermute x16, waiting for transfers between devices, routed(): lax.ppermute(block, axis, [(source(i), i) for i in range(lax.axis_size(ax...  7.93 us
    pallas_call x2, Pallas kernels, shards(): ghost_force_call(low, half, other_half, cols, turned, weight, ghost_waves...  7.63 us
    pallas_call x2, Pallas kernels, shards(): cols, waves, turned = own_call(position, species, projection, phase_shift)  6.81 us
    pallas_call x3, Pallas kernels, count(): call(functools.partial(count_kernel, part), shape((ghosts, own), F32), [p...  5.41 us
    pallas_call x1, Pallas kernels, shards(): sines, low = describe_call(weight_turned, waves, ghost_waves, turned)  2.67 us
  transfers between devices with their start and end apart: 20, of which 5 were waited for; matrix products, arithmetic and copies ran while one was open for 0% of the time, Pallas kernels for 48%

profile of v2, /device:TPU:6, one launch (start us, length us, event | category | flops | bytes accessed | tf_op | source)
XLA Modules:
  0.0 85.2 jit_solution(3747273735613076786)
XLA Ops:
  0.8 0.9 %copy-done = bf16[2,250,512]{2,0,1:T(2,128)(2,1)S(1)} copy-done((bf16[2,250,512]{2,0,1:T(2,128)(2,1)S(1)}, bf16[2,250,512]{2,0,1:T(2,128)(2,1)}, u32[]{:S(2)}) %copy-start) | copy-done | bytes 512024
  3.8 3.3 %collective-permute-start.2 = (f32[64,512]{1,0:T(8,128)S(1)}, f32[64,512]{1,0:T(8,128)S(1)}, u32[]{:S(2)}, u32[]{:S(2)}) collective-permute-start(f32[64,512]{1,0:T(8,128)S(1)} %fusion.part_ref), channel_id=1, source_target_pairs={{4,0},{5,1},{6,2},{7,3},{0,4},{1,5},{2,6},{3,7},{12,8},{13,9},{14,... | collective-permute-start | bytes 393224 | tf_op jit(solution)/shard_map/ppermute | solution.py:474
  7.1 3.3 %collective-permute-start.1 = (f32[4,128]{1,0:T(4,128)S(1)}, f32[4,128]{1,0:T(4,128)S(1)}, u32[]{:S(2)}, u32[]{:S(2)}) collective-permute-start(f32[4,128]{1,0:T(4,128)S(1)} %get-tuple-element.61), channel_id=1, source_target_pairs={{120,0},{16,8},{8,16},{32,24},{24,32},{48,40},{40,48},{64,56},{56,... | collective-permute-start | bytes 6152 | tf_op jit(solution)/shard_map/ppermute | solution.py:474
  10.4 3.4 %shard_map.114 = (f32[512,128]{1,0:T(8,128)S(1)}, bf16[512,2048]{1,0:T(8,128)(2,1)S(1)}, f32[512,2048]{1,0:T(8,128)S(1)}) custom-call(f32[3,1,512]{2,1,0:T(1,128)S(1)} %bitcast.21, s32[1,512]{1,0:T(1,128)S(1)} %bitcast.29, f32[3,2,512]{2,1,0:T(2,128)S(1)} %bitcast.12, f32[2,512]{1,0:T(2,128)S(1)} %copy-done.6), custom_call_target="tpu_custom_call" | custom-call | tf_op jit(solution)/shard_map/pallas_call | solution.py:622
  13.9 0.9 %collective-permute-start.3 = (bf16[64,512]{1,0:T(8,128)(2,1)S(1)}, bf16[64,512]{1,0:T(8,128)(2,1)S(1)}, u32[]{:S(2)}, u32[]{:S(2)}) collective-permute-start(bf16[64,512]{1,0:T(8,128)(2,1)S(1)} %get-tuple-element.64), channel_id=1, source_target_pairs={{1,0},{0,1},{3,2},{2,3},{5,4},{4,5},{7,6},{6,7},{9,8},{8,9},{11,10... | collective-permute-start | bytes 196616 | tf_op jit(solution)/shard_map/ppermute | solution.py:474
  14.8 1.8 %shard_map.116.rest_0_ = f32[256,512]{1,0:T(8,128)S(1)} custom-call(s32[32,512]{1,0:T(8,128)S(1)} %copy-done.2, s32[1,512]{1,0:T(1,128)S(1)} %bitcast.33), custom_call_target="tpu_custom_call" | custom-call | tf_op jit(solution)/shard_map/pallas_call | solution.py:552
  16.6 1.9 %collective-permute-done.3.other_ref = bf16[64,512]{1,0:T(8,128)(2,1)S(1)} collective-permute-done((bf16[64,512]{1,0:T(8,128)(2,1)S(1)}, bf16[64,512]{1,0:T(8,128)(2,1)S(1)}, u32[]{:S(2)}, u32[]{:S(2)}) %collective-permute-start.3) | collective-permute-done | bytes 65568 | tf_op jit(solution)/shard_map/ppermute | solution.py:474
  18.5 1.5 %collective-permute-start.4 = (bf16[64,512]{1,0:T(8,128)(2,1)S(1)}, bf16[64,512]{1,0:T(8,128)(2,1)S(1)}, u32[]{:S(2)}, u32[]{:S(2)}) collective-permute-start(bf16[64,512]{1,0:T(8,128)(2,1)S(1)} %get-tuple-element.68), channel_id=1, source_target_pairs={{2,0},{3,1},{0,2},{1,3},{6,4},{7,5},{4,6},{5,7},{10,8},{11,9},{8,1... | collective-permute-start | bytes 196616 | tf_op jit(solution)/shard_map/ppermute | solution.py:474
  20.0 1.8 %shard_map.118.rest_1_ = f32[256,512]{1,0:T(8,128)S(1)} custom-call(s32[32,512]{1,0:T(8,128)S(1)} %copy-done.2, s32[1,512]{1,0:T(1,128)S(1)} %bitcast.34), custom_call_target="tpu_custom_call" | custom-call | tf_op jit(solution)/shard_map/pallas_call | solution.py:552
  21.8 2.6 %collective-permute-done.4.other_ref = bf16[64,512]{1,0:T(8,128)(2,1)S(1)} collective-permute-done((bf16[64,512]{1,0:T(8,128)(2,1)S(1)}, bf16[64,512]{1,0:T(8,128)(2,1)S(1)}, u32[]{:S(2)}, u32[]{:S(2)}) %collective-permute-start.4) | collective-permute-done | bytes 65568 | tf_op jit(solution)/shard_map/ppermute | solution.py:474
  24.5 1.8 %shard_map.120.rest_2_ = f32[256,512]{1,0:T(8,128)S(1)} custom-call(s32[32,512]{1,0:T(8,128)S(1)} %copy-done.2, s32[1,512]{1,0:T(1,128)S(1)} %bitcast.35), custom_call_target="tpu_custom_call" | custom-call | tf_op jit(solution)/shard_map/pallas_call | solution.py:552
  26.3 2.5 %shard_map.121 = (f32[256,128]{1,0:T(8,128)S(1)}, f32[768,512]{1,0:T(8,128)S(1)}, bf16[512,768]{1,0:T(8,128)(2,1)S(1)}, bf16[256,2048]{1,0:T(8,128)(2,1)S(1)}) custom-call(f32[3,1,512]{2,1,0:T(1,128)S(1)} %bitcast.22, f32[4,128]{1,0:T(4,128)S(1)} %collective-permute-done.near_ref, f32[4,128]{1,0:T(4,128)S(1)} %collective-permute-done.1.far_ref, ...), custom_call_target="tpu_custom_call" | custom-call | tf_op jit(solution)/shard_map/pallas_call | solution.py:638
  28.8 2.2 %collective-permute-start.8 = (bf16[128,512]{1,0:T(8,128)(2,1)S(1)}, bf16[128,512]{1,0:T(8,128)(2,1)S(1)}, u32[]{:S(2)}, u32[]{:S(2)}) collective-permute-start(bf16[128,512]{1,0:T(8,128)(2,1)S(1)} %shard_map.122.refs_0_), channel_id=1, source_target_pairs={{32,0},{40,8},{48,16},{56,24},{64,32},{72,40},{80,48},{88,56},{96,... | collective-permute-start | bytes 393224 | tf_op jit(solution)/shard_map/ppermute | solution.py:474
  31.0 1.8 %collective-permute-start.7 = (bf16[128,512]{1,0:T(8,128)(2,1)S(1)}, bf16[128,512]{1,0:T(8,128)(2,1)S(1)}, u32[]{:S(2)}, u32[]{:S(2)}) collective-permute-start(bf16[128,512]{1,0:T(8,128)(2,1)S(1)} %shard_map.122.refs_0_), channel_id=1, source_target_pairs={{64,0},{72,8},{80,16},{88,24},{96,32},{104,40},{112,48},{120,56},{... | collective-permute-start | bytes 393224 | tf_op jit(solution)/shard_map/ppermute | solution.py:474
  32.8 1.0 %collective-permute-start.6 = (bf16[128,512]{1,0:T(8,128)(2,1)S(1)}, bf16[128,512]{1,0:T(8,128)(2,1)S(1)}, u32[]{:S(2)}, u32[]{:S(2)}) collective-permute-start(bf16[128,512]{1,0:T(8,128)(2,1)S(1)} %shard_map.122.refs_0_), channel_id=1, source_target_pairs={{96,0},{104,8},{112,16},{120,24},{0,32},{8,40},{16,48},{24,56},{32... | collective-permute-start | bytes 393224 | tf_op jit(solution)/shard_map/ppermute | solution.py:474
  33.8 2.7 %shard_map.123 = (f32[512,1024]{1,0:T(8,128)S(1)}, bf16[512,512]{1,0:T(8,128)(2,1)S(1)}) custom-call(bf16[512,768]{1,0:T(8,128)(2,1)S(1)} %get-tuple-element.78.weight_turned, bf16[512,2048]{1,0:T(8,128)(2,1)S(1)} %get-tuple-element.79.own_waves.waves, bf16[256,2048]{1,0:T(8,128)(2,1)S(1)} %get-tuple-element.76.ghost_waves.waves, ...), custom_call_target="tpu_custom_call" | custom-call | tf_op jit(solution)/shard_map/pallas_call | solution.py:644
  36.5 1.0 %collective-permute-done.7.refs_2_ = bf16[128,512]{1,0:T(8,128)(2,1)S(1)} collective-permute-done((bf16[128,512]{1,0:T(8,128)(2,1)S(1)}, bf16[128,512]{1,0:T(8,128)(2,1)S(1)}, u32[]{:S(2)}, u32[]{:S(2)}) %collective-permute-start.7) | collective-permute-done | bytes 131104 | tf_op jit(solution)/shard_map/ppermute | solution.py:474
  37.5 1.5 %collective-permute-done.6.refs_1_ = bf16[128,512]{1,0:T(8,128)(2,1)S(1)} collective-permute-done((bf16[128,512]{1,0:T(8,128)(2,1)S(1)}, bf16[128,512]{1,0:T(8,128)(2,1)S(1)}, u32[]{:S(2)}, u32[]{:S(2)}) %collective-permute-start.6) | collective-permute-done | bytes 131104 | tf_op jit(solution)/shard_map/ppermute | solution.py:474
  40.0 1.0 %collective-permute-done.9.other_ref = bf16[512,512]{1,0:T(8,128)(2,1)S(1)} collective-permute-done((bf16[512,512]{1,0:T(8,128)(2,1)S(1)}, bf16[512,512]{1,0:T(8,128)(2,1)S(1)}, u32[]{:S(2)}, u32[]{:S(2)}) %collective-permute-start.9) | collective-permute-done | bytes 524320 | tf_op jit(solution)/shard_map/ppermute | solution.py:474
  41.0 3.8 %collective-permute-start.12 = (f32[3,1,512]{2,1,0:T(1,128)S(1)}, f32[3,1,512]{2,1,0:T(1,128)S(1)}, u32[]{:S(2)}, u32[]{:S(2)}) collective-permute-start(f32[3,1,512]{2,1,0:T(1,128)S(1)} %bitcast.24), channel_id=1, source_target_pairs={{7,0},{0,1},{1,2},{2,3},{3,4},{4,5},{5,6},{6,7},{15,8},{8,9},{9,10... | collective-permute-start | bytes 18440 | tf_op jit(solution)/shard_map/ppermute | solution.py:470
  44.8 3.8 %shard_map.125 = (f32[512,512]{1,0:T(8,128)S(1)}, bf16[512,2048]{1,0:T(8,128)(2,1)S(1)}, f32[3,512]{1,0:T(4,128)S(1)}, f32[3,128]{1,0:T(4,128)S(1)}, f32[3,128]{1,0:T(4,128)S(1)}) custom-call(bf16[512,512]{1,0:T(8,128)(2,1)S(1)} %get-tuple-element.81.low, bf16[512,512]{1,0:T(8,128)(2,1)S(1)} %shard_map.124.half_ref, ...), custom_call_target="tpu_custom_call" | custom-call | tf_op jit(solution)/shard_map/pallas_call | solution.py:657
  48.9 1.2 %collective-permute-start.11 = (f32[3,128]{1,0:T(4,128)S(1)}, f32[3,128]{1,0:T(4,128)S(1)}, u32[]{:S(2)}, u32[]{:S(2)}) collective-permute-start(f32[3,128]{1,0:T(4,128)S(1)} %get-tuple-element.90), channel_id=1, source_target_pairs={{120,0},{16,8},{8,16},{32,24},{24,32},{48,40},{40,48},{64,56},{56,... | collective-permute-start | bytes 4616 | tf_op jit(solution)/shard_map/ppermute | solution.py:474
  50.1 5.3 %shard_map.126.force_ref = f32[3,512]{1,0:T(4,128)S(1)} custom-call(f32[512,512]{1,0:T(8,128)S(1)} %get-tuple-element.85.grad, bf16[512,2048]{1,0:T(8,128)(2,1)S(1)} %get-tuple-element.86.spread, f32[512,1024]{1,0:T(8,128)S(1)} %get-tuple-element.87.sines, bf16[512,2048]{1,0:T(8,128)(2,1)S(1)} %get-tuple-element.79.own_waves.waves, ...), custom_call_target="tpu_custom_call" | custom-call | tf_op jit(solution)/shard_map/pallas_call | solution.py:671
  56.5 2.8 %collective-permute-start.15 = (f32[4,128]{1,0:T(4,128)S(1)}, f32[4,128]{1,0:T(4,128)S(1)}, u32[]{:S(2)}, u32[]{:S(2)}) collective-permute-start(f32[4,128]{1,0:T(4,128)S(1)} %get-tuple-element.94), channel_id=1, source_target_pairs={{120,0},{16,8},{8,16},{32,24},{24,32},{48,40},{40,48},{64,56},{56,... | collective-permute-start | bytes 6152 | tf_op jit(solution)/shard_map/ppermute | solution.py:474
  59.2 3.4 %shard_map.128 = (f32[512,128]{1,0:T(8,128)S(1)}, bf16[512,2048]{1,0:T(8,128)(2,1)S(1)}, f32[512,2048]{1,0:T(8,128)S(1)}) custom-call(f32[3,1,512]{2,1,0:T(1,128)S(1)} %get-tuple-element.111.position_ref, s32[1,512]{1,0:T(1,128)S(1)} %bitcast.31, f32[3,2,512]{2,1,0:T(2,128)S(1)} %bitcast.16, f32[2,512]{1,0:T(2,128)S(1)} %copy-done.6), custom_call_target="tpu_custom_call" | custom-call | tf_op jit(solution)/shard_map/pallas_call | solution.py:622
  62.8 2.5 %shard_map.129 = (f32[256,128]{1,0:T(8,128)S(1)}, f32[768,512]{1,0:T(8,128)S(1)}, bf16[512,768]{1,0:T(8,128)(2,1)S(1)}, bf16[256,2048]{1,0:T(8,128)(2,1)S(1)}) custom-call(f32[3,1,512]{2,1,0:T(1,128)S(1)} %get-tuple-element.111.position_ref, f32[4,128]{1,0:T(4,128)S(1)} %collective-permute-done.14.near_ref, f32[4,128]{1,0:T(4,128)S(1)} %collective-permute-done.15.far_ref, ...), custom_call_target="tpu_custom_call" | custom-call | tf_op jit(solution)/shard_map/pallas_call | solution.py:652
  65.2 2.7 %shard_map.130 = (f32[512,1024]{1,0:T(8,128)S(1)}, bf16[512,512]{1,0:T(8,128)(2,1)S(1)}) custom-call(bf16[512,768]{1,0:T(8,128)(2,1)S(1)} %get-tuple-element.96.weight_turned, bf16[512,2048]{1,0:T(8,128)(2,1)S(1)} %get-tuple-element.97.own_waves.waves, bf16[256,2048]{1,0:T(8,128)(2,1)S(1)} %get-tuple-element.98.ghost_waves.waves, ...), custom_call_target="tpu_custom_call" | custom-call | tf_op jit(solution)/shard_map/pallas_call | solution.py:655
  67.9 5.7 %collective-permute-start.18 = (f32[3,1,512]{2,1,0:T(1,128)S(1)}, f32[3,1,512]{2,1,0:T(1,128)S(1)}, u32[]{:S(2)}, u32[]{:S(2)}) collective-permute-start(f32[3,1,512]{2,1,0:T(1,128)S(1)} %get-tuple-element.111.position_ref), channel_id=1, source_target_pairs={{7,0},{0,1},{1,2},{2,3},{3,4},{4,5},{5,6},{6,7},{15,8},{8,9},{9,10... | collective-permute-start | bytes 18440 | tf_op jit(solution)/shard_map/ppermute | solution.py:470
  73.6 3.8 %shard_map.131 = (f32[512,512]{1,0:T(8,128)S(1)}, bf16[512,2048]{1,0:T(8,128)(2,1)S(1)}, f32[3,512]{1,0:T(4,128)S(1)}, f32[3,128]{1,0:T(4,128)S(1)}, f32[3,128]{1,0:T(4,128)S(1)}) custom-call(bf16[512,512]{1,0:T(8,128)(2,1)S(1)} %get-tuple-element.100.low, bf16[512,512]{1,0:T(8,128)(2,1)S(1)} %shard_map.124.half_ref, ...), custom_call_target="tpu_custom_call" | custom-call | tf_op jit(solution)/shard_map/pallas_call | solution.py:657
  77.5 1.4 %collective-permute-start.17 = (f32[3,128]{1,0:T(4,128)S(1)}, f32[3,128]{1,0:T(4,128)S(1)}, u32[]{:S(2)}, u32[]{:S(2)}) collective-permute-start(f32[3,128]{1,0:T(4,128)S(1)} %get-tuple-element.108), channel_id=1, source_target_pairs={{120,0},{16,8},{8,16},{32,24},{24,32},{48,40},{40,48},{64,56},{56,... | collective-permute-start | bytes 4616 | tf_op jit(solution)/shard_map/ppermute | solution.py:474
  78.9 5.3 %shard_map.132.force_ref = f32[3,512]{1,0:T(4,128)S(1)} custom-call(f32[512,512]{1,0:T(8,128)S(1)} %get-tuple-element.103.grad, bf16[512,2048]{1,0:T(8,128)(2,1)S(1)} %get-tuple-element.104.spread, f32[512,1024]{1,0:T(8,128)S(1)} %get-tuple-element.105.sines, bf16[512,2048]{1,0:T(8,128)(2,1)S(1)} %get-tuple-element.97.own_waves.waves, ...), custom_call_target="tpu_custom_call" | custom-call | tf_op jit(solution)/shard_map/pallas_call | solution.py:671
  84.2 1.0 %shard_map.133 = (f32[3,1,512]{2,1,0:T(1,128)}, f32[3,1,512]{2,1,0:T(1,128)}) custom-call(f32[3,512]{1,0:T(4,128)S(1)} %shard_map.132.force_ref, f32[3,128]{1,0:T(4,128)S(1)} %collective-permute-done.16.near_back_ref, f32[3,128]{1,0:T(4,128)S(1)} %collective-permute-done.17.far_back_ref, s32[2,128]{1,0:T(2,128)S(1)} %copy-done.7, ...), custom_call_target="tpu_custom_call" | custom-call | tf_op jit(solution)/shard_map/pallas_call | solution.py:675
  (51 shorter events, 4.9 us)
Async XLA Ops:
  0.6 1.0 %copy-start = (bf16[2,250,512]{2,0,1:T(2,128)(2,1)S(1)}, bf16[2,250,512]{2,0,1:T(2,128)(2,1)}, u32[]{:S(2)}) copy-start(bf16[2,250,512]{2,0,1:T(2,128)(2,1)} %param.18) | copy-start | bytes 1536004
  0.6 2.7 %copy-start.3 = (f32[1,3,512]{2,0,1:T(1,128)S(1)}, f32[1,3,512]{2,0,1:T(1,128)}, u32[]{:S(2)}) copy-start(f32[1,3,512]{2,0,1:T(1,128)} %param.10) | copy-start | bytes 18436
  0.7 2.7 %copy-start.4 = (s32[512]{0:T(512)S(1)}, s32[512]{0:T(512)}, u32[]{:S(2)}) copy-start(s32[512]{0:T(512)} %param.12) | copy-start | bytes 6148
  0.7 2.7 %copy-start.7 = (s32[2,128]{1,0:T(2,128)S(1)}, s32[2,128]{1,0:T(2,128)}, u32[]{:S(2)}) copy-start(s32[2,128]{1,0:T(2,128)} %lists_ref.5) | copy-start | bytes 3076
  0.7 9.7 %copy-start.1 = (f32[2,3,512]{2,0,1:T(2,128)S(1)}, f32[2,3,512]{2,0,1:T(2,128)}, u32[]{:S(2)}) copy-start(f32[2,3,512]{2,0,1:T(2,128)} %param.16) | copy-start | bytes 36868
  0.7 9.7 %copy-start.6 = (f32[2,512]{1,0:T(2,128)S(1)}, f32[2,512]{1,0:T(2,128)}, u32[]{:S(2)}) copy-start(f32[2,512]{1,0:T(2,128)} %shift_ref.3) | copy-start | bytes 12292
  0.7 14.1 %copy-start.2 = (s32[32,512]{1,0:T(8,128)S(1)}, s32[32,512]{1,0:T(8,128)}, u32[]{:S(2)}) copy-start(s32[32,512]{1,0:T(8,128)} %neighbours_ref.2) | copy-start | bytes 196612
  0.7 14.1 %copy-start.5 = (s32[512]{0:T(512)S(1)}, s32[512]{0:T(512)}, u32[]{:S(2)}) copy-start(s32[512]{0:T(512)} %param.14) | copy-start | bytes 6148
  3.8 10.0 %collective-permute-start.2 = (f32[64,512]{1,0:T(8,128)S(1)}, f32[64,512]{1,0:T(8,128)S(1)}, u32[]{:S(2)}, u32[]{:S(2)}) collective-permute-start(f32[64,512]{1,0:T(8,128)S(1)} %fusion.part_ref), channel_id=1, source_target_pairs={{4,0},{5,1},{6,2},{7,3},{0,4},{1,5},{2,6},{3,7},{12,8},{13,9},{14,... | collective-permute-start | bytes 393224 | tf_op jit(solution)/shard_map/ppermute | solution.py:474
  7.1 6.7 %collective-permute-start.1 = (f32[4,128]{1,0:T(4,128)S(1)}, f32[4,128]{1,0:T(4,128)S(1)}, u32[]{:S(2)}, u32[]{:S(2)}) collective-permute-start(f32[4,128]{1,0:T(4,128)S(1)} %get-tuple-element.61), channel_id=1, source_target_pairs={{120,0},{16,8},{8,16},{32,24},{24,32},{48,40},{40,48},{64,56},{56,... | collective-permute-start | bytes 6152 | tf_op jit(solution)/shard_map/ppermute | solution.py:474
  10.4 3.4 %collective-permute-start = (f32[4,128]{1,0:T(4,128)S(1)}, f32[4,128]{1,0:T(4,128)S(1)}, u32[]{:S(2)}, u32[]{:S(2)}) collective-permute-start(f32[4,128]{1,0:T(4,128)S(1)} %get-tuple-element.58), channel_id=1, source_target_pairs={{8,0},{0,8},{24,16},{16,24},{40,32},{32,40},{56,48},{48,56},{72,64... | collective-permute-start | bytes 6152 | tf_op jit(solution)/shard_map/ppermute | solution.py:474
  13.9 4.6 %collective-permute-start.3 = (bf16[64,512]{1,0:T(8,128)(2,1)S(1)}, bf16[64,512]{1,0:T(8,128)(2,1)S(1)}, u32[]{:S(2)}, u32[]{:S(2)}) collective-permute-start(bf16[64,512]{1,0:T(8,128)(2,1)S(1)} %get-tuple-element.64), channel_id=1, source_target_pairs={{1,0},{0,1},{3,2},{2,3},{5,4},{4,5},{7,6},{6,7},{9,8},{8,9},{11,10... | collective-permute-start | bytes 196616 | tf_op jit(solution)/shard_map/ppermute | solution.py:474
  18.5 5.8 %collective-permute-start.4 = (bf16[64,512]{1,0:T(8,128)(2,1)S(1)}, bf16[64,512]{1,0:T(8,128)(2,1)S(1)}, u32[]{:S(2)}, u32[]{:S(2)}) collective-permute-start(bf16[64,512]{1,0:T(8,128)(2,1)S(1)} %get-tuple-element.68), channel_id=1, source_target_pairs={{2,0},{3,1},{0,2},{1,3},{6,4},{7,5},{4,6},{5,7},{10,8},{11,9},{8,1... | collective-permute-start | bytes 196616 | tf_op jit(solution)/shard_map/ppermute | solution.py:474
  24.4 4.4 %collective-permute-start.5 = (bf16[64,512]{1,0:T(8,128)(2,1)S(1)}, bf16[64,512]{1,0:T(8,128)(2,1)S(1)}, u32[]{:S(2)}, u32[]{:S(2)}) collective-permute-start(bf16[64,512]{1,0:T(8,128)(2,1)S(1)} %shard_map.119.held_ref), channel_id=1, source_target_pairs={{16,0},{24,8},{0,16},{8,24},{48,32},{56,40},{32,48},{40,56},{80,64... | collective-permute-start | bytes 196616 | tf_op jit(solution)/shard_map/ppermute | solution.py:474
  28.8 7.7 %collective-permute-start.8 = (bf16[128,512]{1,0:T(8,128)(2,1)S(1)}, bf16[128,512]{1,0:T(8,128)(2,1)S(1)}, u32[]{:S(2)}, u32[]{:S(2)}) collective-permute-start(bf16[128,512]{1,0:T(8,128)(2,1)S(1)} %shard_map.122.refs_0_), channel_id=1, source_target_pairs={{32,0},{40,8},{48,16},{56,24},{64,32},{72,40},{80,48},{88,56},{96,... | collective-permute-start | bytes 393224 | tf_op jit(solution)/shard_map/ppermute | solution.py:474
  31.0 6.5 %collective-permute-start.7 = (bf16[128,512]{1,0:T(8,128)(2,1)S(1)}, bf16[128,512]{1,0:T(8,128)(2,1)S(1)}, u32[]{:S(2)}, u32[]{:S(2)}) collective-permute-start(bf16[128,512]{1,0:T(8,128)(2,1)S(1)} %shard_map.122.refs_0_), channel_id=1, source_target_pairs={{64,0},{72,8},{80,16},{88,24},{96,32},{104,40},{112,48},{120,56},{... | collective-permute-start | bytes 393224 | tf_op jit(solution)/shard_map/ppermute | solution.py:474
  32.8 6.2 %collective-permute-start.6 = (bf16[128,512]{1,0:T(8,128)(2,1)S(1)}, bf16[128,512]{1,0:T(8,128)(2,1)S(1)}, u32[]{:S(2)}, u32[]{:S(2)}) collective-permute-start(bf16[128,512]{1,0:T(8,128)(2,1)S(1)} %shard_map.122.refs_0_), channel_id=1, source_target_pairs={{96,0},{104,8},{112,16},{120,24},{0,32},{8,40},{16,48},{24,56},{32... | collective-permute-start | bytes 393224 | tf_op jit(solution)/shard_map/ppermute | solution.py:474
  39.0 2.0 %collective-permute-start.9 = (bf16[512,512]{1,0:T(8,128)(2,1)S(1)}, bf16[512,512]{1,0:T(8,128)(2,1)S(1)}, u32[]{:S(2)}, u32[]{:S(2)}) collective-permute-start(bf16[512,512]{1,0:T(8,128)(2,1)S(1)} %shard_map.124.half_ref), channel_id=1, source_target_pairs={{8,0},{0,8},{24,16},{16,24},{40,32},{32,40},{56,48},{48,56},{72,64... | collective-permute-start | bytes 1572872 | tf_op jit(solution)/shard_map/ppermute | solution.py:474
  39.1 16.3 %collective-permute-start.13 = (f32[3,1,512]{2,1,0:T(1,128)S(1)}, f32[3,1,512]{2,1,0:T(1,128)S(1)}, u32[]{:S(2)}, u32[]{:S(2)}) collective-permute-start(f32[3,1,512]{2,1,0:T(1,128)S(1)} %bitcast.23), channel_id=1, source_target_pairs={{1,0},{2,1},{3,2},{4,3},{5,4},{6,5},{7,6},{0,7},{9,8},{10,9},{11,1... | collective-permute-start | bytes 18440 | tf_op jit(solution)/shard_map/ppermute | solution.py:470
  41.0 14.4 %collective-permute-start.12 = (f32[3,1,512]{2,1,0:T(1,128)S(1)}, f32[3,1,512]{2,1,0:T(1,128)S(1)}, u32[]{:S(2)}, u32[]{:S(2)}) collective-permute-start(f32[3,1,512]{2,1,0:T(1,128)S(1)} %bitcast.24), channel_id=1, source_target_pairs={{7,0},{0,1},{1,2},{2,3},{3,4},{4,5},{5,6},{6,7},{15,8},{8,9},{9,10... | collective-permute-start | bytes 18440 | tf_op jit(solution)/shard_map/ppermute | solution.py:470
  48.6 6.8 %collective-permute-start.10 = (f32[3,128]{1,0:T(4,128)S(1)}, f32[3,128]{1,0:T(4,128)S(1)}, u32[]{:S(2)}, u32[]{:S(2)}) collective-permute-start(f32[3,128]{1,0:T(4,128)S(1)} %get-tuple-element.89), channel_id=1, source_target_pairs={{8,0},{0,8},{24,16},{16,24},{40,32},{32,40},{56,48},{48,56},{72,64... | collective-permute-start | bytes 4616 | tf_op jit(solution)/shard_map/ppermute | solution.py:474
  48.9 6.5 %collective-permute-start.11 = (f32[3,128]{1,0:T(4,128)S(1)}, f32[3,128]{1,0:T(4,128)S(1)}, u32[]{:S(2)}, u32[]{:S(2)}) collective-permute-start(f32[3,128]{1,0:T(4,128)S(1)} %get-tuple-element.90), channel_id=1, source_target_pairs={{120,0},{16,8},{8,16},{32,24},{24,32},{48,40},{40,48},{64,56},{56,... | collective-permute-start | bytes 4616 | tf_op jit(solution)/shard_map/ppermute | solution.py:474
  50.1 5.3 %copy-start.8 = (f32[1,3,512]{2,0,1:T(1,128)S(1)}, f32[1,3,512]{2,0,1:T(1,128)}, u32[]{:S(2)}) copy-start(f32[1,3,512]{2,0,1:T(1,128)} %param.11) | copy-start | bytes 18436
  56.3 6.3 %collective-permute-start.14 = (f32[4,128]{1,0:T(4,128)S(1)}, f32[4,128]{1,0:T(4,128)S(1)}, u32[]{:S(2)}, u32[]{:S(2)}) collective-permute-start(f32[4,128]{1,0:T(4,128)S(1)} %get-tuple-element.93), channel_id=1, source_target_pairs={{8,0},{0,8},{24,16},{16,24},{40,32},{32,40},{56,48},{48,56},{72,64... | collective-permute-start | bytes 6152 | tf_op jit(solution)/shard_map/ppermute | solution.py:474
  56.5 6.2 %collective-permute-start.15 = (f32[4,128]{1,0:T(4,128)S(1)}, f32[4,128]{1,0:T(4,128)S(1)}, u32[]{:S(2)}, u32[]{:S(2)}) collective-permute-start(f32[4,128]{1,0:T(4,128)S(1)} %get-tuple-element.94), channel_id=1, source_target_pairs={{120,0},{16,8},{8,16},{32,24},{24,32},{48,40},{40,48},{64,56},{56,... | collective-permute-start | bytes 6152 | tf_op jit(solution)/shard_map/ppermute | solution.py:474
  62.7 21.5 %collective-permute-start.19 = (f32[3,1,512]{2,1,0:T(1,128)S(1)}, f32[3,1,512]{2,1,0:T(1,128)S(1)}, u32[]{:S(2)}, u32[]{:S(2)}) collective-permute-start(f32[3,1,512]{2,1,0:T(1,128)S(1)} %get-tuple-element.111.position_ref), channel_id=1, source_target_pairs={{1,0},{2,1},{3,2},{4,3},{5,4},{6,5},{7,6},{0,7},{9,8},{10,9},{11,1... | collective-permute-start | bytes 18440 | tf_op jit(solution)/shard_map/ppermute | solution.py:470
  67.9 16.3 %collective-permute-start.18 = (f32[3,1,512]{2,1,0:T(1,128)S(1)}, f32[3,1,512]{2,1,0:T(1,128)S(1)}, u32[]{:S(2)}, u32[]{:S(2)}) collective-permute-start(f32[3,1,512]{2,1,0:T(1,128)S(1)} %get-tuple-element.111.position_ref), channel_id=1, source_target_pairs={{7,0},{0,1},{1,2},{2,3},{3,4},{4,5},{5,6},{6,7},{15,8},{8,9},{9,10... | collective-permute-start | bytes 18440 | tf_op jit(solution)/shard_map/ppermute | solution.py:470
  77.4 6.8 %collective-permute-start.16 = (f32[3,128]{1,0:T(4,128)S(1)}, f32[3,128]{1,0:T(4,128)S(1)}, u32[]{:S(2)}, u32[]{:S(2)}) collective-permute-start(f32[3,128]{1,0:T(4,128)S(1)} %get-tuple-element.107), channel_id=1, source_target_pairs={{8,0},{0,8},{24,16},{16,24},{40,32},{32,40},{56,48},{48,56},{72,64... | collective-permute-start | bytes 4616 | tf_op jit(solution)/shard_map/ppermute | solution.py:474
  77.5 6.7 %collective-permute-start.17 = (f32[3,128]{1,0:T(4,128)S(1)}, f32[3,128]{1,0:T(4,128)S(1)}, u32[]{:S(2)}, u32[]{:S(2)}) collective-permute-start(f32[3,128]{1,0:T(4,128)S(1)} %get-tuple-element.108), channel_id=1, source_target_pairs={{120,0},{16,8},{8,16},{32,24},{24,32},{48,40},{40,48},{64,56},{56,... | collective-permute-start | bytes 4616 | tf_op jit(solution)/shard_map/ppermute | solution.py:474

commit v3 on v2

--- a/solution.py
+++ b/solution.py
@@ -54,25 +54,21 @@
 
 
 def count_kernel(part, neighbours_ref, count_ref, number_ref, named):
+    rows, atoms = number_ref.shape
     slot = lax.broadcasted_iota(jnp.int32, neighbours_ref.shape, 0)
-    named[...] = jnp.where(slot < count_ref[...], neighbours_ref[...], -1)
-    rows, atoms = number_ref.shape
-    ghosts = rows // 2
-    core = core_of()
-
-    def chunk(c, carry):
-        start = pl.multiple_of(c * ROWS, ROWS)
-        row = start + part * rows
-        swap = jnp.where(core == 0, ghosts, 0)
-        shift = jnp.where(row >= atoms + ghosts, -swap, jnp.where(row >= atoms, swap, 0))
-        local = lax.broadcasted_iota(jnp.int32, (ROWS, atoms), 0) + (row + shift)
-        total = jnp.zeros((ROWS, atoms), F32)
+    row = jnp.where(slot < count_ref[...], neighbours_ref[...] - part * rows, -1)
+    if part * rows >= atoms:
+        swapped = jnp.where(row >= rows // 2, row - rows // 2, row + rows // 2)
+        row = jnp.where((core_of() == 0) & (row >= 0), swapped, row)
+    named[...] = jnp.where((row >= 0) & (row < rows), row, -1).astype(F32)
+    one, zero = jnp.ones((), BF16), jnp.zeros((), BF16)
+    step = 2 * ROWS
+    for start in range(0, rows, step):
+        local = (lax.broadcasted_iota(jnp.int32, (step, atoms), 0) + start).astype(F32).astype(BF16)
+        total = jnp.zeros((step, atoms), BF16)
         for k in range(NEIGH):
-            total = total + jnp.where(local == named[k : k + 1, :], 1.0, 0.0)
-        number_ref[pl.ds(start, ROWS), :] = total
-        return carry
-
-    lax.fori_loop(0, rows // ROWS, chunk, 0)
+            total = total + jnp.where(local == named[k : k + 1, :].astype(BF16), one, zero)
+        number_ref[start : start + step, :] = total.astype(F32)
 
 
 def near_far_lists(lists_ref):
@@ -153,12 +149,14 @@
         send_rows(rows, species.astype(F32), lists, rest[0], rest[1], wide)
 
 
-def each(count, body, unroll=4, carry=0):
-    return lax.fori_loop(0, count // ROWS, body, carry, unroll=min(unroll, count // ROWS))
+def each(count, body, carry=0):
+    for c in range(count // ROWS):
+        carry = body(c, carry)
+    return carry
 
 
 def chunk_rows(c, first=0):
-    return pl.ds(pl.multiple_of(first + c * ROWS, ROWS), ROWS)
+    return slice(first + c * ROWS, first + (c + 1) * ROWS)
 
 
 def own_kernel(
@@ -453,7 +451,7 @@
             parts[a, rows, :] = -fold(t0 * raw[0][a] + t1 * raw[1][a])
         return carry
 
-    each(own, turn, 2)
+    each(own, turn)
     centre = pull_rows(
         0, cols, waves, weight, spread, projection_ref, here, parts, back, product
     )
@@ -482,16 +480,22 @@
     return routed(block, "dom", lambda i: (i - 1 + i % 2 * 2) % lax.axis_size("dom"))
 
 
+def across(block):
+    beads = lax.axis_size("bead")
+    route = [(i ^ (2 * beads + 4), i) for i in range(beads * lax.axis_size("dom"))]
+    return lax.ppermute(block, ("dom", "bead"), route)
+
+
 def after(value, *others):
     return lax.optimization_barrier((value, others))[0]
 
 
 def matrix_part(points, point_weights):
     dom = lax.axis_index("dom")
-    which, height = dom % 2, points.shape[2] // 8
+    which, height = dom % 2, points.shape[2] // 4
     p = lax.dynamic_index_in_dim(points, which, 0, keepdims=False).astype(F32)
     w = lax.dynamic_index_in_dim(point_weights, which, 0, keepdims=False).astype(F32)
-    left = lax.dynamic_slice_in_dim(p, (dom // 4 * 2 + dom // 2 % 2) * height, height, axis=1)
+    left = lax.dynamic_slice_in_dim(p, dom // 4 * height, height, axis=1)
     return lax.dot_general(
         left * (2.0 * w)[:, None],
         p,
@@ -505,13 +509,6 @@
     total = part_ref[...] + other_ref[...].astype(F32)
     for out in outs:
         out[...] = total.astype(out.dtype)
-
-
-def pair_kernel(held_ref, other_ref, out_ref):
-    rows = held_ref.shape[0]
-    bit = lax.axis_index("dom") // 2 % 2
-    out_ref[pl.ds(pl.multiple_of(bit * rows, rows), rows), :] = held_ref[...]
-    out_ref[pl.ds(pl.multiple_of((1 - bit) * rows, rows), rows), :] = other_ref[...]
 
 
 def ring_kernel(*refs):
@@ -545,14 +542,14 @@
     projection = projection.transpose(1, 0, 2)
     sends = (shape((4, sent), F32),) * 2
     wide = pltpu.VMEM((LANES, own), F32)
-    slab = (features // 8, features)
+    slab = (features // 4, features)
     counts = neighbour_count.reshape(1, own)
 
-    def count(part, neighbours):
+    def count(part):
         return call(
             functools.partial(count_kernel, part),
             shape((ghosts, own), F32),
-            [pltpu.VMEM((NEIGH, own), jnp.int32)],
+            [pltpu.VMEM((NEIGH, own), F32)],
         )(neighbours, counts)
 
     own_call = call(
@@ -609,44 +606,41 @@
         LIMIT,
     )
 
-    above = passed_along(position, "bead", -1)
     to_near, to_far = call(first_kernel, sends, [wide])(position, species, send_lists)
-    part = after(matrix_part(points, point_weights), to_near, to_far)
+    part = matrix_part(points, point_weights)
+    sent_part = part.astype(BF16)
     for step in range(STEPS):
         last = step == STEPS - 1
         if step == 0:
-            other = routed(part, "bead", lambda i: i ^ 4)
-            to_far = after(to_far, part)
+            other = across(sent_part)
+            number = [count(k) for k in range(3)]
+            part, held = call(add_kernel, (shape(slab, F32), shape(slab, BF16)))(
+                part, after(other, to_far, to_near, *number)
+            )
+            other = routed(held, "bead", lambda i: i ^ 1)
+            to_far, to_near = after(to_far, held), after(to_near, held)
         from_far = far_pair(to_far)
         from_near = near_pair(to_near)
-        cols, waves, turned = own_call(position, species, projection, phase_shift)
+        start = after(position, held) if step == 0 else position
+        cols, waves, turned = own_call(start, species, projection, phase_shift)
         if step == 0:
-            number = []
             part, held = call(add_kernel, (shape(slab, F32), shape(slab, BF16)))(
                 part, after(other, cols, from_far, from_near)
             )
-            other = routed(held, "bead", lambda i: i ^ 1)
-            number.append(count(0, after(neighbours, held)))
-            part, held = call(add_kernel, (shape(slab, F32), shape(slab, BF16)))(
-                part, after(other, number[-1])
+            other = routed(held, "bead", lambda i: i ^ 3)
+            above = passed_along(after(position, held), "bead", -1)
+            state = weigh_call(
+                after(position, held), from_near, from_far, cols, projection, *number
             )
-            other = routed(held, "bead", lambda i: i ^ 2)
-            number.append(count(1, after(neighbours, held)))
-            held = call(add_kernel, (shape(slab, BF16),))(part, after(other, number[-1]))[0]
-            other = routed(held, "dom", lambda i: i ^ 2)
-            number.append(count(2, after(neighbours, held)))
-            state = weigh_call(position, from_near, from_far, cols, projection, *number)
             ghost_cols, weight, weight_turned, ghost_waves = state
-            held = call(pair_kernel, shape((2 * slab[0], features), BF16))(
-                held, after(other, *state)
-            )
+            held = call(add_kernel, (shape(slab, BF16),))(part, after(other, above, *state))[0]
             pieces = [held] + [routed(held, "dom", lambda i: (i - 4 * k) % 16) for k in (1, 2, 3)]
             sines, low = describe_call(after(weight_turned, held), waves, ghost_waves, turned)
             half = call(ring_kernel, shape((features, features), BF16))(
                 pieces[0], *[after(piece, low) for piece in pieces[1:]]
             )
             other_half = near_pair(half)
-            below = passed_along(after(position, other_half), "bead", 1)
+            below = passed_along(after(position, half), "bead", 1)
         else:
             above = passed_along(after(position, cols, from_far, from_near), "bead", -1)
             ghost_cols, weight, weight_turned, ghost_waves = weigh_call(

time: 85.4 us -> 72.6 us (0.85)
  Pallas kernels: 43.2 us -> 31.3 us
  starting transfers between devices: 30.4 us -> 23.4 us
  waiting for transfers between devices: 7.94 us -> 14 us
    ppermute x4, waiting for transfers between devices: 0.01 us -> 7.1 us  [passed_along(): return lax.ppermute(block, axis, route)]
    ppermute x16 -> x14, starting transfers between devices: 20 us -> 13.1 us  [routed(): lax.ppermute(block, axis, [(source(i), i) for i in range(lax.axis_size(ax...]
    pallas_call x2, Pallas kernels: 10.6 us -> 6.99 us  [shards(): own_force_call(grad, spread, sines, waves, weight, cols, position, centre...]
    ppermute x4, starting transfers between devices: 10.5 us -> 7.29 us  [passed_along(): return lax.ppermute(block, axis, route)]
    ppermute x0 -> x1, starting transfers between devices: none -> 3.09 us  [across(): return lax.ppermute(block, ('dom', 'bead'), route)]
    pallas_call x3, Pallas kernels: 5.41 us -> 3.22 us  [count(): call(functools.partial(count_kernel, part), shape((ghosts, own), F32), [p...]
    pallas_call x2, Pallas kernels: 7.63 us -> 5.55 us  [shards(): ghost_force_call(low, half, other_half, cols, turned, weight, ghost_waves...]
    pallas_call x5 -> x4, Pallas kernels: 9.32 us -> 7.48 us  [the longest x2 5.73 us: shards(): cols, waves, turned = own_call(start, species, projection, phase_shift)]
  transfers between devices with their start and end apart: 20 -> 19, of which waited for: 5 -> 6; matrix products, arithmetic and copies ran while one was open for 0% -> 0% of each run, Pallas kernels for 48% -> 40%
where the time goes in v3:
time: 72.6 us; the launch traced here: 72.4 us
  Pallas kernels  31.3 us (43%)
  starting transfers between devices  23.4 us (32%)
  waiting for transfers between devices  14 us (19%)
  local copies, waits for them, and re-layouts  1.6 us (2%)
  between operations  0.98 us (1%)
    ppermute x14, starting transfers between devices, routed(): lax.ppermute(block, axis, [(source(i), i) for i in range(lax.axis_size(ax...  13.1 us
    ppermute x4, starting transfers between devices, passed_along(): return lax.ppermute(block, axis, route)  7.29 us
    ppermute x4, waiting for transfers between devices, passed_along(): return lax.ppermute(block, axis, route)  7.1 us
    pallas_call x2, Pallas kernels, shards(): own_force_call(grad, spread, sines, waves, weight, cols, position, centre...  6.99 us
    ppermute x14, waiting for transfers between devices, routed(): lax.ppermute(block, axis, [(source(i), i) for i in range(lax.axis_size(ax...  6.89 us
    pallas_call x2, Pallas kernels, shards(): cols, waves, turned = own_call(start, species, projection, phase_shift)  5.73 us
    pallas_call x2, Pallas kernels, shards(): ghost_force_call(low, half, other_half, cols, turned, weight, ghost_waves...  5.55 us
    pallas_call x3, Pallas kernels, count(): call(functools.partial(count_kernel, part), shape((ghosts, own), F32), [p...  3.22 us
  transfers between devices with their start and end apart: 19, of which 6 were waited for; matrix products, arithmetic and copies ran while one was open for 0% of the time, Pallas kernels for 40%

profile of v3, /device:TPU:6, one launch (start us, length us, event | category | flops | bytes accessed | tf_op | source)
XLA Modules:
  0.0 72.4 jit_solution(1382339554203451185)
XLA Ops:
  0.7 1.0 %copy-done = bf16[2,250,512]{2,0,1:T(2,128)(2,1)S(1)} copy-done((bf16[2,250,512]{2,0,1:T(2,128)(2,1)S(1)}, bf16[2,250,512]{2,0,1:T(2,128)(2,1)}, u32[]{:S(2)}) %copy-start) | copy-done | bytes 512024
  2.3 0.7 convert_multiply_fusion
  3.4 3.1 %collective-permute-start = (bf16[128,512]{1,0:T(8,128)(2,1)S(1)}, bf16[128,512]{1,0:T(8,128)(2,1)S(1)}, u32[]{:S(2)}, u32[]{:S(2)}) collective-permute-start(bf16[128,512]{1,0:T(8,128)(2,1)S(1)} %get-tuple-element.110), channel_id=1, source_target_pairs={{20,0},{21,1},{22,2},{23,3},{16,4},{17,5},{18,6},{19,7},{28,8},{29... | collective-permute-start | bytes 393224 | tf_op jit(solution)/shard_map/ppermute | solution.py:486
  6.5 1.1 %shard_map.114.rest_0_ = f32[256,512]{1,0:T(8,128)S(1)} custom-call(s32[32,512]{1,0:T(8,128)S(1)} %copy-done.2, s32[1,512]{1,0:T(1,128)S(1)} %bitcast.33), custom_call_target="tpu_custom_call" | custom-call | tf_op jit(solution)/shard_map/pallas_call | solution.py:549
  7.6 1.1 %shard_map.115.rest_1_ = f32[256,512]{1,0:T(8,128)S(1)} custom-call(s32[32,512]{1,0:T(8,128)S(1)} %copy-done.2, s32[1,512]{1,0:T(1,128)S(1)} %bitcast.34), custom_call_target="tpu_custom_call" | custom-call | tf_op jit(solution)/shard_map/pallas_call | solution.py:549
  8.6 1.1 %shard_map.116.rest_2_ = f32[256,512]{1,0:T(8,128)S(1)} custom-call(s32[32,512]{1,0:T(8,128)S(1)} %copy-done.2, s32[1,512]{1,0:T(1,128)S(1)} %bitcast.35), custom_call_target="tpu_custom_call" | custom-call | tf_op jit(solution)/shard_map/pallas_call | solution.py:549
  10.3 0.9 %collective-permute-start.1 = (bf16[128,512]{1,0:T(8,128)(2,1)S(1)}, bf16[128,512]{1,0:T(8,128)(2,1)S(1)}, u32[]{:S(2)}, u32[]{:S(2)}) collective-permute-start(bf16[128,512]{1,0:T(8,128)(2,1)S(1)} %get-tuple-element.60), channel_id=1, source_target_pairs={{1,0},{0,1},{3,2},{2,3},{5,4},{4,5},{7,6},{6,7},{9,8},{8,9},{11,10... | collective-permute-start | bytes 393224 | tf_op jit(solution)/shard_map/ppermute | solution.py:472
  11.2 2.5 %collective-permute-start.2 = (f32[4,128]{1,0:T(4,128)S(1)}, f32[4,128]{1,0:T(4,128)S(1)}, u32[]{:S(2)}, u32[]{:S(2)}) collective-permute-start(f32[4,128]{1,0:T(4,128)S(1)} %get-tuple-element.63), channel_id=1, source_target_pairs={{120,0},{16,8},{8,16},{32,24},{24,32},{48,40},{40,48},{64,56},{56,... | collective-permute-start | bytes 6152 | tf_op jit(solution)/shard_map/ppermute | solution.py:472
  13.7 2.9 %shard_map.118 = (f32[512,128]{1,0:T(8,128)S(1)}, bf16[512,2048]{1,0:T(8,128)(2,1)S(1)}, f32[512,2048]{1,0:T(8,128)S(1)}) custom-call(f32[3,1,512]{2,1,0:T(1,128)S(1)} %bitcast.21, s32[1,512]{1,0:T(1,128)S(1)} %bitcast.29, f32[3,2,512]{2,1,0:T(2,128)S(1)} %bitcast.12, f32[2,512]{1,0:T(2,128)S(1)} %copy-done.6), custom_call_target="tpu_custom_call" | custom-call | tf_op jit(solution)/shard_map/pallas_call | solution.py:625
  16.6 1.2 %collective-permute-start.4 = (bf16[128,512]{1,0:T(8,128)(2,1)S(1)}, bf16[128,512]{1,0:T(8,128)(2,1)S(1)}, u32[]{:S(2)}, u32[]{:S(2)}) collective-permute-start(bf16[128,512]{1,0:T(8,128)(2,1)S(1)} %get-tuple-element.66), channel_id=1, source_target_pairs={{3,0},{2,1},{1,2},{0,3},{7,4},{6,5},{5,6},{4,7},{11,8},{10,9},{9,1... | collective-permute-start | bytes 393224 | tf_op jit(solution)/shard_map/ppermute | solution.py:472
  18.0 1.7 %shard_map.120 = (f32[256,128]{1,0:T(8,128)S(1)}, f32[768,512]{1,0:T(8,128)S(1)}, bf16[512,768]{1,0:T(8,128)(2,1)S(1)}, bf16[256,2048]{1,0:T(8,128)(2,1)S(1)}) custom-call(f32[3,1,512]{2,1,0:T(1,128)S(1)} %bitcast.23, f32[4,128]{1,0:T(4,128)S(1)} %collective-permute-done.3.near_ref, f32[4,128]{1,0:T(4,128)S(1)} %collective-permute-done.2.far_ref, ...), custom_call_target="tpu_custom_call" | custom-call | tf_op jit(solution)/shard_map/pallas_call | solution.py:632
  19.7 7.1 %collective-permute-done.5.above_ref = f32[3,1,512]{2,1,0:T(1,128)S(1)} collective-permute-done((f32[3,1,512]{2,1,0:T(1,128)S(1)}, f32[3,1,512]{2,1,0:T(1,128)S(1)}, u32[]{:S(2)}, u32[]{:S(2)}) %collective-permute-start.5) | collective-permute-done | bytes 6176 | tf_op jit(solution)/shard_map/ppermute | solution.py:468
  26.9 2.0 %collective-permute-start.8 = (bf16[128,512]{1,0:T(8,128)(2,1)S(1)}, bf16[128,512]{1,0:T(8,128)(2,1)S(1)}, u32[]{:S(2)}, u32[]{:S(2)}) collective-permute-start(bf16[128,512]{1,0:T(8,128)(2,1)S(1)} %shard_map.121.refs_0_), channel_id=1, source_target_pairs={{32,0},{40,8},{48,16},{56,24},{64,32},{72,40},{80,48},{88,56},{96,... | collective-permute-start | bytes 393224 | tf_op jit(solution)/shard_map/ppermute | solution.py:472
  28.9 1.1 %collective-permute-start.6 = (bf16[128,512]{1,0:T(8,128)(2,1)S(1)}, bf16[128,512]{1,0:T(8,128)(2,1)S(1)}, u32[]{:S(2)}, u32[]{:S(2)}) collective-permute-start(bf16[128,512]{1,0:T(8,128)(2,1)S(1)} %shard_map.121.refs_0_), channel_id=1, source_target_pairs={{96,0},{104,8},{112,16},{120,24},{0,32},{8,40},{16,48},{24,56},{32... | collective-permute-start | bytes 393224 | tf_op jit(solution)/shard_map/ppermute | solution.py:472
  30.1 1.9 %shard_map.122 = (f32[512,1024]{1,0:T(8,128)S(1)}, bf16[512,512]{1,0:T(8,128)(2,1)S(1)}) custom-call(bf16[512,768]{1,0:T(8,128)(2,1)S(1)} %get-tuple-element.74.weight_turned, bf16[512,2048]{1,0:T(8,128)(2,1)S(1)} %get-tuple-element.75.own_waves.waves, bf16[256,2048]{1,0:T(8,128)(2,1)S(1)} %get-tuple-element.72.ghost_waves.waves, ...), custom_call_target="tpu_custom_call" | custom-call | tf_op jit(solution)/shard_map/pallas_call | solution.py:638
  32.0 1.1 %collective-permute-done.8.refs_3_ = bf16[128,512]{1,0:T(8,128)(2,1)S(1)} collective-permute-done((bf16[128,512]{1,0:T(8,128)(2,1)S(1)}, bf16[128,512]{1,0:T(8,128)(2,1)S(1)}, u32[]{:S(2)}, u32[]{:S(2)}) %collective-permute-start.8) | collective-permute-done | bytes 131104 | tf_op jit(solution)/shard_map/ppermute | solution.py:472
  33.2 2.7 %collective-permute-done.7.refs_2_ = bf16[128,512]{1,0:T(8,128)(2,1)S(1)} collective-permute-done((bf16[128,512]{1,0:T(8,128)(2,1)S(1)}, bf16[128,512]{1,0:T(8,128)(2,1)S(1)}, u32[]{:S(2)}, u32[]{:S(2)}) %collective-permute-start.7) | collective-permute-done | bytes 131104 | tf_op jit(solution)/shard_map/ppermute | solution.py:472
  35.8 1.1 %collective-permute-done.6.refs_1_ = bf16[128,512]{1,0:T(8,128)(2,1)S(1)} collective-permute-done((bf16[128,512]{1,0:T(8,128)(2,1)S(1)}, bf16[128,512]{1,0:T(8,128)(2,1)S(1)}, u32[]{:S(2)}, u32[]{:S(2)}) %collective-permute-start.6) | collective-permute-done | bytes 131104 | tf_op jit(solution)/shard_map/ppermute | solution.py:472
  37.1 1.4 %collective-permute-start.12 = (f32[3,1,512]{2,1,0:T(1,128)S(1)}, f32[3,1,512]{2,1,0:T(1,128)S(1)}, u32[]{:S(2)}, u32[]{:S(2)}) collective-permute-start(f32[3,1,512]{2,1,0:T(1,128)S(1)} %bitcast.24), channel_id=1, source_target_pairs={{7,0},{0,1},{1,2},{2,3},{3,4},{4,5},{5,6},{6,7},{15,8},{8,9},{9,10... | collective-permute-start | bytes 18440 | tf_op jit(solution)/shard_map/ppermute | solution.py:468
  39.0 2.8 %shard_map.124 = (f32[512,512]{1,0:T(8,128)S(1)}, bf16[512,2048]{1,0:T(8,128)(2,1)S(1)}, f32[3,512]{1,0:T(4,128)S(1)}, f32[3,128]{1,0:T(4,128)S(1)}, f32[3,128]{1,0:T(4,128)S(1)}) custom-call(bf16[512,512]{1,0:T(8,128)(2,1)S(1)} %get-tuple-element.77.low, bf16[512,512]{1,0:T(8,128)(2,1)S(1)} %shard_map.123.half_ref, ...), custom_call_target="tpu_custom_call" | custom-call | tf_op jit(solution)/shard_map/pallas_call | solution.py:651
  42.2 3.5 %shard_map.125.force_ref = f32[3,512]{1,0:T(4,128)S(1)} custom-call(f32[512,512]{1,0:T(8,128)S(1)} %get-tuple-element.81.grad, bf16[512,2048]{1,0:T(8,128)(2,1)S(1)} %get-tuple-element.82.spread, f32[512,1024]{1,0:T(8,128)S(1)} %get-tuple-element.83.sines, bf16[512,2048]{1,0:T(8,128)(2,1)S(1)} %get-tuple-element.75.own_waves.waves, ...), custom_call_target="tpu_custom_call" | custom-call | tf_op jit(solution)/shard_map/pallas_call | solution.py:665
  45.7 1.4 %collective-permute-done.11.far_back_ref = f32[3,128]{1,0:T(4,128)S(1)} collective-permute-done((f32[3,128]{1,0:T(4,128)S(1)}, f32[3,128]{1,0:T(4,128)S(1)}, u32[]{:S(2)}, u32[]{:S(2)}) %collective-permute-start.11) | collective-permute-done | bytes 1568 | tf_op jit(solution)/shard_map/ppermute | solution.py:472
  47.1 0.9 %shard_map.126 = (f32[3,1,512]{2,1,0:T(1,128)S(1)}, f32[3,1,512]{2,1,0:T(1,128)S(1)}, f32[4,128]{1,0:T(4,128)S(1)}, f32[4,128]{1,0:T(4,128)S(1)}) custom-call(f32[3,512]{1,0:T(4,128)S(1)} %shard_map.125.force_ref, f32[3,128]{1,0:T(4,128)S(1)} %collective-permute-done.10.near_back_ref, f32[3,128]{1,0:T(4,128)S(1)} %collective-permute-done.11.far_back_ref, ...), custom_call_target="tpu_custom_call" | custom-call | tf_op jit(solution)/shard_map/pallas_call | solution.py:669
  48.1 2.6 %collective-permute-start.14 = (f32[4,128]{1,0:T(4,128)S(1)}, f32[4,128]{1,0:T(4,128)S(1)}, u32[]{:S(2)}, u32[]{:S(2)}) collective-permute-start(f32[4,128]{1,0:T(4,128)S(1)} %get-tuple-element.90), channel_id=1, source_target_pairs={{120,0},{16,8},{8,16},{32,24},{24,32},{48,40},{40,48},{64,56},{56,... | collective-permute-start | bytes 6152 | tf_op jit(solution)/shard_map/ppermute | solution.py:472
  50.7 2.9 %shard_map.127 = (f32[512,128]{1,0:T(8,128)S(1)}, bf16[512,2048]{1,0:T(8,128)(2,1)S(1)}, f32[512,2048]{1,0:T(8,128)S(1)}) custom-call(f32[3,1,512]{2,1,0:T(1,128)S(1)} %get-tuple-element.107.position_ref, s32[1,512]{1,0:T(1,128)S(1)} %bitcast.31, f32[3,2,512]{2,1,0:T(2,128)S(1)} %bitcast.16, f32[2,512]{1,0:T(2,128)S(1)} %copy-done.6), custom_call_target="tpu_custom_call" | custom-call | tf_op jit(solution)/shard_map/pallas_call | solution.py:625
  53.9 1.7 %shard_map.128 = (f32[256,128]{1,0:T(8,128)S(1)}, f32[768,512]{1,0:T(8,128)S(1)}, bf16[512,768]{1,0:T(8,128)(2,1)S(1)}, bf16[256,2048]{1,0:T(8,128)(2,1)S(1)}) custom-call(f32[3,1,512]{2,1,0:T(1,128)S(1)} %get-tuple-element.107.position_ref, f32[4,128]{1,0:T(4,128)S(1)} %collective-permute-done.13.near_ref, f32[4,128]{1,0:T(4,128)S(1)} %collective-permute-done.14.far_ref, ...), custom_call_target="tpu_custom_call" | custom-call | tf_op jit(solution)/shard_map/pallas_call | solution.py:646
  55.6 1.9 %shard_map.129 = (f32[512,1024]{1,0:T(8,128)S(1)}, bf16[512,512]{1,0:T(8,128)(2,1)S(1)}) custom-call(bf16[512,768]{1,0:T(8,128)(2,1)S(1)} %get-tuple-element.92.weight_turned, bf16[512,2048]{1,0:T(8,128)(2,1)S(1)} %get-tuple-element.93.own_waves.waves, bf16[256,2048]{1,0:T(8,128)(2,1)S(1)} %get-tuple-element.94.ghost_waves.waves, ...), custom_call_target="tpu_custom_call" | custom-call | tf_op jit(solution)/shard_map/pallas_call | solution.py:649
  57.5 5.5 %collective-permute-start.17 = (f32[3,1,512]{2,1,0:T(1,128)S(1)}, f32[3,1,512]{2,1,0:T(1,128)S(1)}, u32[]{:S(2)}, u32[]{:S(2)}) collective-permute-start(f32[3,1,512]{2,1,0:T(1,128)S(1)} %get-tuple-element.107.position_ref), channel_id=1, source_target_pairs={{7,0},{0,1},{1,2},{2,3},{3,4},{4,5},{5,6},{6,7},{15,8},{8,9},{9,10... | collective-permute-start | bytes 18440 | tf_op jit(solution)/shard_map/ppermute | solution.py:468
  63.0 2.8 %shard_map.130 = (f32[512,512]{1,0:T(8,128)S(1)}, bf16[512,2048]{1,0:T(8,128)(2,1)S(1)}, f32[3,512]{1,0:T(4,128)S(1)}, f32[3,128]{1,0:T(4,128)S(1)}, f32[3,128]{1,0:T(4,128)S(1)}) custom-call(bf16[512,512]{1,0:T(8,128)(2,1)S(1)} %get-tuple-element.96.low, bf16[512,512]{1,0:T(8,128)(2,1)S(1)} %shard_map.123.half_ref, ...), custom_call_target="tpu_custom_call" | custom-call | tf_op jit(solution)/shard_map/pallas_call | solution.py:651
  65.9 1.9 %collective-permute-start.16 = (f32[3,128]{1,0:T(4,128)S(1)}, f32[3,128]{1,0:T(4,128)S(1)}, u32[]{:S(2)}, u32[]{:S(2)}) collective-permute-start(f32[3,128]{1,0:T(4,128)S(1)} %get-tuple-element.104), channel_id=1, source_target_pairs={{120,0},{16,8},{8,16},{32,24},{24,32},{48,40},{40,48},{64,56},{56,... | collective-permute-start | bytes 4616 | tf_op jit(solution)/shard_map/ppermute | solution.py:472
  67.8 3.5 %shard_map.131.force_ref = f32[3,512]{1,0:T(4,128)S(1)} custom-call(f32[512,512]{1,0:T(8,128)S(1)} %get-tuple-element.99.grad, bf16[512,2048]{1,0:T(8,128)(2,1)S(1)} %get-tuple-element.100.spread, f32[512,1024]{1,0:T(8,128)S(1)} %get-tuple-element.101.sines, bf16[512,2048]{1,0:T(8,128)(2,1)S(1)} %get-tuple-element.93.own_waves.waves, ...), custom_call_target="tpu_custom_call" | custom-call | tf_op jit(solution)/shard_map/pallas_call | solution.py:665
  71.4 1.0 %shard_map.132 = (f32[3,1,512]{2,1,0:T(1,128)}, f32[3,1,512]{2,1,0:T(1,128)}) custom-call(f32[3,512]{1,0:T(4,128)S(1)} %shard_map.131.force_ref, f32[3,128]{1,0:T(4,128)S(1)} %collective-permute-done.15.near_back_ref, f32[3,128]{1,0:T(4,128)S(1)} %collective-permute-done.16.far_back_ref, s32[2,128]{1,0:T(2,128)S(1)} %copy-done.7, ...), custom_call_target="tpu_custom_call" | custom-call | tf_op jit(solution)/shard_map/pallas_call | solution.py:669
  (48 shorter events, 3.4 us)
Async XLA Ops:
  0.6 1.0 %copy-start = (bf16[2,250,512]{2,0,1:T(2,128)(2,1)S(1)}, bf16[2,250,512]{2,0,1:T(2,128)(2,1)}, u32[]{:S(2)}) copy-start(bf16[2,250,512]{2,0,1:T(2,128)(2,1)} %param.18) | copy-start | bytes 1536004
  0.6 5.8 %copy-start.5 = (s32[512]{0:T(512)S(1)}, s32[512]{0:T(512)}, u32[]{:S(2)}) copy-start(s32[512]{0:T(512)} %param.14) | copy-start | bytes 6148
  0.7 5.8 %copy-start.2 = (s32[32,512]{1,0:T(8,128)S(1)}, s32[32,512]{1,0:T(8,128)}, u32[]{:S(2)}) copy-start(s32[32,512]{1,0:T(8,128)} %neighbours_ref.5) | copy-start | bytes 196612
  1.7 8.1 %copy-start.3 = (f32[1,3,512]{2,0,1:T(1,128)S(1)}, f32[1,3,512]{2,0,1:T(1,128)}, u32[]{:S(2)}) copy-start(f32[1,3,512]{2,0,1:T(1,128)} %param.10) | copy-start | bytes 18436
  1.7 8.1 %copy-start.4 = (s32[512]{0:T(512)S(1)}, s32[512]{0:T(512)}, u32[]{:S(2)}) copy-start(s32[512]{0:T(512)} %param.12) | copy-start | bytes 6148
  1.7 8.1 %copy-start.7 = (s32[2,128]{1,0:T(2,128)S(1)}, s32[2,128]{1,0:T(2,128)}, u32[]{:S(2)}) copy-start(s32[2,128]{1,0:T(2,128)} %lists_ref.5) | copy-start | bytes 3076
  1.7 12.0 %copy-start.1 = (f32[2,3,512]{2,0,1:T(2,128)S(1)}, f32[2,3,512]{2,0,1:T(2,128)}, u32[]{:S(2)}) copy-start(f32[2,3,512]{2,0,1:T(2,128)} %param.16) | copy-start | bytes 36868
  1.7 12.0 %copy-start.6 = (f32[2,512]{1,0:T(2,128)S(1)}, f32[2,512]{1,0:T(2,128)}, u32[]{:S(2)}) copy-start(f32[2,512]{1,0:T(2,128)} %shift_ref.3) | copy-start | bytes 12292
  3.4 6.8 %collective-permute-start = (bf16[128,512]{1,0:T(8,128)(2,1)S(1)}, bf16[128,512]{1,0:T(8,128)(2,1)S(1)}, u32[]{:S(2)}, u32[]{:S(2)}) collective-permute-start(bf16[128,512]{1,0:T(8,128)(2,1)S(1)} %get-tuple-element.110), channel_id=1, source_target_pairs={{20,0},{21,1},{22,2},{23,3},{16,4},{17,5},{18,6},{19,7},{28,8},{29... | collective-permute-start | bytes 393224 | tf_op jit(solution)/shard_map/ppermute | solution.py:486
  10.3 6.3 %collective-permute-start.1 = (bf16[128,512]{1,0:T(8,128)(2,1)S(1)}, bf16[128,512]{1,0:T(8,128)(2,1)S(1)}, u32[]{:S(2)}, u32[]{:S(2)}) collective-permute-start(bf16[128,512]{1,0:T(8,128)(2,1)S(1)} %get-tuple-element.60), channel_id=1, source_target_pairs={{1,0},{0,1},{3,2},{2,3},{5,4},{4,5},{7,6},{6,7},{9,8},{8,9},{11,10... | collective-permute-start | bytes 393224 | tf_op jit(solution)/shard_map/ppermute | solution.py:472
  11.2 5.4 %collective-permute-start.2 = (f32[4,128]{1,0:T(4,128)S(1)}, f32[4,128]{1,0:T(4,128)S(1)}, u32[]{:S(2)}, u32[]{:S(2)}) collective-permute-start(f32[4,128]{1,0:T(4,128)S(1)} %get-tuple-element.63), channel_id=1, source_target_pairs={{120,0},{16,8},{8,16},{32,24},{24,32},{48,40},{40,48},{64,56},{56,... | collective-permute-start | bytes 6152 | tf_op jit(solution)/shard_map/ppermute | solution.py:472
  13.7 2.9 %collective-permute-start.3 = (f32[4,128]{1,0:T(4,128)S(1)}, f32[4,128]{1,0:T(4,128)S(1)}, u32[]{:S(2)}, u32[]{:S(2)}) collective-permute-start(f32[4,128]{1,0:T(4,128)S(1)} %get-tuple-element.64), channel_id=1, source_target_pairs={{8,0},{0,8},{24,16},{16,24},{40,32},{32,40},{56,48},{48,56},{72,64... | collective-permute-start | bytes 6152 | tf_op jit(solution)/shard_map/ppermute | solution.py:472
  16.6 10.2 %collective-permute-start.4 = (bf16[128,512]{1,0:T(8,128)(2,1)S(1)}, bf16[128,512]{1,0:T(8,128)(2,1)S(1)}, u32[]{:S(2)}, u32[]{:S(2)}) collective-permute-start(bf16[128,512]{1,0:T(8,128)(2,1)S(1)} %get-tuple-element.66), channel_id=1, source_target_pairs={{3,0},{2,1},{1,2},{0,3},{7,4},{6,5},{5,6},{4,7},{11,8},{10,9},{9,1... | collective-permute-start | bytes 393224 | tf_op jit(solution)/shard_map/ppermute | solution.py:472
  17.9 9.0 %collective-permute-start.5 = (f32[3,1,512]{2,1,0:T(1,128)S(1)}, f32[3,1,512]{2,1,0:T(1,128)S(1)}, u32[]{:S(2)}, u32[]{:S(2)}) collective-permute-start(f32[3,1,512]{2,1,0:T(1,128)S(1)} %bitcast.22), channel_id=1, source_target_pairs={{1,0},{2,1},{3,2},{4,3},{5,4},{6,5},{7,6},{0,7},{9,8},{10,9},{11,1... | collective-permute-start | bytes 18440 | tf_op jit(solution)/shard_map/ppermute | solution.py:468
  26.9 6.3 %collective-permute-start.8 = (bf16[128,512]{1,0:T(8,128)(2,1)S(1)}, bf16[128,512]{1,0:T(8,128)(2,1)S(1)}, u32[]{:S(2)}, u32[]{:S(2)}) collective-permute-start(bf16[128,512]{1,0:T(8,128)(2,1)S(1)} %shard_map.121.refs_0_), channel_id=1, source_target_pairs={{32,0},{40,8},{48,16},{56,24},{64,32},{72,40},{80,48},{88,56},{96,... | collective-permute-start | bytes 393224 | tf_op jit(solution)/shard_map/ppermute | solution.py:472
  28.8 7.0 %collective-permute-start.7 = (bf16[128,512]{1,0:T(8,128)(2,1)S(1)}, bf16[128,512]{1,0:T(8,128)(2,1)S(1)}, u32[]{:S(2)}, u32[]{:S(2)}) collective-permute-start(bf16[128,512]{1,0:T(8,128)(2,1)S(1)} %shard_map.121.refs_0_), channel_id=1, source_target_pairs={{64,0},{72,8},{80,16},{88,24},{96,32},{104,40},{112,48},{120,56},{... | collective-permute-start | bytes 393224 | tf_op jit(solution)/shard_map/ppermute | solution.py:472
  28.9 8.0 %collective-permute-start.6 = (bf16[128,512]{1,0:T(8,128)(2,1)S(1)}, bf16[128,512]{1,0:T(8,128)(2,1)S(1)}, u32[]{:S(2)}, u32[]{:S(2)}) collective-permute-start(bf16[128,512]{1,0:T(8,128)(2,1)S(1)} %shard_map.121.refs_0_), channel_id=1, source_target_pairs={{96,0},{104,8},{112,16},{120,24},{0,32},{8,40},{16,48},{24,56},{32... | collective-permute-start | bytes 393224 | tf_op jit(solution)/shard_map/ppermute | solution.py:472
  37.0 2.0 %collective-permute-start.9 = (bf16[512,512]{1,0:T(8,128)(2,1)S(1)}, bf16[512,512]{1,0:T(8,128)(2,1)S(1)}, u32[]{:S(2)}, u32[]{:S(2)}) collective-permute-start(bf16[512,512]{1,0:T(8,128)(2,1)S(1)} %shard_map.123.half_ref), channel_id=1, source_target_pairs={{8,0},{0,8},{24,16},{16,24},{40,32},{32,40},{56,48},{48,56},{72,64... | collective-permute-start | bytes 1572872 | tf_op jit(solution)/shard_map/ppermute | solution.py:472
  37.1 8.6 %collective-permute-start.12 = (f32[3,1,512]{2,1,0:T(1,128)S(1)}, f32[3,1,512]{2,1,0:T(1,128)S(1)}, u32[]{:S(2)}, u32[]{:S(2)}) collective-permute-start(f32[3,1,512]{2,1,0:T(1,128)S(1)} %bitcast.24), channel_id=1, source_target_pairs={{7,0},{0,1},{1,2},{2,3},{3,4},{4,5},{5,6},{6,7},{15,8},{8,9},{9,10... | collective-permute-start | bytes 18440 | tf_op jit(solution)/shard_map/ppermute | solution.py:468
  41.8 3.9 %collective-permute-start.10 = (f32[3,128]{1,0:T(4,128)S(1)}, f32[3,128]{1,0:T(4,128)S(1)}, u32[]{:S(2)}, u32[]{:S(2)}) collective-permute-start(f32[3,128]{1,0:T(4,128)S(1)} %get-tuple-element.85), channel_id=1, source_target_pairs={{8,0},{0,8},{24,16},{16,24},{40,32},{32,40},{56,48},{48,56},{72,64... | collective-permute-start | bytes 4616 | tf_op jit(solution)/shard_map/ppermute | solution.py:472
  42.0 5.1 %collective-permute-start.11 = (f32[3,128]{1,0:T(4,128)S(1)}, f32[3,128]{1,0:T(4,128)S(1)}, u32[]{:S(2)}, u32[]{:S(2)}) collective-permute-start(f32[3,128]{1,0:T(4,128)S(1)} %get-tuple-element.86), channel_id=1, source_target_pairs={{120,0},{16,8},{8,16},{32,24},{24,32},{48,40},{40,48},{64,56},{56,... | collective-permute-start | bytes 4616 | tf_op jit(solution)/shard_map/ppermute | solution.py:472
  42.2 4.9 %copy-start.8 = (f32[1,3,512]{2,0,1:T(1,128)S(1)}, f32[1,3,512]{2,0,1:T(1,128)}, u32[]{:S(2)}) copy-start(f32[1,3,512]{2,0,1:T(1,128)} %param.11) | copy-start | bytes 18436
  48.0 5.6 %collective-permute-start.13 = (f32[4,128]{1,0:T(4,128)S(1)}, f32[4,128]{1,0:T(4,128)S(1)}, u32[]{:S(2)}, u32[]{:S(2)}) collective-permute-start(f32[4,128]{1,0:T(4,128)S(1)} %get-tuple-element.89), channel_id=1, source_target_pairs={{8,0},{0,8},{24,16},{16,24},{40,32},{32,40},{56,48},{48,56},{72,64... | collective-permute-start | bytes 6152 | tf_op jit(solution)/shard_map/ppermute | solution.py:472
  48.1 5.5 %collective-permute-start.14 = (f32[4,128]{1,0:T(4,128)S(1)}, f32[4,128]{1,0:T(4,128)S(1)}, u32[]{:S(2)}, u32[]{:S(2)}) collective-permute-start(f32[4,128]{1,0:T(4,128)S(1)} %get-tuple-element.90), channel_id=1, source_target_pairs={{120,0},{16,8},{8,16},{32,24},{24,32},{48,40},{40,48},{64,56},{56,... | collective-permute-start | bytes 6152 | tf_op jit(solution)/shard_map/ppermute | solution.py:472
  53.6 17.8 %collective-permute-start.18 = (f32[3,1,512]{2,1,0:T(1,128)S(1)}, f32[3,1,512]{2,1,0:T(1,128)S(1)}, u32[]{:S(2)}, u32[]{:S(2)}) collective-permute-start(f32[3,1,512]{2,1,0:T(1,128)S(1)} %get-tuple-element.107.position_ref), channel_id=1, source_target_pairs={{1,0},{2,1},{3,2},{4,3},{5,4},{6,5},{7,6},{0,7},{9,8},{10,9},{11,1... | collective-permute-start | bytes 18440 | tf_op jit(solution)/shard_map/ppermute | solution.py:468
  57.5 13.8 %collective-permute-start.17 = (f32[3,1,512]{2,1,0:T(1,128)S(1)}, f32[3,1,512]{2,1,0:T(1,128)S(1)}, u32[]{:S(2)}, u32[]{:S(2)}) collective-permute-start(f32[3,1,512]{2,1,0:T(1,128)S(1)} %get-tuple-element.107.position_ref), channel_id=1, source_target_pairs={{7,0},{0,1},{1,2},{2,3},{3,4},{4,5},{5,6},{6,7},{15,8},{8,9},{9,10... | collective-permute-start | bytes 18440 | tf_op jit(solution)/shard_map/ppermute | solution.py:468
  65.8 5.5 %collective-permute-start.15 = (f32[3,128]{1,0:T(4,128)S(1)}, f32[3,128]{1,0:T(4,128)S(1)}, u32[]{:S(2)}, u32[]{:S(2)}) collective-permute-start(f32[3,128]{1,0:T(4,128)S(1)} %get-tuple-element.103), channel_id=1, source_target_pairs={{8,0},{0,8},{24,16},{16,24},{40,32},{32,40},{56,48},{48,56},{72,64... | collective-permute-start | bytes 4616 | tf_op jit(solution)/shard_map/ppermute | solution.py:472
  65.9 5.5 %collective-permute-start.16 = (f32[3,128]{1,0:T(4,128)S(1)}, f32[3,128]{1,0:T(4,128)S(1)}, u32[]{:S(2)}, u32[]{:S(2)}) collective-permute-start(f32[3,128]{1,0:T(4,128)S(1)} %get-tuple-element.104), channel_id=1, source_target_pairs={{120,0},{16,8},{8,16},{32,24},{24,32},{48,40},{40,48},{64,56},{56,... | collective-permute-start | bytes 4616 | tf_op jit(solution)/shard_map/ppermute | solution.py:472

commit v4 on v3

--- a/solution.py
+++ b/solution.py
@@ -511,13 +511,28 @@
         out[...] = total.astype(out.dtype)
 
 
+def block_at(k):
+    width = 128
+    return pl.ds(pl.multiple_of(k % 4 * width, width), width)
+
+
+def cut_kernel(part_ref, *outs):
+    height = lax.axis_index("dom") // 4
+    for j in range(3):
+        block = part_ref[:, block_at(height + j)]
+        for out in outs:
+            out[:, j * LANES : (j + 1) * LANES] = block.astype(out.dtype)
+
+
 def ring_kernel(*refs):
     *pieces, out_ref = refs
-    rows = pieces[0].shape[0]
     height = lax.axis_index("dom") // 4
     for k, piece in enumerate(pieces):
-        place = (height + 4 - k) % 4
-        out_ref[pl.ds(pl.multiple_of(place * rows, rows), rows), :] = piece[...]
+        row = height + 4 - k
+        for j in range(3):
+            out_ref[block_at(row), block_at(row + j)] = piece[:, j * LANES : (j + 1) * LANES]
+        turned = piece[:, LANES : 2 * LANES].astype(F32).T.astype(BF16)
+        out_ref[block_at(row + 1), block_at(row)] = turned
 
 
 def shards(
@@ -542,7 +557,7 @@
     projection = projection.transpose(1, 0, 2)
     sends = (shape((4, sent), F32),) * 2
     wide = pltpu.VMEM((LANES, own), F32)
-    slab = (features // 4, features)
+    slab = (features // 4, features // 4 * 3)
     counts = neighbour_count.reshape(1, own)
 
     def count(part):
@@ -607,8 +622,9 @@
     )
 
     to_near, to_far = call(first_kernel, sends, [wide])(position, species, send_lists)
-    part = matrix_part(points, point_weights)
-    sent_part = part.astype(BF16)
+    part, sent_part = call(cut_kernel, (shape(slab, F32), shape(slab, BF16)))(
+        matrix_part(points, point_weights)
+    )
     for step in range(STEPS):
         last = step == STEPS - 1
         if step == 0:
@@ -628,16 +644,16 @@
                 part, after(other, cols, from_far, from_near)
             )
             other = routed(held, "bead", lambda i: i ^ 3)
-            above = passed_along(after(position, held), "bead", -1)
             state = weigh_call(
                 after(position, held), from_near, from_far, cols, projection, *number
             )
             ghost_cols, weight, weight_turned, ghost_waves = state
-            held = call(add_kernel, (shape(slab, BF16),))(part, after(other, above, *state))[0]
+            held = call(add_kernel, (shape(slab, BF16),))(part, after(other, *state))[0]
             pieces = [held] + [routed(held, "dom", lambda i: (i - 4 * k) % 16) for k in (1, 2, 3)]
+            above = passed_along(after(position, held), "bead", -1)
             sines, low = describe_call(after(weight_turned, held), waves, ghost_waves, turned)
             half = call(ring_kernel, shape((features, features), BF16))(
-                pieces[0], *[after(piece, low) for piece in pieces[1:]]
+                pieces[0], *[after(piece, low, above) for piece in pieces[1:]]
             )
             other_half = near_pair(half)
             below = passed_along(after(position, half), "bead", 1)

time: 72.6 us -> 71.8 us (0.989)
  waiting for transfers between devices: 14 us -> 10.1 us
  starting transfers between devices: 23.4 us -> 26.2 us
    ppermute x14, starting transfers between devices: 13.1 us -> 15.6 us  [routed(): lax.ppermute(block, axis, [(source(i), i) for i in range(lax.axis_size(ax...]
    ppermute x14, waiting for transfers between devices: 6.89 us -> 4.83 us  [routed(): lax.ppermute(block, axis, [(source(i), i) for i in range(lax.axis_size(ax...]
    ppermute x4, waiting for transfers between devices: 7.1 us -> 5.28 us  [passed_along(): return lax.ppermute(block, axis, route)]
  transfers between devices with their start and end apart: 19 -> 19, of which waited for: 6 -> 5; matrix products, arithmetic and copies ran while one was open for 0% -> 0% of each run, Pallas kernels for 40% -> 41%
where the time goes in v4:
time: 71.8 us; the launch traced here: 71.6 us
  Pallas kernels  31.7 us (44%)
  starting transfers between devices  26.2 us (36%)
  waiting for transfers between devices  10.1 us (14%)
  local copies, waits for them, and re-layouts  1.6 us (2%)
  between operations  0.98 us (1%)
    ppermute x14, starting transfers between devices, routed(): lax.ppermute(block, axis, [(source(i), i) for i in range(lax.axis_size(ax...  15.6 us
    ppermute x4, starting transfers between devices, passed_along(): return lax.ppermute(block, axis, route)  7.46 us
    pallas_call x2, Pallas kernels, shards(): own_force_call(grad, spread, sines, waves, weight, cols, position, centre...  7.05 us
    pallas_call x2, Pallas kernels, shards(): cols, waves, turned = own_call(start, species, projection, phase_shift)  5.72 us
    pallas_call x2, Pallas kernels, shards(): ghost_force_call(low, half, other_half, cols, turned, weight, ghost_waves...  5.61 us
    ppermute x4, waiting for transfers between devices, passed_along(): return lax.ppermute(block, axis, route)  5.28 us
    ppermute x14, waiting for transfers between devices, routed(): lax.ppermute(block, axis, [(source(i), i) for i in range(lax.axis_size(ax...  4.83 us
    pallas_call x3, Pallas kernels, count(): call(functools.partial(count_kernel, part), shape((ghosts, own), F32), [p...  3.22 us
  transfers between devices with their start and end apart: 19, of which 5 were waited for; matrix products, arithmetic and copies ran while one was open for 0% of the time, Pallas kernels for 41%

profile of v4, /device:TPU:6, one launch (start us, length us, event | category | flops | bytes accessed | tf_op | source)
XLA Modules:
  0.0 71.6 jit_solution(3722497549581991480)
XLA Ops:
  0.7 1.0 %copy-done = bf16[2,250,512]{2,0,1:T(2,128)(2,1)S(1)} copy-done((bf16[2,250,512]{2,0,1:T(2,128)(2,1)S(1)}, bf16[2,250,512]{2,0,1:T(2,128)(2,1)}, u32[]{:S(2)}) %copy-start) | copy-done | bytes 512024
  1.7 0.5 constant_dynamic-slice_fusion
  2.3 0.7 convert_multiply_fusion
  3.4 3.1 %collective-permute-start = (bf16[128,384]{1,0:T(8,128)(2,1)S(1)}, bf16[128,384]{1,0:T(8,128)(2,1)S(1)}, u32[]{:S(2)}, u32[]{:S(2)}) collective-permute-start(bf16[128,384]{1,0:T(8,128)(2,1)S(1)} %get-tuple-element.60), channel_id=1, source_target_pairs={{20,0},{21,1},{22,2},{23,3},{16,4},{17,5},{18,6},{19,7},{28,8},{29... | collective-permute-start | bytes 294920 | tf_op jit(solution)/shard_map/ppermute | solution.py:486
  6.5 1.1 %shard_map.115.rest_0_ = f32[256,512]{1,0:T(8,128)S(1)} custom-call(s32[32,512]{1,0:T(8,128)S(1)} %copy-done.2, s32[1,512]{1,0:T(1,128)S(1)} %bitcast.33), custom_call_target="tpu_custom_call" | custom-call | tf_op jit(solution)/shard_map/pallas_call | solution.py:564
  7.6 1.1 %shard_map.116.rest_1_ = f32[256,512]{1,0:T(8,128)S(1)} custom-call(s32[32,512]{1,0:T(8,128)S(1)} %copy-done.2, s32[1,512]{1,0:T(1,128)S(1)} %bitcast.34), custom_call_target="tpu_custom_call" | custom-call | tf_op jit(solution)/shard_map/pallas_call | solution.py:564
  8.7 1.1 %shard_map.117.rest_2_ = f32[256,512]{1,0:T(8,128)S(1)} custom-call(s32[32,512]{1,0:T(8,128)S(1)} %copy-done.2, s32[1,512]{1,0:T(1,128)S(1)} %bitcast.35), custom_call_target="tpu_custom_call" | custom-call | tf_op jit(solution)/shard_map/pallas_call | solution.py:564
  10.3 0.9 %collective-permute-start.1 = (bf16[128,384]{1,0:T(8,128)(2,1)S(1)}, bf16[128,384]{1,0:T(8,128)(2,1)S(1)}, u32[]{:S(2)}, u32[]{:S(2)}) collective-permute-start(bf16[128,384]{1,0:T(8,128)(2,1)S(1)} %get-tuple-element.65), channel_id=1, source_target_pairs={{1,0},{0,1},{3,2},{2,3},{5,4},{4,5},{7,6},{6,7},{9,8},{8,9},{11,10... | collective-permute-start | bytes 294920 | tf_op jit(solution)/shard_map/ppermute | solution.py:472
  11.2 2.5 %collective-permute-start.2 = (f32[4,128]{1,0:T(4,128)S(1)}, f32[4,128]{1,0:T(4,128)S(1)}, u32[]{:S(2)}, u32[]{:S(2)}) collective-permute-start(f32[4,128]{1,0:T(4,128)S(1)} %get-tuple-element.68), channel_id=1, source_target_pairs={{120,0},{16,8},{8,16},{32,24},{24,32},{48,40},{40,48},{64,56},{56,... | collective-permute-start | bytes 6152 | tf_op jit(solution)/shard_map/ppermute | solution.py:472
  13.7 2.9 %shard_map.119 = (f32[512,128]{1,0:T(8,128)S(1)}, bf16[512,2048]{1,0:T(8,128)(2,1)S(1)}, f32[512,2048]{1,0:T(8,128)S(1)}) custom-call(f32[3,1,512]{2,1,0:T(1,128)S(1)} %bitcast.21, s32[1,512]{1,0:T(1,128)S(1)} %bitcast.29, f32[3,2,512]{2,1,0:T(2,128)S(1)} %bitcast.12, f32[2,512]{1,0:T(2,128)S(1)} %copy-done.6), custom_call_target="tpu_custom_call" | custom-call | tf_op jit(solution)/shard_map/pallas_call | solution.py:641
  16.7 1.2 %collective-permute-start.4 = (bf16[128,384]{1,0:T(8,128)(2,1)S(1)}, bf16[128,384]{1,0:T(8,128)(2,1)S(1)}, u32[]{:S(2)}, u32[]{:S(2)}) collective-permute-start(bf16[128,384]{1,0:T(8,128)(2,1)S(1)} %get-tuple-element.71), channel_id=1, source_target_pairs={{3,0},{2,1},{1,2},{0,3},{7,4},{6,5},{5,6},{4,7},{11,8},{10,9},{9,1... | collective-permute-start | bytes 294920 | tf_op jit(solution)/shard_map/ppermute | solution.py:472
  17.9 1.7 %shard_map.121 = (f32[256,128]{1,0:T(8,128)S(1)}, f32[768,512]{1,0:T(8,128)S(1)}, bf16[512,768]{1,0:T(8,128)(2,1)S(1)}, bf16[256,2048]{1,0:T(8,128)(2,1)S(1)}) custom-call(f32[3,1,512]{2,1,0:T(1,128)S(1)} %bitcast.22, f32[4,128]{1,0:T(4,128)S(1)} %collective-permute-done.3.near_ref, f32[4,128]{1,0:T(4,128)S(1)} %collective-permute-done.2.far_ref, ...), custom_call_target="tpu_custom_call" | custom-call | tf_op jit(solution)/shard_map/pallas_call | solution.py:647
  19.6 3.5 %collective-permute-done.4.other_ref = bf16[128,384]{1,0:T(8,128)(2,1)S(1)} collective-permute-done((bf16[128,384]{1,0:T(8,128)(2,1)S(1)}, bf16[128,384]{1,0:T(8,128)(2,1)S(1)}, u32[]{:S(2)}, u32[]{:S(2)}) %collective-permute-start.4) | collective-permute-done | bytes 98336 | tf_op jit(solution)/shard_map/ppermute | solution.py:472
  23.2 2.0 %collective-permute-start.8 = (bf16[128,384]{1,0:T(8,128)(2,1)S(1)}, bf16[128,384]{1,0:T(8,128)(2,1)S(1)}, u32[]{:S(2)}, u32[]{:S(2)}) collective-permute-start(bf16[128,384]{1,0:T(8,128)(2,1)S(1)} %shard_map.122.refs_0_), channel_id=1, source_target_pairs={{32,0},{40,8},{48,16},{56,24},{64,32},{72,40},{80,48},{88,56},{96,... | collective-permute-start | bytes 294920 | tf_op jit(solution)/shard_map/ppermute | solution.py:472
  25.2 1.3 %collective-permute-start.5 = (bf16[128,384]{1,0:T(8,128)(2,1)S(1)}, bf16[128,384]{1,0:T(8,128)(2,1)S(1)}, u32[]{:S(2)}, u32[]{:S(2)}) collective-permute-start(bf16[128,384]{1,0:T(8,128)(2,1)S(1)} %shard_map.122.refs_0_), channel_id=1, source_target_pairs={{96,0},{104,8},{112,16},{120,24},{0,32},{8,40},{16,48},{24,56},{32... | collective-permute-start | bytes 294920 | tf_op jit(solution)/shard_map/ppermute | solution.py:472
  26.5 2.0 %shard_map.123 = (f32[512,1024]{1,0:T(8,128)S(1)}, bf16[512,512]{1,0:T(8,128)(2,1)S(1)}) custom-call(bf16[512,768]{1,0:T(8,128)(2,1)S(1)} %get-tuple-element.79.weight_turned, bf16[512,2048]{1,0:T(8,128)(2,1)S(1)} %get-tuple-element.80.own_waves.waves, bf16[256,2048]{1,0:T(8,128)(2,1)S(1)} %get-tuple-element.77.ghost_waves.waves, ...), custom_call_target="tpu_custom_call" | custom-call | tf_op jit(solution)/shard_map/pallas_call | solution.py:654
  28.5 5.3 %collective-permute-done.6.above_ref = f32[3,1,512]{2,1,0:T(1,128)S(1)} collective-permute-done((f32[3,1,512]{2,1,0:T(1,128)S(1)}, f32[3,1,512]{2,1,0:T(1,128)S(1)}, u32[]{:S(2)}, u32[]{:S(2)}) %collective-permute-start.6) | collective-permute-done | bytes 6176 | tf_op jit(solution)/shard_map/ppermute | solution.py:468
  34.0 1.8 %collective-permute-start.12 = (f32[3,1,512]{2,1,0:T(1,128)S(1)}, f32[3,1,512]{2,1,0:T(1,128)S(1)}, u32[]{:S(2)}, u32[]{:S(2)}) collective-permute-start(f32[3,1,512]{2,1,0:T(1,128)S(1)} %bitcast.24), channel_id=1, source_target_pairs={{7,0},{0,1},{1,2},{2,3},{3,4},{4,5},{5,6},{6,7},{15,8},{8,9},{9,10... | collective-permute-start | bytes 18440 | tf_op jit(solution)/shard_map/ppermute | solution.py:468
  35.9 2.8 %shard_map.125 = (f32[512,512]{1,0:T(8,128)S(1)}, bf16[512,2048]{1,0:T(8,128)(2,1)S(1)}, f32[3,512]{1,0:T(4,128)S(1)}, f32[3,128]{1,0:T(4,128)S(1)}, f32[3,128]{1,0:T(4,128)S(1)}) custom-call(bf16[512,512]{1,0:T(8,128)(2,1)S(1)} %get-tuple-element.82.low, bf16[512,512]{1,0:T(8,128)(2,1)S(1)} %shard_map.124.half_ref, ...), custom_call_target="tpu_custom_call" | custom-call | tf_op jit(solution)/shard_map/pallas_call | solution.py:667
  38.9 3.9 %collective-permute-start.11 = (f32[3,128]{1,0:T(4,128)S(1)}, f32[3,128]{1,0:T(4,128)S(1)}, u32[]{:S(2)}, u32[]{:S(2)}) collective-permute-start(f32[3,128]{1,0:T(4,128)S(1)} %get-tuple-element.92), channel_id=1, source_target_pairs={{120,0},{16,8},{8,16},{32,24},{24,32},{48,40},{40,48},{64,56},{56,... | collective-permute-start | bytes 4616 | tf_op jit(solution)/shard_map/ppermute | solution.py:472
  42.8 3.5 %shard_map.126.force_ref = f32[3,512]{1,0:T(4,128)S(1)} custom-call(f32[512,512]{1,0:T(8,128)S(1)} %get-tuple-element.87.grad, bf16[512,2048]{1,0:T(8,128)(2,1)S(1)} %get-tuple-element.88.spread, f32[512,1024]{1,0:T(8,128)S(1)} %get-tuple-element.89.sines, bf16[512,2048]{1,0:T(8,128)(2,1)S(1)} %get-tuple-element.80.own_waves.waves, ...), custom_call_target="tpu_custom_call" | custom-call | tf_op jit(solution)/shard_map/pallas_call | solution.py:681
  46.4 0.9 %shard_map.127 = (f32[3,1,512]{2,1,0:T(1,128)S(1)}, f32[3,1,512]{2,1,0:T(1,128)S(1)}, f32[4,128]{1,0:T(4,128)S(1)}, f32[4,128]{1,0:T(4,128)S(1)}) custom-call(f32[3,512]{1,0:T(4,128)S(1)} %shard_map.126.force_ref, f32[3,128]{1,0:T(4,128)S(1)} %collective-permute-done.10.near_back_ref, f32[3,128]{1,0:T(4,128)S(1)} %collective-permute-done.11.far_back_ref, ...), custom_call_target="tpu_custom_call" | custom-call | tf_op jit(solution)/shard_map/pallas_call | solution.py:685
  47.4 1.9 %collective-permute-start.14 = (f32[4,128]{1,0:T(4,128)S(1)}, f32[4,128]{1,0:T(4,128)S(1)}, u32[]{:S(2)}, u32[]{:S(2)}) collective-permute-start(f32[4,128]{1,0:T(4,128)S(1)} %get-tuple-element.96), channel_id=1, source_target_pairs={{120,0},{16,8},{8,16},{32,24},{24,32},{48,40},{40,48},{64,56},{56,... | collective-permute-start | bytes 6152 | tf_op jit(solution)/shard_map/ppermute | solution.py:472
  49.2 2.9 %shard_map.128 = (f32[512,128]{1,0:T(8,128)S(1)}, bf16[512,2048]{1,0:T(8,128)(2,1)S(1)}, f32[512,2048]{1,0:T(8,128)S(1)}) custom-call(f32[3,1,512]{2,1,0:T(1,128)S(1)} %get-tuple-element.113.position_ref, s32[1,512]{1,0:T(1,128)S(1)} %bitcast.31, f32[3,2,512]{2,1,0:T(2,128)S(1)} %bitcast.16, f32[2,512]{1,0:T(2,128)S(1)} %copy-done.6), custom_call_target="tpu_custom_call" | custom-call | tf_op jit(solution)/shard_map/pallas_call | solution.py:641
  52.1 0.7 collective-permute-done.14.far_ref
  53.0 1.7 %shard_map.129 = (f32[256,128]{1,0:T(8,128)S(1)}, f32[768,512]{1,0:T(8,128)S(1)}, bf16[512,768]{1,0:T(8,128)(2,1)S(1)}, bf16[256,2048]{1,0:T(8,128)(2,1)S(1)}) custom-call(f32[3,1,512]{2,1,0:T(1,128)S(1)} %get-tuple-element.113.position_ref, f32[4,128]{1,0:T(4,128)S(1)} %collective-permute-done.13.near_ref, f32[4,128]{1,0:T(4,128)S(1)} %collective-permute-done.14.far_ref, ...), custom_call_target="tpu_custom_call" | custom-call | tf_op jit(solution)/shard_map/pallas_call | solution.py:662
  54.7 2.0 %shard_map.130 = (f32[512,1024]{1,0:T(8,128)S(1)}, bf16[512,512]{1,0:T(8,128)(2,1)S(1)}) custom-call(bf16[512,768]{1,0:T(8,128)(2,1)S(1)} %get-tuple-element.98.weight_turned, bf16[512,2048]{1,0:T(8,128)(2,1)S(1)} %get-tuple-element.99.own_waves.waves, bf16[256,2048]{1,0:T(8,128)(2,1)S(1)} %get-tuple-element.100.ghost_waves.waves, ...), custom_call_target="tpu_custom_call" | custom-call | tf_op jit(solution)/shard_map/pallas_call | solution.py:665
  56.7 5.5 %collective-permute-start.17 = (f32[3,1,512]{2,1,0:T(1,128)S(1)}, f32[3,1,512]{2,1,0:T(1,128)S(1)}, u32[]{:S(2)}, u32[]{:S(2)}) collective-permute-start(f32[3,1,512]{2,1,0:T(1,128)S(1)} %get-tuple-element.113.position_ref), channel_id=1, source_target_pairs={{7,0},{0,1},{1,2},{2,3},{3,4},{4,5},{5,6},{6,7},{15,8},{8,9},{9,10... | collective-permute-start | bytes 18440 | tf_op jit(solution)/shard_map/ppermute | solution.py:468
  62.2 2.8 %shard_map.131 = (f32[512,512]{1,0:T(8,128)S(1)}, bf16[512,2048]{1,0:T(8,128)(2,1)S(1)}, f32[3,512]{1,0:T(4,128)S(1)}, f32[3,128]{1,0:T(4,128)S(1)}, f32[3,128]{1,0:T(4,128)S(1)}) custom-call(bf16[512,512]{1,0:T(8,128)(2,1)S(1)} %get-tuple-element.102.low, bf16[512,512]{1,0:T(8,128)(2,1)S(1)} %shard_map.124.half_ref, ...), custom_call_target="tpu_custom_call" | custom-call | tf_op jit(solution)/shard_map/pallas_call | solution.py:667
  65.1 1.5 %collective-permute-start.16 = (f32[3,128]{1,0:T(4,128)S(1)}, f32[3,128]{1,0:T(4,128)S(1)}, u32[]{:S(2)}, u32[]{:S(2)}) collective-permute-start(f32[3,128]{1,0:T(4,128)S(1)} %get-tuple-element.110), channel_id=1, source_target_pairs={{120,0},{16,8},{8,16},{32,24},{24,32},{48,40},{40,48},{64,56},{56,... | collective-permute-start | bytes 4616 | tf_op jit(solution)/shard_map/ppermute | solution.py:472
  66.6 3.5 %shard_map.132.force_ref = f32[3,512]{1,0:T(4,128)S(1)} custom-call(f32[512,512]{1,0:T(8,128)S(1)} %get-tuple-element.105.grad, bf16[512,2048]{1,0:T(8,128)(2,1)S(1)} %get-tuple-element.106.spread, f32[512,1024]{1,0:T(8,128)S(1)} %get-tuple-element.107.sines, bf16[512,2048]{1,0:T(8,128)(2,1)S(1)} %get-tuple-element.99.own_waves.waves, ...), custom_call_target="tpu_custom_call" | custom-call | tf_op jit(solution)/shard_map/pallas_call | solution.py:681
  70.6 1.0 %shard_map.133 = (f32[3,1,512]{2,1,0:T(1,128)}, f32[3,1,512]{2,1,0:T(1,128)}) custom-call(f32[3,512]{1,0:T(4,128)S(1)} %shard_map.132.force_ref, f32[3,128]{1,0:T(4,128)S(1)} %collective-permute-done.15.near_back_ref, f32[3,128]{1,0:T(4,128)S(1)} %collective-permute-done.16.far_back_ref, s32[2,128]{1,0:T(2,128)S(1)} %copy-done.7, ...), custom_call_target="tpu_custom_call" | custom-call | tf_op jit(solution)/shard_map/pallas_call | solution.py:685
  (49 shorter events, 2.5 us)
Async XLA Ops:
  0.6 1.0 %copy-start = (bf16[2,250,512]{2,0,1:T(2,128)(2,1)S(1)}, bf16[2,250,512]{2,0,1:T(2,128)(2,1)}, u32[]{:S(2)}) copy-start(bf16[2,250,512]{2,0,1:T(2,128)(2,1)} %param.18) | copy-start | bytes 1536004
  0.6 5.9 %copy-start.5 = (s32[512]{0:T(512)S(1)}, s32[512]{0:T(512)}, u32[]{:S(2)}) copy-start(s32[512]{0:T(512)} %param.14) | copy-start | bytes 6148
  0.7 5.9 %copy-start.2 = (s32[32,512]{1,0:T(8,128)S(1)}, s32[32,512]{1,0:T(8,128)}, u32[]{:S(2)}) copy-start(s32[32,512]{1,0:T(8,128)} %neighbours_ref.5) | copy-start | bytes 196612
  1.7 8.1 %copy-start.3 = (f32[1,3,512]{2,0,1:T(1,128)S(1)}, f32[1,3,512]{2,0,1:T(1,128)}, u32[]{:S(2)}) copy-start(f32[1,3,512]{2,0,1:T(1,128)} %param.10) | copy-start | bytes 18436
  1.7 8.1 %copy-start.4 = (s32[512]{0:T(512)S(1)}, s32[512]{0:T(512)}, u32[]{:S(2)}) copy-start(s32[512]{0:T(512)} %param.12) | copy-start | bytes 6148
  1.7 8.1 %copy-start.7 = (s32[2,128]{1,0:T(2,128)S(1)}, s32[2,128]{1,0:T(2,128)}, u32[]{:S(2)}) copy-start(s32[2,128]{1,0:T(2,128)} %lists_ref.5) | copy-start | bytes 3076
  2.2 11.5 %copy-start.1 = (f32[2,3,512]{2,0,1:T(2,128)S(1)}, f32[2,3,512]{2,0,1:T(2,128)}, u32[]{:S(2)}) copy-start(f32[2,3,512]{2,0,1:T(2,128)} %param.16) | copy-start | bytes 36868
  2.2 11.5 %copy-start.6 = (f32[2,512]{1,0:T(2,128)S(1)}, f32[2,512]{1,0:T(2,128)}, u32[]{:S(2)}) copy-start(f32[2,512]{1,0:T(2,128)} %shift_ref.3) | copy-start | bytes 12292
  3.4 6.8 %collective-permute-start = (bf16[128,384]{1,0:T(8,128)(2,1)S(1)}, bf16[128,384]{1,0:T(8,128)(2,1)S(1)}, u32[]{:S(2)}, u32[]{:S(2)}) collective-permute-start(bf16[128,384]{1,0:T(8,128)(2,1)S(1)} %get-tuple-element.60), channel_id=1, source_target_pairs={{20,0},{21,1},{22,2},{23,3},{16,4},{17,5},{18,6},{19,7},{28,8},{29... | collective-permute-start | bytes 294920 | tf_op jit(solution)/shard_map/ppermute | solution.py:486
  10.3 6.3 %collective-permute-start.1 = (bf16[128,384]{1,0:T(8,128)(2,1)S(1)}, bf16[128,384]{1,0:T(8,128)(2,1)S(1)}, u32[]{:S(2)}, u32[]{:S(2)}) collective-permute-start(bf16[128,384]{1,0:T(8,128)(2,1)S(1)} %get-tuple-element.65), channel_id=1, source_target_pairs={{1,0},{0,1},{3,2},{2,3},{5,4},{4,5},{7,6},{6,7},{9,8},{8,9},{11,10... | collective-permute-start | bytes 294920 | tf_op jit(solution)/shard_map/ppermute | solution.py:472
  11.2 5.4 %collective-permute-start.2 = (f32[4,128]{1,0:T(4,128)S(1)}, f32[4,128]{1,0:T(4,128)S(1)}, u32[]{:S(2)}, u32[]{:S(2)}) collective-permute-start(f32[4,128]{1,0:T(4,128)S(1)} %get-tuple-element.68), channel_id=1, source_target_pairs={{120,0},{16,8},{8,16},{32,24},{24,32},{48,40},{40,48},{64,56},{56,... | collective-permute-start | bytes 6152 | tf_op jit(solution)/shard_map/ppermute | solution.py:472
  13.7 2.9 %collective-permute-start.3 = (f32[4,128]{1,0:T(4,128)S(1)}, f32[4,128]{1,0:T(4,128)S(1)}, u32[]{:S(2)}, u32[]{:S(2)}) collective-permute-start(f32[4,128]{1,0:T(4,128)S(1)} %get-tuple-element.69), channel_id=1, source_target_pairs={{8,0},{0,8},{24,16},{16,24},{40,32},{32,40},{56,48},{48,56},{72,64... | collective-permute-start | bytes 6152 | tf_op jit(solution)/shard_map/ppermute | solution.py:472
  16.7 6.5 %collective-permute-start.4 = (bf16[128,384]{1,0:T(8,128)(2,1)S(1)}, bf16[128,384]{1,0:T(8,128)(2,1)S(1)}, u32[]{:S(2)}, u32[]{:S(2)}) collective-permute-start(bf16[128,384]{1,0:T(8,128)(2,1)S(1)} %get-tuple-element.71), channel_id=1, source_target_pairs={{3,0},{2,1},{1,2},{0,3},{7,4},{6,5},{5,6},{4,7},{11,8},{10,9},{9,1... | collective-permute-start | bytes 294920 | tf_op jit(solution)/shard_map/ppermute | solution.py:472
  23.2 10.5 %collective-permute-start.8 = (bf16[128,384]{1,0:T(8,128)(2,1)S(1)}, bf16[128,384]{1,0:T(8,128)(2,1)S(1)}, u32[]{:S(2)}, u32[]{:S(2)}) collective-permute-start(bf16[128,384]{1,0:T(8,128)(2,1)S(1)} %shard_map.122.refs_0_), channel_id=1, source_target_pairs={{32,0},{40,8},{48,16},{56,24},{64,32},{72,40},{80,48},{88,56},{96,... | collective-permute-start | bytes 294920 | tf_op jit(solution)/shard_map/ppermute | solution.py:472
  25.2 8.5 %collective-permute-start.7 = (bf16[128,384]{1,0:T(8,128)(2,1)S(1)}, bf16[128,384]{1,0:T(8,128)(2,1)S(1)}, u32[]{:S(2)}, u32[]{:S(2)}) collective-permute-start(bf16[128,384]{1,0:T(8,128)(2,1)S(1)} %shard_map.122.refs_0_), channel_id=1, source_target_pairs={{64,0},{72,8},{80,16},{88,24},{96,32},{104,40},{112,48},{120,56},{... | collective-permute-start | bytes 294920 | tf_op jit(solution)/shard_map/ppermute | solution.py:472
  25.2 8.5 %collective-permute-start.5 = (bf16[128,384]{1,0:T(8,128)(2,1)S(1)}, bf16[128,384]{1,0:T(8,128)(2,1)S(1)}, u32[]{:S(2)}, u32[]{:S(2)}) collective-permute-start(bf16[128,384]{1,0:T(8,128)(2,1)S(1)} %shard_map.122.refs_0_), channel_id=1, source_target_pairs={{96,0},{104,8},{112,16},{120,24},{0,32},{8,40},{16,48},{24,56},{32... | collective-permute-start | bytes 294920 | tf_op jit(solution)/shard_map/ppermute | solution.py:472
  26.5 7.2 %collective-permute-start.6 = (f32[3,1,512]{2,1,0:T(1,128)S(1)}, f32[3,1,512]{2,1,0:T(1,128)S(1)}, u32[]{:S(2)}, u32[]{:S(2)}) collective-permute-start(f32[3,1,512]{2,1,0:T(1,128)S(1)} %bitcast.23), channel_id=1, source_target_pairs={{1,0},{2,1},{3,2},{4,3},{5,4},{6,5},{7,6},{0,7},{9,8},{10,9},{11,1... | collective-permute-start | bytes 18440 | tf_op jit(solution)/shard_map/ppermute | solution.py:468
  33.9 2.0 %collective-permute-start.9 = (bf16[512,512]{1,0:T(8,128)(2,1)S(1)}, bf16[512,512]{1,0:T(8,128)(2,1)S(1)}, u32[]{:S(2)}, u32[]{:S(2)}) collective-permute-start(bf16[512,512]{1,0:T(8,128)(2,1)S(1)} %shard_map.124.half_ref), channel_id=1, source_target_pairs={{8,0},{0,8},{24,16},{16,24},{40,32},{32,40},{56,48},{48,56},{72,64... | collective-permute-start | bytes 1572872 | tf_op jit(solution)/shard_map/ppermute | solution.py:472
  34.0 12.3 %collective-permute-start.12 = (f32[3,1,512]{2,1,0:T(1,128)S(1)}, f32[3,1,512]{2,1,0:T(1,128)S(1)}, u32[]{:S(2)}, u32[]{:S(2)}) collective-permute-start(f32[3,1,512]{2,1,0:T(1,128)S(1)} %bitcast.24), channel_id=1, source_target_pairs={{7,0},{0,1},{1,2},{2,3},{3,4},{4,5},{5,6},{6,7},{15,8},{8,9},{9,10... | collective-permute-start | bytes 18440 | tf_op jit(solution)/shard_map/ppermute | solution.py:468
  38.7 7.7 %collective-permute-start.10 = (f32[3,128]{1,0:T(4,128)S(1)}, f32[3,128]{1,0:T(4,128)S(1)}, u32[]{:S(2)}, u32[]{:S(2)}) collective-permute-start(f32[3,128]{1,0:T(4,128)S(1)} %get-tuple-element.91), channel_id=1, source_target_pairs={{8,0},{0,8},{24,16},{16,24},{40,32},{32,40},{56,48},{48,56},{72,64... | collective-permute-start | bytes 4616 | tf_op jit(solution)/shard_map/ppermute | solution.py:472
  38.9 7.5 %collective-permute-start.11 = (f32[3,128]{1,0:T(4,128)S(1)}, f32[3,128]{1,0:T(4,128)S(1)}, u32[]{:S(2)}, u32[]{:S(2)}) collective-permute-start(f32[3,128]{1,0:T(4,128)S(1)} %get-tuple-element.92), channel_id=1, source_target_pairs={{120,0},{16,8},{8,16},{32,24},{24,32},{48,40},{40,48},{64,56},{56,... | collective-permute-start | bytes 4616 | tf_op jit(solution)/shard_map/ppermute | solution.py:472
  42.8 3.5 %copy-start.8 = (f32[1,3,512]{2,0,1:T(1,128)S(1)}, f32[1,3,512]{2,0,1:T(1,128)}, u32[]{:S(2)}) copy-start(f32[1,3,512]{2,0,1:T(1,128)} %param.11) | copy-start | bytes 18436
  47.3 4.8 %collective-permute-start.13 = (f32[4,128]{1,0:T(4,128)S(1)}, f32[4,128]{1,0:T(4,128)S(1)}, u32[]{:S(2)}, u32[]{:S(2)}) collective-permute-start(f32[4,128]{1,0:T(4,128)S(1)} %get-tuple-element.95), channel_id=1, source_target_pairs={{8,0},{0,8},{24,16},{16,24},{40,32},{32,40},{56,48},{48,56},{72,64... | collective-permute-start | bytes 6152 | tf_op jit(solution)/shard_map/ppermute | solution.py:472
  47.4 5.4 %collective-permute-start.14 = (f32[4,128]{1,0:T(4,128)S(1)}, f32[4,128]{1,0:T(4,128)S(1)}, u32[]{:S(2)}, u32[]{:S(2)}) collective-permute-start(f32[4,128]{1,0:T(4,128)S(1)} %get-tuple-element.96), channel_id=1, source_target_pairs={{120,0},{16,8},{8,16},{32,24},{24,32},{48,40},{40,48},{64,56},{56,... | collective-permute-start | bytes 6152 | tf_op jit(solution)/shard_map/ppermute | solution.py:472
  52.8 17.8 %collective-permute-start.18 = (f32[3,1,512]{2,1,0:T(1,128)S(1)}, f32[3,1,512]{2,1,0:T(1,128)S(1)}, u32[]{:S(2)}, u32[]{:S(2)}) collective-permute-start(f32[3,1,512]{2,1,0:T(1,128)S(1)} %get-tuple-element.113.position_ref), channel_id=1, source_target_pairs={{1,0},{2,1},{3,2},{4,3},{5,4},{6,5},{7,6},{0,7},{9,8},{10,9},{11,1... | collective-permute-start | bytes 18440 | tf_op jit(solution)/shard_map/ppermute | solution.py:468
  56.7 13.9 %collective-permute-start.17 = (f32[3,1,512]{2,1,0:T(1,128)S(1)}, f32[3,1,512]{2,1,0:T(1,128)S(1)}, u32[]{:S(2)}, u32[]{:S(2)}) collective-permute-start(f32[3,1,512]{2,1,0:T(1,128)S(1)} %get-tuple-element.113.position_ref), channel_id=1, source_target_pairs={{7,0},{0,1},{1,2},{2,3},{3,4},{4,5},{5,6},{6,7},{15,8},{8,9},{9,10... | collective-permute-start | bytes 18440 | tf_op jit(solution)/shard_map/ppermute | solution.py:468
  65.0 5.1 %collective-permute-start.15 = (f32[3,128]{1,0:T(4,128)S(1)}, f32[3,128]{1,0:T(4,128)S(1)}, u32[]{:S(2)}, u32[]{:S(2)}) collective-permute-start(f32[3,128]{1,0:T(4,128)S(1)} %get-tuple-element.109), channel_id=1, source_target_pairs={{8,0},{0,8},{24,16},{16,24},{40,32},{32,40},{56,48},{48,56},{72,64... | collective-permute-start | bytes 4616 | tf_op jit(solution)/shard_map/ppermute | solution.py:472
  65.1 5.5 %collective-permute-start.16 = (f32[3,128]{1,0:T(4,128)S(1)}, f32[3,128]{1,0:T(4,128)S(1)}, u32[]{:S(2)}, u32[]{:S(2)}) collective-permute-start(f32[3,128]{1,0:T(4,128)S(1)} %get-tuple-element.110), channel_id=1, source_target_pairs={{120,0},{16,8},{8,16},{32,24},{24,32},{48,40},{40,48},{64,56},{56,... | collective-permute-start | bytes 4616 | tf_op jit(solution)/shard_map/ppermute | solution.py:472

commit v5 on v4

--- a/solution.py
+++ b/solution.py
@@ -16,6 +16,7 @@
 
 F32, BF16 = jnp.float32, jnp.bfloat16
 LANES = 128
+PACKED = 16
 ROWS = 32
 FB = 256
 TURN = 0.15915494309189535
@@ -110,8 +111,8 @@
     lists_ref,
     position_ref,
     velocity_ref,
-    below_ref,
-    above_ref,
+    one_bead_ref,
+    other_bead_ref,
     species_ref,
     new_position_ref,
     new_velocity_ref,
@@ -138,7 +139,7 @@
     rows = []
     for a in range(3):
         here = position_ref[a]
-        chain = 2.0 * here - below_ref[a] - above_ref[a]
+        chain = 2.0 * here - one_bead_ref[a] - other_bead_ref[a]
         total = force_ref[a : a + 1, :] + extra[a] - KAPPA * mass * chain
         velocity = velocity_ref[a] + DT * (total / mass)
         place = here + DT * velocity
@@ -284,13 +285,14 @@
     own = weight_turned.shape[0]
     features = low.shape[1]
     for block in range(features // FB):
+        these = slice(block * 4 * FB, (block + 1) * 4 * FB)
+        sums[:, these] = jnp.dot(
+            weight_turned[:, 0:own], own_waves[:, these], preferred_element_type=F32
+        ) + jnp.dot(weight_turned[:, own:], ghost_waves[:, these], preferred_element_type=F32)
+
+    for block in range(features // FB):
         mine = slice(block * FB, (block + 1) * FB)
         base = block * 4 * FB
-        sums[...] = jnp.dot(
-            weight_turned[:, 0:own], own_waves[:, base : base + 4 * FB], preferred_element_type=F32
-        ) + jnp.dot(
-            weight_turned[:, own:], ghost_waves[:, base : base + 4 * FB], preferred_element_type=F32
-        )
 
         def describe(c, carry):
             rows = chunk_rows(c)
@@ -298,8 +300,7 @@
             for s in range(2):
                 at = base + s * 2 * FB
                 tr, ti = turned[rows, at : at + FB], turned[rows, at + FB : at + 2 * FB]
-                ur = sums[rows, s * 2 * FB : s * 2 * FB + FB]
-                ui = sums[rows, s * 2 * FB + FB : s * 2 * FB + 2 * FB]
+                ur, ui = sums[rows, at : at + FB], sums[rows, at + FB : at + 2 * FB]
                 total = total + (tr * ur - ti * ui)
                 first = s * features + block * FB
                 sines[rows, first : first + FB] = tr * ui + ti * ur
@@ -316,15 +317,21 @@
     return total
 
 
-def pull_rows(first, cols, waves, weight, spread, projection_ref, here, parts, back, product):
+def pull_rows(
+    along_first, first, cols, waves, weight, spread, projection_ref, here, parts, back, product
+):
     count = cols.shape[0]
     features = projection_ref.shape[2]
     held = weight[first : first + count, :].astype(BF16)
-    for block in range(features // FB):
+
+    def back_of(block):
+        these = slice(block * 4 * FB, (block + 1) * 4 * FB)
+        back[:, these] = jnp.dot(held, spread[:, these], preferred_element_type=F32)
+
+    def pull_block(block):
         mine = slice(block * FB, (block + 1) * FB)
         base = block * 4 * FB
         raw = [[projection_ref[a, s : s + 1, mine] for a in range(3)] for s in range(2)]
-        back[...] = jnp.dot(held, spread[:, base : base + 4 * FB], preferred_element_type=F32)
 
         def pull(c, carry):
             rows = chunk_rows(c)
@@ -334,8 +341,8 @@
                 at = base + s * 2 * FB
                 er = waves[rows, at : at + FB].astype(F32)
                 ei = waves[rows, at + FB : at + 2 * FB].astype(F32)
-                vr = back[rows, s * 2 * FB : s * 2 * FB + FB]
-                vi = back[rows, s * 2 * FB + FB : s * 2 * FB + 2 * FB]
+                vr = back[rows, at : at + FB]
+                vi = back[rows, at + FB : at + 2 * FB]
                 total = total + (ei * vr - er * vi)
             for a in range(3):
                 coeff = jnp.where(second, raw[1][a], raw[0][a])
@@ -343,10 +350,6 @@
             return carry
 
         each(count, pull)
-
-    product[...] = lax.dot_general(
-        waves[...], spread[...], (((1,), (1,)), ((), ())), preferred_element_type=F32
-    )
 
     def along(c, carry):
         rows = chunk_rows(c)
@@ -362,8 +365,27 @@
             out.append(carry[a] + total)
         return tuple(out)
 
+    def product_of():
+        product[...] = lax.dot_general(
+            waves[...], spread[...], (((1,), (1,)), ((), ())), preferred_element_type=F32
+        )
+
     start = tuple(jnp.zeros((8, here[0].shape[1]), F32) for _ in range(3))
-    return each(count, along, carry=start)
+    blocks = range(features // FB)
+    if along_first:
+        product_of()
+        for block in blocks:
+            back_of(block)
+        centre = each(count, along, carry=start)
+        for block in blocks:
+            pull_block(block)
+    else:
+        for block in blocks:
+            back_of(block)
+            pull_block(block)
+        product_of()
+        centre = each(count, along, carry=start)
+    return centre
 
 
 def ghost_force_kernel(
@@ -414,7 +436,7 @@
 
     parts[...] = jnp.zeros_like(parts)
     centre = pull_rows(
-        own, cols, waves, weight, spread, projection_ref, here, parts, back, product
+        True, own, cols, waves, weight, spread, projection_ref, here, parts, back, product
     )
     for a in range(3):
         row = jnp.sum(parts[a].T, axis=0, keepdims=True)
@@ -453,7 +475,7 @@
 
     each(own, turn)
     centre = pull_rows(
-        0, cols, waves, weight, spread, projection_ref, here, parts, back, product
+        False, 0, cols, waves, weight, spread, projection_ref, here, parts, back, product
     )
     for a in range(3):
         row = jnp.sum(parts[a].T, axis=0, keepdims=True)
@@ -462,12 +484,6 @@
         )
 
 
-def passed_along(block, axis, distance):
-    devices = range(lax.axis_size(axis))
-    route = [((i - distance) % len(devices), i) for i in devices]
-    return lax.ppermute(block, axis, route)
-
-
 def routed(block, axis, source):
     return lax.ppermute(block, axis, [(source(i), i) for i in range(lax.axis_size(axis))])
 
@@ -484,6 +500,14 @@
     beads = lax.axis_size("bead")
     route = [(i ^ (2 * beads + 4), i) for i in range(beads * lax.axis_size("dom"))]
     return lax.ppermute(block, ("dom", "bead"), route)
+
+
+def even_bead(block):
+    return routed(block, "bead", lambda i: i ^ 1)
+
+
+def odd_bead(block):
+    return routed(block, "bead", lambda i: (i - 1 + i % 2 * 2) % lax.axis_size("bead"))
 
 
 def after(value, *others):
@@ -505,10 +529,53 @@
     )
 
 
-def add_kernel(part_ref, other_ref, *outs):
-    total = part_ref[...] + other_ref[...].astype(F32)
-    for out in outs:
-        out[...] = total.astype(out.dtype)
+def packed_places(atoms):
+    pieces = atoms // LANES
+    for axis_id in range(3):
+        for part in range(3):
+            for piece in range(pieces):
+                k = (axis_id * 3 + part) * pieces + piece
+                yield axis_id, part, piece, k // 3, k % 3
+
+
+def add_pack_kernel(part_ref, other_ref, position_ref, total_ref, sent_ref, *rest):
+    rows = part_ref.shape[0]
+    total = part_ref[...] + other_ref[0:rows, :].astype(F32)
+    total_ref[...] = total
+    sent_ref[0:rows, :] = total.astype(BF16)
+    if len(rest) > 1:
+        unpack(other_ref, rows, rest[0])
+    packed = rest[-1]
+    packed[...] = jnp.zeros_like(packed)
+    split = []
+    for a in range(3):
+        left = position_ref[a]
+        split.append([])
+        for _ in range(3):
+            part = left.astype(BF16).astype(F32)
+            split[a].append(part)
+            left = left - part
+    for a, part, piece, row, column in packed_places(position_ref.shape[2]):
+        packed[row : row + 1, column * LANES : (column + 1) * LANES] = split[a][part][
+            :, piece * LANES : (piece + 1) * LANES
+        ]
+    sent_ref[rows : rows + PACKED, :] = packed[...].astype(BF16)
+
+
+def unpack(sent_ref, rows, position_ref):
+    packed = sent_ref[rows : rows + PACKED, :].astype(F32)
+    sums = {}
+    for a, part, piece, row, column in packed_places(position_ref.shape[2]):
+        value = packed[row : row + 1, column * LANES : (column + 1) * LANES]
+        sums[a, piece] = value if part == 0 else sums[a, piece] + value
+    for (a, piece), value in sums.items():
+        position_ref[a, :, piece * LANES : (piece + 1) * LANES] = value
+
+
+def add_unpack_kernel(part_ref, other_ref, held_ref, position_ref):
+    rows = part_ref.shape[0]
+    held_ref[...] = (part_ref[...] + other_ref[0:rows, :].astype(F32)).astype(BF16)
+    unpack(other_ref, rows, position_ref)
 
 
 def block_at(k):
@@ -560,7 +627,7 @@
     slab = (features // 4, features // 4 * 3)
     counts = neighbour_count.reshape(1, own)
 
-    def count(part):
+    def count(part, neighbours):
         return call(
             functools.partial(count_kernel, part),
             shape((ghosts, own), F32),
@@ -591,7 +658,7 @@
     describe_call = call(
         describe_kernel,
         (shape((own, 2 * features), F32), shape((own, features), BF16)),
-        [pltpu.VMEM((own, 4 * FB), F32)],
+        [pltpu.VMEM((own, 4 * features), F32)],
         LIMIT,
     )
     ghost_force_call = call(
@@ -604,7 +671,7 @@
             shape((3, sent), F32),
         ),
         [
-            pltpu.VMEM((ghosts, 4 * FB), F32),
+            pltpu.VMEM((ghosts, 4 * features), F32),
             pltpu.VMEM((ghosts, own), F32),
             pltpu.VMEM((3, ghosts, LANES), F32),
         ],
@@ -614,7 +681,7 @@
         own_force_kernel,
         shape((3, own), F32),
         [
-            pltpu.VMEM((own, 4 * FB), F32),
+            pltpu.VMEM((own, 4 * features), F32),
             pltpu.VMEM((own, own), F32),
             pltpu.VMEM((3, own, LANES), F32),
         ],
@@ -629,41 +696,46 @@
         last = step == STEPS - 1
         if step == 0:
             other = across(sent_part)
-            number = [count(k) for k in range(3)]
-            part, held = call(add_kernel, (shape(slab, F32), shape(slab, BF16)))(
-                part, after(other, to_far, to_near, *number)
-            )
-            other = routed(held, "bead", lambda i: i ^ 1)
-            to_far, to_near = after(to_far, held), after(to_near, held)
+            to_far, to_near = after(to_far, sent_part), after(to_near, sent_part)
         from_far = far_pair(to_far)
         from_near = near_pair(to_near)
+        if step == 0:
+            number = [count(k, neighbours) for k in range(2)]
+            with_positions = shape((slab[0] + PACKED, slab[1]), BF16)
+            packed = [pltpu.VMEM((PACKED, slab[1]), F32)]
+            part, held = call(add_pack_kernel, (shape(slab, F32), with_positions), packed)(
+                part, after(other, from_far, from_near, *number), position
+            )
+            other = even_bead(held)
         start = after(position, held) if step == 0 else position
         cols, waves, turned = own_call(start, species, projection, phase_shift)
         if step == 0:
-            part, held = call(add_kernel, (shape(slab, F32), shape(slab, BF16)))(
-                part, after(other, cols, from_far, from_near)
-            )
-            other = routed(held, "bead", lambda i: i ^ 3)
+            bead_shape = shape(position.shape, F32)
+            part, held, one_bead = call(
+                add_pack_kernel, (shape(slab, F32), with_positions, bead_shape), packed
+            )(part, after(other, cols), position)
+            other = odd_bead(held)
+            number.append(count(2, after(neighbours, held)))
             state = weigh_call(
                 after(position, held), from_near, from_far, cols, projection, *number
             )
             ghost_cols, weight, weight_turned, ghost_waves = state
-            held = call(add_kernel, (shape(slab, BF16),))(part, after(other, *state))[0]
+            held, other_bead = call(add_unpack_kernel, (shape(slab, BF16), bead_shape))(
+                part, after(other, *state)
+            )
             pieces = [held] + [routed(held, "dom", lambda i: (i - 4 * k) % 16) for k in (1, 2, 3)]
-            above = passed_along(after(position, held), "bead", -1)
             sines, low = describe_call(after(weight_turned, held), waves, ghost_waves, turned)
             half = call(ring_kernel, shape((features, features), BF16))(
-                pieces[0], *[after(piece, low, above) for piece in pieces[1:]]
+                pieces[0], *[after(piece, low) for piece in pieces[1:]]
             )
             other_half = near_pair(half)
-            below = passed_along(after(position, half), "bead", 1)
         else:
-            above = passed_along(after(position, cols, from_far, from_near), "bead", -1)
+            one_bead = even_bead(after(position, cols, from_far, from_near))
             ghost_cols, weight, weight_turned, ghost_waves = weigh_call(
                 position, from_near, from_far, cols, projection, *number
             )
             sines, low = describe_call(weight_turned, waves, ghost_waves, turned)
-            below = passed_along(after(position, low), "bead", 1)
+            other_bead = odd_bead(after(position, low))
         grad, spread, centre, near_force, far_force = ghost_force_call(
             low,
             half,
@@ -693,8 +765,8 @@
             send_lists,
             position,
             velocity,
-            below,
-            above,
+            other_bead,
+            one_bead,
             species,
         )
         if not last:

time: 71.8 us -> 68.6 us (0.955)
  the two profiles are of different devices: /device:TPU:6 before, /device:TPU:0 now
where the time goes in v5:
time: 68.6 us; the launch traced here: 68.5 us
  Pallas kernels  31.8 us (46%)
  starting transfers between devices  24.4 us (36%)
  waiting for transfers between devices  9.49 us (14%)
  between operations  0.94 us (1%)
  other arithmetic  0.8 us (1%)
  local copies, waits for them, and re-layouts  0.74 us (1%)
    ppermute x16, starting transfers between devices, routed(): lax.ppermute(block, axis, [(source(i), i) for i in range(lax.axis_size(ax...  21.2 us
    ppermute x16, waiting for transfers between devices, routed(): lax.ppermute(block, axis, [(source(i), i) for i in range(lax.axis_size(ax...  9.49 us
    pallas_call x2, Pallas kernels, shards(): own_force_call(grad, spread, sines, waves, weight, cols, position, centre...  7.05 us
    pallas_call x2, Pallas kernels, shards(): cols, waves, turned = own_call(start, species, projection, phase_shift)  5.72 us
    pallas_call x2, Pallas kernels, shards(): ghost_force_call(low, half, other_half, cols, turned, weight, ghost_waves...  5.66 us
    pallas_call x3, Pallas kernels, count(): call(functools.partial(count_kernel, part), shape((ghosts, own), F32), [p...  3.22 us
    ppermute x1, starting transfers between devices, across(): return lax.ppermute(block, ('dom', 'bead'), route)  3.17 us
    pallas_call x1, Pallas kernels, shards(): describe_call(after(weight_turned, held), waves, ghost_waves, turned)  1.96 us
  transfers between devices with their start and end apart: 17, of which 8 were waited for; matrix products, arithmetic and copies ran while one was open for 0% of the time, Pallas kernels for 39%

profile of v5, /device:TPU:0, one launch (start us, length us, event | category | flops | bytes accessed | tf_op | source)
XLA Modules:
  0.0 68.5 jit_solution(1674163569612146353)
XLA Ops:
  0.7 0.8 %convert_multiply_fusion = f32[1,250]{1,0:T(1,128)S(1)} fusion(bf16[2,250]{1,0:T(2,128)(2,1)} %param.19, s32[]{:T(128)S(6)} %select_n.21), kind=kLoop, calls=%fused_computation.6 | loop fusion | flops 500 | bytes 1504 | tf_op jit(solution)/shard_map/mul | solution.py:524
  2.7 3.2 %collective-permute-start = (bf16[128,384]{1,0:T(8,128)(2,1)S(1)}, bf16[128,384]{1,0:T(8,128)(2,1)S(1)}, u32[]{:S(2)}, u32[]{:S(2)}) collective-permute-start(bf16[128,384]{1,0:T(8,128)(2,1)S(1)} %get-tuple-element.62), channel_id=1, source_target_pairs={{20,0},{21,1},{22,2},{23,3},{16,4},{17,5},{18,6},{19,7},{28,8},{29... | collective-permute-start | bytes 294920 | tf_op jit(solution)/shard_map/ppermute | solution.py:502
  6.4 2.9 %collective-permute-start.1 = (f32[4,128]{1,0:T(4,128)S(1)}, f32[4,128]{1,0:T(4,128)S(1)}, u32[]{:S(2)}, u32[]{:S(2)}) collective-permute-start(f32[4,128]{1,0:T(4,128)S(1)} %get-tuple-element.64), channel_id=1, source_target_pairs={{120,0},{16,8},{8,16},{32,24},{24,32},{48,40},{40,48},{64,56},{56,... | collective-permute-start | bytes 6152 | tf_op jit(solution)/shard_map/ppermute | solution.py:488
  9.2 1.1 %shard_map.116.rest_1_ = f32[256,512]{1,0:T(8,128)S(1)} custom-call(s32[32,512]{1,0:T(8,128)S(1)} %copy-done.2, s32[1,512]{1,0:T(1,128)S(1)} %bitcast.33), custom_call_target="tpu_custom_call" | custom-call | tf_op jit(solution)/shard_map/pallas_call | solution.py:631
  10.3 1.1 %shard_map.115.rest_0_ = f32[256,512]{1,0:T(8,128)S(1)} custom-call(s32[32,512]{1,0:T(8,128)S(1)} %copy-done.2, s32[1,512]{1,0:T(1,128)S(1)} %bitcast.34), custom_call_target="tpu_custom_call" | custom-call | tf_op jit(solution)/shard_map/pallas_call | solution.py:631
  11.6 1.6 %collective-permute-start.3 = (bf16[144,384]{1,0:T(8,128)(2,1)S(1)}, bf16[144,384]{1,0:T(8,128)(2,1)S(1)}, u32[]{:S(2)}, u32[]{:S(2)}) collective-permute-start(bf16[144,384]{1,0:T(8,128)(2,1)S(1)} %get-tuple-element.69), channel_id=1, source_target_pairs={{1,0},{0,1},{3,2},{2,3},{5,4},{4,5},{7,6},{6,7},{9,8},{8,9},{11,10... | collective-permute-start | bytes 331784 | tf_op jit(solution)/shard_map/ppermute | solution.py:488
  13.2 2.9 %shard_map.118 = (f32[512,128]{1,0:T(8,128)S(1)}, bf16[512,2048]{1,0:T(8,128)(2,1)S(1)}, f32[512,2048]{1,0:T(8,128)S(1)}) custom-call(f32[3,1,512]{2,1,0:T(1,128)S(1)} %bitcast.22, s32[1,512]{1,0:T(1,128)S(1)} %bitcast.29, f32[3,2,512]{2,1,0:T(2,128)S(1)} %bitcast.12, f32[2,512]{1,0:T(2,128)S(1)} %copy-done.6), custom_call_target="tpu_custom_call" | custom-call | tf_op jit(solution)/shard_map/pallas_call | solution.py:711
  16.1 0.9 %collective-permute-done.3.other_ref = bf16[144,384]{1,0:T(8,128)(2,1)S(1)} collective-permute-done((bf16[144,384]{1,0:T(8,128)(2,1)S(1)}, bf16[144,384]{1,0:T(8,128)(2,1)S(1)}, u32[]{:S(2)}, u32[]{:S(2)}) %collective-permute-start.3) | collective-permute-done | bytes 110624 | tf_op jit(solution)/shard_map/ppermute | solution.py:488
  17.1 3.9 %collective-permute-start.4 = (bf16[144,384]{1,0:T(8,128)(2,1)S(1)}, bf16[144,384]{1,0:T(8,128)(2,1)S(1)}, u32[]{:S(2)}, u32[]{:S(2)}) collective-permute-start(bf16[144,384]{1,0:T(8,128)(2,1)S(1)} %get-tuple-element.73), channel_id=1, source_target_pairs={{7,0},{2,1},{1,2},{4,3},{3,4},{6,5},{5,6},{0,7},{15,8},{10,9},{9,1... | collective-permute-start | bytes 331784 | tf_op jit(solution)/shard_map/ppermute | solution.py:488
  21.0 1.1 %shard_map.120.rest_2_ = f32[256,512]{1,0:T(8,128)S(1)} custom-call(s32[32,512]{1,0:T(8,128)S(1)} %copy-done.2, s32[1,512]{1,0:T(1,128)S(1)} %bitcast.35), custom_call_target="tpu_custom_call" | custom-call | tf_op jit(solution)/shard_map/pallas_call | solution.py:631
  22.1 1.7 %shard_map.121 = (f32[256,128]{1,0:T(8,128)S(1)}, f32[768,512]{1,0:T(8,128)S(1)}, bf16[512,768]{1,0:T(8,128)(2,1)S(1)}, bf16[256,2048]{1,0:T(8,128)(2,1)S(1)}) custom-call(f32[3,1,512]{2,1,0:T(1,128)S(1)} %bitcast.24, f32[4,128]{1,0:T(4,128)S(1)} %collective-permute-done.2.near_ref, f32[4,128]{1,0:T(4,128)S(1)} %collective-permute-done.1.far_ref, ...), custom_call_target="tpu_custom_call" | custom-call | tf_op jit(solution)/shard_map/pallas_call | solution.py:719
  23.8 1.7 %collective-permute-done.4.other_ref = bf16[144,384]{1,0:T(8,128)(2,1)S(1)} collective-permute-done((bf16[144,384]{1,0:T(8,128)(2,1)S(1)}, bf16[144,384]{1,0:T(8,128)(2,1)S(1)}, u32[]{:S(2)}, u32[]{:S(2)}) %collective-permute-start.4) | collective-permute-done | bytes 110624 | tf_op jit(solution)/shard_map/ppermute | solution.py:488
  25.5 2.3 %collective-permute-start.7 = (bf16[128,384]{1,0:T(8,128)(2,1)S(1)}, bf16[128,384]{1,0:T(8,128)(2,1)S(1)}, u32[]{:S(2)}, u32[]{:S(2)}) collective-permute-start(bf16[128,384]{1,0:T(8,128)(2,1)S(1)} %get-tuple-element.82.refs_0_), channel_id=1, source_target_pairs={{32,0},{40,8},{48,16},{56,24},{64,32},{72,40},{80,48},{88,56},{96,... | collective-permute-start | bytes 294920 | tf_op jit(solution)/shard_map/ppermute | solution.py:488
  27.9 1.3 %collective-permute-start.5 = (bf16[128,384]{1,0:T(8,128)(2,1)S(1)}, bf16[128,384]{1,0:T(8,128)(2,1)S(1)}, u32[]{:S(2)}, u32[]{:S(2)}) collective-permute-start(bf16[128,384]{1,0:T(8,128)(2,1)S(1)} %get-tuple-element.82.refs_0_), channel_id=1, source_target_pairs={{96,0},{104,8},{112,16},{120,24},{0,32},{8,40},{16,48},{24,56},{32... | collective-permute-start | bytes 294920 | tf_op jit(solution)/shard_map/ppermute | solution.py:488
  29.2 2.0 %shard_map.123 = (f32[512,1024]{1,0:T(8,128)S(1)}, bf16[512,512]{1,0:T(8,128)(2,1)S(1)}) custom-call(bf16[512,768]{1,0:T(8,128)(2,1)S(1)} %get-tuple-element.83.weight_turned, bf16[512,2048]{1,0:T(8,128)(2,1)S(1)} %get-tuple-element.84.own_waves.waves, bf16[256,2048]{1,0:T(8,128)(2,1)S(1)} %get-tuple-element.80.ghost_waves.waves, ...), custom_call_target="tpu_custom_call" | custom-call | tf_op jit(solution)/shard_map/pallas_call | solution.py:727
  31.1 3.0 %collective-permute-done.6.refs_2_ = bf16[128,384]{1,0:T(8,128)(2,1)S(1)} collective-permute-done((bf16[128,384]{1,0:T(8,128)(2,1)S(1)}, bf16[128,384]{1,0:T(8,128)(2,1)S(1)}, u32[]{:S(2)}, u32[]{:S(2)}) %collective-permute-start.6) | collective-permute-done | bytes 98336 | tf_op jit(solution)/shard_map/ppermute | solution.py:488
  34.1 0.7 collective-permute-done.5.refs_1_
  35.0 1.9 %collective-permute-done.8.other_ref = bf16[512,512]{1,0:T(8,128)(2,1)S(1)} collective-permute-done((bf16[512,512]{1,0:T(8,128)(2,1)S(1)}, bf16[512,512]{1,0:T(8,128)(2,1)S(1)}, u32[]{:S(2)}, u32[]{:S(2)}) %collective-permute-start.8) | collective-permute-done | bytes 524320 | tf_op jit(solution)/shard_map/ppermute | solution.py:488
  36.9 2.8 %shard_map.125 = (f32[512,512]{1,0:T(8,128)S(1)}, bf16[512,2048]{1,0:T(8,128)(2,1)S(1)}, f32[3,512]{1,0:T(4,128)S(1)}, f32[3,128]{1,0:T(4,128)S(1)}, f32[3,128]{1,0:T(4,128)S(1)}) custom-call(bf16[512,512]{1,0:T(8,128)(2,1)S(1)} %get-tuple-element.86.low, bf16[512,512]{1,0:T(8,128)(2,1)S(1)} %shard_map.124.half_ref, ...), custom_call_target="tpu_custom_call" | custom-call | tf_op jit(solution)/shard_map/pallas_call | solution.py:739
  40.0 1.2 %collective-permute-start.10 = (f32[3,128]{1,0:T(4,128)S(1)}, f32[3,128]{1,0:T(4,128)S(1)}, u32[]{:S(2)}, u32[]{:S(2)}) collective-permute-start(f32[3,128]{1,0:T(4,128)S(1)} %get-tuple-element.95), channel_id=1, source_target_pairs={{120,0},{16,8},{8,16},{32,24},{24,32},{48,40},{40,48},{64,56},{56,... | collective-permute-start | bytes 4616 | tf_op jit(solution)/shard_map/ppermute | solution.py:488
  41.2 3.5 %shard_map.126.force_ref = f32[3,512]{1,0:T(4,128)S(1)} custom-call(f32[512,512]{1,0:T(8,128)S(1)} %get-tuple-element.90.grad, bf16[512,2048]{1,0:T(8,128)(2,1)S(1)} %get-tuple-element.91.spread, f32[512,1024]{1,0:T(8,128)S(1)} %get-tuple-element.92.sines, bf16[512,2048]{1,0:T(8,128)(2,1)S(1)} %get-tuple-element.84.own_waves.waves, ...), custom_call_target="tpu_custom_call" | custom-call | tf_op jit(solution)/shard_map/pallas_call | solution.py:753
  45.1 0.9 %shard_map.127 = (f32[3,1,512]{2,1,0:T(1,128)S(1)}, f32[3,1,512]{2,1,0:T(1,128)S(1)}, f32[4,128]{1,0:T(4,128)S(1)}, f32[4,128]{1,0:T(4,128)S(1)}) custom-call(f32[3,512]{1,0:T(4,128)S(1)} %shard_map.126.force_ref, f32[3,128]{1,0:T(4,128)S(1)} %collective-permute-done.9.near_back_ref, f32[3,128]{1,0:T(4,128)S(1)} %collective-permute-done.10.far_back_ref, ...), custom_call_target="tpu_custom_call" | custom-call | tf_op jit(solution)/shard_map/pallas_call | solution.py:757
  46.1 2.6 %collective-permute-start.12 = (f32[4,128]{1,0:T(4,128)S(1)}, f32[4,128]{1,0:T(4,128)S(1)}, u32[]{:S(2)}, u32[]{:S(2)}) collective-permute-start(f32[4,128]{1,0:T(4,128)S(1)} %get-tuple-element.100), channel_id=1, source_target_pairs={{120,0},{16,8},{8,16},{32,24},{24,32},{48,40},{40,48},{64,56},{56,... | collective-permute-start | bytes 6152 | tf_op jit(solution)/shard_map/ppermute | solution.py:488
  48.6 2.9 %shard_map.128 = (f32[512,128]{1,0:T(8,128)S(1)}, bf16[512,2048]{1,0:T(8,128)(2,1)S(1)}, f32[512,2048]{1,0:T(8,128)S(1)}) custom-call(f32[3,1,512]{2,1,0:T(1,128)S(1)} %get-tuple-element.117.position_ref, s32[1,512]{1,0:T(1,128)S(1)} %bitcast.31, f32[3,2,512]{2,1,0:T(2,128)S(1)} %bitcast.16, f32[2,512]{1,0:T(2,128)S(1)} %copy-done.6), custom_call_target="tpu_custom_call" | custom-call | tf_op jit(solution)/shard_map/pallas_call | solution.py:711
  51.6 1.7 %shard_map.129 = (f32[256,128]{1,0:T(8,128)S(1)}, f32[768,512]{1,0:T(8,128)S(1)}, bf16[512,768]{1,0:T(8,128)(2,1)S(1)}, bf16[256,2048]{1,0:T(8,128)(2,1)S(1)}) custom-call(f32[3,1,512]{2,1,0:T(1,128)S(1)} %get-tuple-element.117.position_ref, f32[4,128]{1,0:T(4,128)S(1)} %collective-permute-done.11.near_ref, f32[4,128]{1,0:T(4,128)S(1)} %collective-permute-done.12.far_ref, ...), custom_call_target="tpu_custom_call" | custom-call | tf_op jit(solution)/shard_map/pallas_call | solution.py:734
  53.4 2.0 %shard_map.130 = (f32[512,1024]{1,0:T(8,128)S(1)}, bf16[512,512]{1,0:T(8,128)(2,1)S(1)}) custom-call(bf16[512,768]{1,0:T(8,128)(2,1)S(1)} %get-tuple-element.102.weight_turned, bf16[512,2048]{1,0:T(8,128)(2,1)S(1)} %get-tuple-element.103.own_waves.waves, bf16[256,2048]{1,0:T(8,128)(2,1)S(1)} %get-tuple-element.104.ghost_waves.waves, ...), custom_call_target="tpu_custom_call" | custom-call | tf_op jit(solution)/shard_map/pallas_call | solution.py:737
  55.3 3.7 %collective-permute-start.15 = (f32[3,1,512]{2,1,0:T(1,128)S(1)}, f32[3,1,512]{2,1,0:T(1,128)S(1)}, u32[]{:S(2)}, u32[]{:S(2)}) collective-permute-start(f32[3,1,512]{2,1,0:T(1,128)S(1)} %get-tuple-element.117.position_ref), channel_id=1, source_target_pairs={{7,0},{2,1},{1,2},{4,3},{3,4},{6,5},{5,6},{0,7},{15,8},{10,9},{9,1... | collective-permute-start | bytes 18440 | tf_op jit(solution)/shard_map/ppermute | solution.py:488
  59.0 2.9 %shard_map.131 = (f32[512,512]{1,0:T(8,128)S(1)}, bf16[512,2048]{1,0:T(8,128)(2,1)S(1)}, f32[3,512]{1,0:T(4,128)S(1)}, f32[3,128]{1,0:T(4,128)S(1)}, f32[3,128]{1,0:T(4,128)S(1)}) custom-call(bf16[512,512]{1,0:T(8,128)(2,1)S(1)} %get-tuple-element.106.low, bf16[512,512]{1,0:T(8,128)(2,1)S(1)} %shard_map.124.half_ref, ...), custom_call_target="tpu_custom_call" | custom-call | tf_op jit(solution)/shard_map/pallas_call | solution.py:739
  62.0 1.2 %collective-permute-start.14 = (f32[3,128]{1,0:T(4,128)S(1)}, f32[3,128]{1,0:T(4,128)S(1)}, u32[]{:S(2)}, u32[]{:S(2)}) collective-permute-start(f32[3,128]{1,0:T(4,128)S(1)} %get-tuple-element.114), channel_id=1, source_target_pairs={{120,0},{16,8},{8,16},{32,24},{24,32},{48,40},{40,48},{64,56},{56,... | collective-permute-start | bytes 4616 | tf_op jit(solution)/shard_map/ppermute | solution.py:488
  63.1 3.5 %shard_map.132.force_ref = f32[3,512]{1,0:T(4,128)S(1)} custom-call(f32[512,512]{1,0:T(8,128)S(1)} %get-tuple-element.109.grad, bf16[512,2048]{1,0:T(8,128)(2,1)S(1)} %get-tuple-element.110.spread, f32[512,1024]{1,0:T(8,128)S(1)} %get-tuple-element.111.sines, bf16[512,2048]{1,0:T(8,128)(2,1)S(1)} %get-tuple-element.103.own_waves.waves, ...), custom_call_target="tpu_custom_call" | custom-call | tf_op jit(solution)/shard_map/pallas_call | solution.py:753
  66.7 0.8 %collective-permute-done.14.far_back_ref = f32[3,128]{1,0:T(4,128)S(1)} collective-permute-done((f32[3,128]{1,0:T(4,128)S(1)}, f32[3,128]{1,0:T(4,128)S(1)}, u32[]{:S(2)}, u32[]{:S(2)}) %collective-permute-start.14) | collective-permute-done | bytes 1568 | tf_op jit(solution)/shard_map/ppermute | solution.py:488
  67.5 1.0 %shard_map.133 = (f32[3,1,512]{2,1,0:T(1,128)}, f32[3,1,512]{2,1,0:T(1,128)}) custom-call(f32[3,512]{1,0:T(4,128)S(1)} %shard_map.132.force_ref, f32[3,128]{1,0:T(4,128)S(1)} %collective-permute-done.13.near_back_ref, f32[3,128]{1,0:T(4,128)S(1)} %collective-permute-done.14.far_back_ref, s32[2,128]{1,0:T(2,128)S(1)} %copy-done.7, ...), custom_call_target="tpu_custom_call" | custom-call | tf_op jit(solution)/shard_map/pallas_call | solution.py:757
  (45 shorter events, 3.1 us)
Async XLA Ops:
  0.6 1.0 %copy-start = (bf16[2,250,512]{2,0,1:T(2,128)(2,1)S(1)}, bf16[2,250,512]{2,0,1:T(2,128)(2,1)}, u32[]{:S(2)}) copy-start(bf16[2,250,512]{2,0,1:T(2,128)(2,1)} %param.18) | copy-start | bytes 1536004
  0.6 5.2 %copy-start.7 = (s32[2,128]{1,0:T(2,128)S(1)}, s32[2,128]{1,0:T(2,128)}, u32[]{:S(2)}) copy-start(s32[2,128]{1,0:T(2,128)} %lists_ref.5) | copy-start | bytes 3076
  0.7 5.2 %copy-start.4 = (s32[512]{0:T(512)S(1)}, s32[512]{0:T(512)}, u32[]{:S(2)}) copy-start(s32[512]{0:T(512)} %param.12) | copy-start | bytes 6148
  0.7 5.2 %copy-start.3 = (f32[1,3,512]{2,0,1:T(1,128)S(1)}, f32[1,3,512]{2,0,1:T(1,128)}, u32[]{:S(2)}) copy-start(f32[1,3,512]{2,0,1:T(1,128)} %param.10) | copy-start | bytes 18436
  0.7 8.5 %copy-start.2 = (s32[32,512]{1,0:T(8,128)S(1)}, s32[32,512]{1,0:T(8,128)}, u32[]{:S(2)}) copy-start(s32[32,512]{1,0:T(8,128)} %neighbours_ref.4) | copy-start | bytes 196612
  0.7 8.5 %copy-start.5 = (s32[512]{0:T(512)S(1)}, s32[512]{0:T(512)}, u32[]{:S(2)}) copy-start(s32[512]{0:T(512)} %param.14) | copy-start | bytes 6148
  0.7 12.5 %copy-start.6 = (f32[2,512]{1,0:T(2,128)S(1)}, f32[2,512]{1,0:T(2,128)}, u32[]{:S(2)}) copy-start(f32[2,512]{1,0:T(2,128)} %shift_ref.3) | copy-start | bytes 12292
  0.7 12.5 %copy-start.1 = (f32[2,3,512]{2,0,1:T(2,128)S(1)}, f32[2,3,512]{2,0,1:T(2,128)}, u32[]{:S(2)}) copy-start(f32[2,3,512]{2,0,1:T(2,128)} %param.16) | copy-start | bytes 36868
  2.7 8.8 %collective-permute-start = (bf16[128,384]{1,0:T(8,128)(2,1)S(1)}, bf16[128,384]{1,0:T(8,128)(2,1)S(1)}, u32[]{:S(2)}, u32[]{:S(2)}) collective-permute-start(bf16[128,384]{1,0:T(8,128)(2,1)S(1)} %get-tuple-element.62), channel_id=1, source_target_pairs={{20,0},{21,1},{22,2},{23,3},{16,4},{17,5},{18,6},{19,7},{28,8},{29... | collective-permute-start | bytes 294920 | tf_op jit(solution)/shard_map/ppermute | solution.py:502
  6.4 5.2 %collective-permute-start.1 = (f32[4,128]{1,0:T(4,128)S(1)}, f32[4,128]{1,0:T(4,128)S(1)}, u32[]{:S(2)}, u32[]{:S(2)}) collective-permute-start(f32[4,128]{1,0:T(4,128)S(1)} %get-tuple-element.64), channel_id=1, source_target_pairs={{120,0},{16,8},{8,16},{32,24},{24,32},{48,40},{40,48},{64,56},{56,... | collective-permute-start | bytes 6152 | tf_op jit(solution)/shard_map/ppermute | solution.py:488
  9.2 2.4 %collective-permute-start.2 = (f32[4,128]{1,0:T(4,128)S(1)}, f32[4,128]{1,0:T(4,128)S(1)}, u32[]{:S(2)}, u32[]{:S(2)}) collective-permute-start(f32[4,128]{1,0:T(4,128)S(1)} %get-tuple-element.66), channel_id=1, source_target_pairs={{8,0},{0,8},{24,16},{16,24},{40,32},{32,40},{56,48},{48,56},{72,64... | collective-permute-start | bytes 6152 | tf_op jit(solution)/shard_map/ppermute | solution.py:488
  11.6 5.4 %collective-permute-start.3 = (bf16[144,384]{1,0:T(8,128)(2,1)S(1)}, bf16[144,384]{1,0:T(8,128)(2,1)S(1)}, u32[]{:S(2)}, u32[]{:S(2)}) collective-permute-start(bf16[144,384]{1,0:T(8,128)(2,1)S(1)} %get-tuple-element.69), channel_id=1, source_target_pairs={{1,0},{0,1},{3,2},{2,3},{5,4},{4,5},{7,6},{6,7},{9,8},{8,9},{11,10... | collective-permute-start | bytes 331784 | tf_op jit(solution)/shard_map/ppermute | solution.py:488
  17.1 8.4 %collective-permute-start.4 = (bf16[144,384]{1,0:T(8,128)(2,1)S(1)}, bf16[144,384]{1,0:T(8,128)(2,1)S(1)}, u32[]{:S(2)}, u32[]{:S(2)}) collective-permute-start(bf16[144,384]{1,0:T(8,128)(2,1)S(1)} %get-tuple-element.73), channel_id=1, source_target_pairs={{7,0},{2,1},{1,2},{4,3},{3,4},{6,5},{5,6},{0,7},{15,8},{10,9},{9,1... | collective-permute-start | bytes 331784 | tf_op jit(solution)/shard_map/ppermute | solution.py:488
  25.5 5.6 %collective-permute-start.7 = (bf16[128,384]{1,0:T(8,128)(2,1)S(1)}, bf16[128,384]{1,0:T(8,128)(2,1)S(1)}, u32[]{:S(2)}, u32[]{:S(2)}) collective-permute-start(bf16[128,384]{1,0:T(8,128)(2,1)S(1)} %get-tuple-element.82.refs_0_), channel_id=1, source_target_pairs={{32,0},{40,8},{48,16},{56,24},{64,32},{72,40},{80,48},{88,56},{96,... | collective-permute-start | bytes 294920 | tf_op jit(solution)/shard_map/ppermute | solution.py:488
  27.9 6.2 %collective-permute-start.6 = (bf16[128,384]{1,0:T(8,128)(2,1)S(1)}, bf16[128,384]{1,0:T(8,128)(2,1)S(1)}, u32[]{:S(2)}, u32[]{:S(2)}) collective-permute-start(bf16[128,384]{1,0:T(8,128)(2,1)S(1)} %get-tuple-element.82.refs_0_), channel_id=1, source_target_pairs={{64,0},{72,8},{80,16},{88,24},{96,32},{104,40},{112,48},{120,56},{... | collective-permute-start | bytes 294920 | tf_op jit(solution)/shard_map/ppermute | solution.py:488
  27.9 6.9 %collective-permute-start.5 = (bf16[128,384]{1,0:T(8,128)(2,1)S(1)}, bf16[128,384]{1,0:T(8,128)(2,1)S(1)}, u32[]{:S(2)}, u32[]{:S(2)}) collective-permute-start(bf16[128,384]{1,0:T(8,128)(2,1)S(1)} %get-tuple-element.82.refs_0_), channel_id=1, source_target_pairs={{96,0},{104,8},{112,16},{120,24},{0,32},{8,40},{16,48},{24,56},{32... | collective-permute-start | bytes 294920 | tf_op jit(solution)/shard_map/ppermute | solution.py:488
  34.9 2.0 %collective-permute-start.8 = (bf16[512,512]{1,0:T(8,128)(2,1)S(1)}, bf16[512,512]{1,0:T(8,128)(2,1)S(1)}, u32[]{:S(2)}, u32[]{:S(2)}) collective-permute-start(bf16[512,512]{1,0:T(8,128)(2,1)S(1)} %shard_map.124.half_ref), channel_id=1, source_target_pairs={{8,0},{0,8},{24,16},{16,24},{40,32},{32,40},{56,48},{48,56},{72,64... | collective-permute-start | bytes 1572872 | tf_op jit(solution)/shard_map/ppermute | solution.py:488
  39.7 5.0 %collective-permute-start.9 = (f32[3,128]{1,0:T(4,128)S(1)}, f32[3,128]{1,0:T(4,128)S(1)}, u32[]{:S(2)}, u32[]{:S(2)}) collective-permute-start(f32[3,128]{1,0:T(4,128)S(1)} %get-tuple-element.94), channel_id=1, source_target_pairs={{8,0},{0,8},{24,16},{16,24},{40,32},{32,40},{56,48},{48,56},{72,64... | collective-permute-start | bytes 4616 | tf_op jit(solution)/shard_map/ppermute | solution.py:488
  40.0 5.1 %collective-permute-start.10 = (f32[3,128]{1,0:T(4,128)S(1)}, f32[3,128]{1,0:T(4,128)S(1)}, u32[]{:S(2)}, u32[]{:S(2)}) collective-permute-start(f32[3,128]{1,0:T(4,128)S(1)} %get-tuple-element.95), channel_id=1, source_target_pairs={{120,0},{16,8},{8,16},{32,24},{24,32},{48,40},{40,48},{64,56},{56,... | collective-permute-start | bytes 4616 | tf_op jit(solution)/shard_map/ppermute | solution.py:488
  41.2 3.9 %copy-start.8 = (f32[1,3,512]{2,0,1:T(1,128)S(1)}, f32[1,3,512]{2,0,1:T(1,128)}, u32[]{:S(2)}) copy-start(f32[1,3,512]{2,0,1:T(1,128)} %param.11) | copy-start | bytes 18436
  46.0 5.6 %collective-permute-start.11 = (f32[4,128]{1,0:T(4,128)S(1)}, f32[4,128]{1,0:T(4,128)S(1)}, u32[]{:S(2)}, u32[]{:S(2)}) collective-permute-start(f32[4,128]{1,0:T(4,128)S(1)} %get-tuple-element.99), channel_id=1, source_target_pairs={{8,0},{0,8},{24,16},{16,24},{40,32},{32,40},{56,48},{48,56},{72,64... | collective-permute-start | bytes 6152 | tf_op jit(solution)/shard_map/ppermute | solution.py:488
  46.1 5.5 %collective-permute-start.12 = (f32[4,128]{1,0:T(4,128)S(1)}, f32[4,128]{1,0:T(4,128)S(1)}, u32[]{:S(2)}, u32[]{:S(2)}) collective-permute-start(f32[4,128]{1,0:T(4,128)S(1)} %get-tuple-element.100), channel_id=1, source_target_pairs={{120,0},{16,8},{8,16},{32,24},{24,32},{48,40},{40,48},{64,56},{56,... | collective-permute-start | bytes 6152 | tf_op jit(solution)/shard_map/ppermute | solution.py:488
  51.5 15.9 %collective-permute-start.16 = (f32[3,1,512]{2,1,0:T(1,128)S(1)}, f32[3,1,512]{2,1,0:T(1,128)S(1)}, u32[]{:S(2)}, u32[]{:S(2)}) collective-permute-start(f32[3,1,512]{2,1,0:T(1,128)S(1)} %get-tuple-element.117.position_ref), channel_id=1, source_target_pairs={{1,0},{0,1},{3,2},{2,3},{5,4},{4,5},{7,6},{6,7},{9,8},{8,9},{11,10... | collective-permute-start | bytes 18440 | tf_op jit(solution)/shard_map/ppermute | solution.py:488
  55.3 12.1 %collective-permute-start.15 = (f32[3,1,512]{2,1,0:T(1,128)S(1)}, f32[3,1,512]{2,1,0:T(1,128)S(1)}, u32[]{:S(2)}, u32[]{:S(2)}) collective-permute-start(f32[3,1,512]{2,1,0:T(1,128)S(1)} %get-tuple-element.117.position_ref), channel_id=1, source_target_pairs={{7,0},{2,1},{1,2},{4,3},{3,4},{6,5},{5,6},{0,7},{15,8},{10,9},{9,1... | collective-permute-start | bytes 18440 | tf_op jit(solution)/shard_map/ppermute | solution.py:488
  61.9 4.8 %collective-permute-start.13 = (f32[3,128]{1,0:T(4,128)S(1)}, f32[3,128]{1,0:T(4,128)S(1)}, u32[]{:S(2)}, u32[]{:S(2)}) collective-permute-start(f32[3,128]{1,0:T(4,128)S(1)} %get-tuple-element.113), channel_id=1, source_target_pairs={{8,0},{0,8},{24,16},{16,24},{40,32},{32,40},{56,48},{48,56},{72,64... | collective-permute-start | bytes 4616 | tf_op jit(solution)/shard_map/ppermute | solution.py:488
  62.0 5.5 %collective-permute-start.14 = (f32[3,128]{1,0:T(4,128)S(1)}, f32[3,128]{1,0:T(4,128)S(1)}, u32[]{:S(2)}, u32[]{:S(2)}) collective-permute-start(f32[3,128]{1,0:T(4,128)S(1)} %get-tuple-element.114), channel_id=1, source_target_pairs={{120,0},{16,8},{8,16},{32,24},{24,32},{48,40},{40,48},{64,56},{56,... | collective-permute-start | bytes 4616 | tf_op jit(solution)/shard_map/ppermute | solution.py:488

commit v6 on v4

--- a/solution.py
+++ b/solution.py
@@ -110,8 +110,8 @@
     lists_ref,
     position_ref,
     velocity_ref,
-    below_ref,
-    above_ref,
+    one_bead_ref,
+    other_bead_ref,
     species_ref,
     new_position_ref,
     new_velocity_ref,
@@ -138,7 +138,7 @@
     rows = []
     for a in range(3):
         here = position_ref[a]
-        chain = 2.0 * here - below_ref[a] - above_ref[a]
+        chain = 2.0 * here - one_bead_ref[a] - other_bead_ref[a]
         total = force_ref[a : a + 1, :] + extra[a] - KAPPA * mass * chain
         velocity = velocity_ref[a] + DT * (total / mass)
         place = here + DT * velocity
@@ -307,6 +307,26 @@
             return carry
 
         each(own, describe)
+
+
+def weigh_describe_kernel(
+    position_ref, near_ref, far_ref, own_cols, projection_ref, own_waves, turned, *rest
+):
+    *numbers, ghost_cols, weight, ghost_waves, sines, low, rows_in, weight_turned, sums = rest
+    weigh_kernel(
+        position_ref,
+        near_ref,
+        far_ref,
+        own_cols,
+        projection_ref,
+        *numbers,
+        ghost_cols,
+        weight,
+        weight_turned,
+        ghost_waves,
+        rows_in,
+    )
+    describe_kernel(weight_turned, own_waves, ghost_waves, turned, sines, low, sums)
 
 
 def fold(value):
@@ -462,12 +482,6 @@
         )
 
 
-def passed_along(block, axis, distance):
-    devices = range(lax.axis_size(axis))
-    route = [((i - distance) % len(devices), i) for i in devices]
-    return lax.ppermute(block, axis, route)
-
-
 def routed(block, axis, source):
     return lax.ppermute(block, axis, [(source(i), i) for i in range(lax.axis_size(axis))])
 
@@ -484,6 +498,14 @@
     beads = lax.axis_size("bead")
     route = [(i ^ (2 * beads + 4), i) for i in range(beads * lax.axis_size("dom"))]
     return lax.ppermute(block, ("dom", "bead"), route)
+
+
+def even_bead(block):
+    return routed(block, "bead", lambda i: i ^ 1)
+
+
+def odd_bead(block):
+    return routed(block, "bead", lambda i: (i - 1 + i % 2 * 2) % lax.axis_size("bead"))
 
 
 def after(value, *others):
@@ -560,7 +582,7 @@
     slab = (features // 4, features // 4 * 3)
     counts = neighbour_count.reshape(1, own)
 
-    def count(part):
+    def count(part, neighbours):
         return call(
             functools.partial(count_kernel, part),
             shape((ghosts, own), F32),
@@ -592,6 +614,22 @@
         describe_kernel,
         (shape((own, 2 * features), F32), shape((own, features), BF16)),
         [pltpu.VMEM((own, 4 * FB), F32)],
+        LIMIT,
+    )
+    weigh_describe_call = call(
+        weigh_describe_kernel,
+        (
+            shape((ghosts, LANES), F32),
+            shape((everyone, own), F32),
+            shape((ghosts, 4 * features), BF16),
+            shape((own, 2 * features), F32),
+            shape((own, features), BF16),
+        ),
+        [
+            pltpu.VMEM((LANES, ghosts), F32),
+            pltpu.VMEM((own, everyone), BF16),
+            pltpu.VMEM((own, 4 * FB), F32),
+        ],
         LIMIT,
     )
     ghost_force_call = call(
@@ -629,41 +667,42 @@
         last = step == STEPS - 1
         if step == 0:
             other = across(sent_part)
-            number = [count(k) for k in range(3)]
+            to_far, to_near = after(to_far, sent_part), after(to_near, sent_part)
+        from_far = far_pair(to_far)
+        from_near = near_pair(to_near)
+        if step == 0:
+            number = [count(k, neighbours) for k in range(2)]
             part, held = call(add_kernel, (shape(slab, F32), shape(slab, BF16)))(
-                part, after(other, to_far, to_near, *number)
+                part, after(other, from_far, from_near, *number)
             )
             other = routed(held, "bead", lambda i: i ^ 1)
-            to_far, to_near = after(to_far, held), after(to_near, held)
-        from_far = far_pair(to_far)
-        from_near = near_pair(to_near)
         start = after(position, held) if step == 0 else position
         cols, waves, turned = own_call(start, species, projection, phase_shift)
         if step == 0:
             part, held = call(add_kernel, (shape(slab, F32), shape(slab, BF16)))(
-                part, after(other, cols, from_far, from_near)
+                part, after(other, cols)
             )
             other = routed(held, "bead", lambda i: i ^ 3)
+            number.append(count(2, after(neighbours, held)))
             state = weigh_call(
                 after(position, held), from_near, from_far, cols, projection, *number
             )
             ghost_cols, weight, weight_turned, ghost_waves = state
             held = call(add_kernel, (shape(slab, BF16),))(part, after(other, *state))[0]
             pieces = [held] + [routed(held, "dom", lambda i: (i - 4 * k) % 16) for k in (1, 2, 3)]
-            above = passed_along(after(position, held), "bead", -1)
+            one_bead = even_bead(after(position, held))
             sines, low = describe_call(after(weight_turned, held), waves, ghost_waves, turned)
             half = call(ring_kernel, shape((features, features), BF16))(
-                pieces[0], *[after(piece, low, above) for piece in pieces[1:]]
+                pieces[0], *[after(piece, low, one_bead) for piece in pieces[1:]]
             )
             other_half = near_pair(half)
-            below = passed_along(after(position, half), "bead", 1)
+            other_bead = odd_bead(after(position, half))
         else:
-            above = passed_along(after(position, cols, from_far, from_near), "bead", -1)
-            ghost_cols, weight, weight_turned, ghost_waves = weigh_call(
-                position, from_near, from_far, cols, projection, *number
+            other_bead = odd_bead(after(position, cols, from_far, from_near))
+            ghost_cols, weight, ghost_waves, sines, low = weigh_describe_call(
+                position, from_near, from_far, cols, projection, waves, turned, *number
             )
-            sines, low = describe_call(weight_turned, waves, ghost_waves, turned)
-            below = passed_along(after(position, low), "bead", 1)
+            one_bead = even_bead(after(position, low, other_bead))
         grad, spread, centre, near_force, far_force = ghost_force_call(
             low,
             half,
@@ -693,8 +732,8 @@
             send_lists,
             position,
             velocity,
-            below,
-            above,
+            other_bead,
+            one_bead,
             species,
         )
         if not last:

time: 71.8 us -> 68 us (0.947)
  the two profiles are of different devices: /device:TPU:6 before, /device:TPU:2 now
where the time goes in v6:
time: 68 us; the launch traced here: 67.9 us
  Pallas kernels  31.1 us (46%)
  starting transfers between devices  27.8 us (41%)
  waiting for transfers between devices  5.38 us (8%)
  local copies, waits for them, and re-layouts  1.55 us (2%)
  between operations  0.97 us (1%)
  other arithmetic  0.69 us (1%)
    ppermute x18, starting transfers between devices, routed(): lax.ppermute(block, axis, [(source(i), i) for i in range(lax.axis_size(ax...  24.7 us
    pallas_call x2, Pallas kernels, shards(): own_force_call(grad, spread, sines, waves, weight, cols, position, centre...  7.04 us
    pallas_call x2, Pallas kernels, shards(): cols, waves, turned = own_call(start, species, projection, phase_shift)  5.72 us
    pallas_call x2, Pallas kernels, shards(): ghost_force_call(low, half, other_half, cols, turned, weight, ghost_waves...  5.6 us
    ppermute x18, waiting for transfers between devices, routed(): lax.ppermute(block, axis, [(source(i), i) for i in range(lax.axis_size(ax...  5.38 us
    pallas_call x3, Pallas kernels, count(): call(functools.partial(count_kernel, part), shape((ghosts, own), F32), [p...  3.22 us
    pallas_call x1, Pallas kernels, shards(): weigh_describe_call(position, from_near, from_far, cols, projection, wave...  3.19 us
    ppermute x1, starting transfers between devices, across(): return lax.ppermute(block, ('dom', 'bead'), route)  3.09 us
  transfers between devices with their start and end apart: 19, of which 7 were waited for; matrix products, arithmetic and copies ran while one was open for 0% of the time, Pallas kernels for 42%

profile of v6, /device:TPU:2, one launch (start us, length us, event | category | flops | bytes accessed | tf_op | source)
XLA Modules:
  0.0 67.9 jit_solution(13474359550358281467)
XLA Ops:
  0.7 0.9 %copy-done = bf16[2,250,512]{2,0,1:T(2,128)(2,1)S(1)} copy-done((bf16[2,250,512]{2,0,1:T(2,128)(2,1)S(1)}, bf16[2,250,512]{2,0,1:T(2,128)(2,1)}, u32[]{:S(2)}) %copy-start) | copy-done | bytes 512024
  2.3 0.7 %convert_multiply_fusion = f32[1,250]{1,0:T(1,128)S(1)} fusion(bf16[2,250]{1,0:T(2,128)(2,1)} %param.19, s32[]{:T(128)S(6)} %select_n.21), kind=kLoop, calls=%fused_computation.6 | loop fusion | flops 500 | bytes 1504 | tf_op jit(solution)/shard_map/mul | solution.py:522
  3.4 3.1 %collective-permute-start = (bf16[128,384]{1,0:T(8,128)(2,1)S(1)}, bf16[128,384]{1,0:T(8,128)(2,1)S(1)}, u32[]{:S(2)}, u32[]{:S(2)}) collective-permute-start(bf16[128,384]{1,0:T(8,128)(2,1)S(1)} %get-tuple-element.60), channel_id=1, source_target_pairs={{20,0},{21,1},{22,2},{23,3},{16,4},{17,5},{18,6},{19,7},{28,8},{29... | collective-permute-start | bytes 294920 | tf_op jit(solution)/shard_map/ppermute | solution.py:500
  7.0 2.9 %collective-permute-start.1 = (f32[4,128]{1,0:T(4,128)S(1)}, f32[4,128]{1,0:T(4,128)S(1)}, u32[]{:S(2)}, u32[]{:S(2)}) collective-permute-start(f32[4,128]{1,0:T(4,128)S(1)} %get-tuple-element.62), channel_id=1, source_target_pairs={{120,0},{16,8},{8,16},{32,24},{24,32},{48,40},{40,48},{64,56},{56,... | collective-permute-start | bytes 6152 | tf_op jit(solution)/shard_map/ppermute | solution.py:486
  9.8 1.1 %shard_map.115.rest_0_ = f32[256,512]{1,0:T(8,128)S(1)} custom-call(s32[32,512]{1,0:T(8,128)S(1)} %copy-done.2, s32[1,512]{1,0:T(1,128)S(1)} %bitcast.33), custom_call_target="tpu_custom_call" | custom-call | tf_op jit(solution)/shard_map/pallas_call | solution.py:586
  10.9 1.1 %shard_map.116.rest_1_ = f32[256,512]{1,0:T(8,128)S(1)} custom-call(s32[32,512]{1,0:T(8,128)S(1)} %copy-done.2, s32[1,512]{1,0:T(1,128)S(1)} %bitcast.34), custom_call_target="tpu_custom_call" | custom-call | tf_op jit(solution)/shard_map/pallas_call | solution.py:586
  12.8 2.9 %shard_map.118 = (f32[512,128]{1,0:T(8,128)S(1)}, bf16[512,2048]{1,0:T(8,128)(2,1)S(1)}, f32[512,2048]{1,0:T(8,128)S(1)}) custom-call(f32[3,1,512]{2,1,0:T(1,128)S(1)} %bitcast.21, s32[1,512]{1,0:T(1,128)S(1)} %bitcast.29, f32[3,2,512]{2,1,0:T(2,128)S(1)} %bitcast.12, f32[2,512]{1,0:T(2,128)S(1)} %copy-done.6), custom_call_target="tpu_custom_call" | custom-call | tf_op jit(solution)/shard_map/pallas_call | solution.py:680
  15.7 1.6 %collective-permute-done.3.other_ref = bf16[128,384]{1,0:T(8,128)(2,1)S(1)} collective-permute-done((bf16[128,384]{1,0:T(8,128)(2,1)S(1)}, bf16[128,384]{1,0:T(8,128)(2,1)S(1)}, u32[]{:S(2)}, u32[]{:S(2)}) %collective-permute-start.3) | collective-permute-done | bytes 98336 | tf_op jit(solution)/shard_map/ppermute | solution.py:486
  17.4 1.6 %collective-permute-start.4 = (bf16[128,384]{1,0:T(8,128)(2,1)S(1)}, bf16[128,384]{1,0:T(8,128)(2,1)S(1)}, u32[]{:S(2)}, u32[]{:S(2)}) collective-permute-start(bf16[128,384]{1,0:T(8,128)(2,1)S(1)} %get-tuple-element.71), channel_id=1, source_target_pairs={{3,0},{2,1},{1,2},{0,3},{7,4},{6,5},{5,6},{4,7},{11,8},{10,9},{9,1... | collective-permute-start | bytes 294920 | tf_op jit(solution)/shard_map/ppermute | solution.py:486
  18.9 1.1 %shard_map.120.rest_2_ = f32[256,512]{1,0:T(8,128)S(1)} custom-call(s32[32,512]{1,0:T(8,128)S(1)} %copy-done.2, s32[1,512]{1,0:T(1,128)S(1)} %bitcast.35), custom_call_target="tpu_custom_call" | custom-call | tf_op jit(solution)/shard_map/pallas_call | solution.py:586
  20.0 1.7 %shard_map.121 = (f32[256,128]{1,0:T(8,128)S(1)}, f32[768,512]{1,0:T(8,128)S(1)}, bf16[512,768]{1,0:T(8,128)(2,1)S(1)}, bf16[256,2048]{1,0:T(8,128)(2,1)S(1)}) custom-call(f32[3,1,512]{2,1,0:T(1,128)S(1)} %bitcast.22, f32[4,128]{1,0:T(4,128)S(1)} %collective-permute-done.2.near_ref, f32[4,128]{1,0:T(4,128)S(1)} %collective-permute-done.1.far_ref, ...), custom_call_target="tpu_custom_call" | custom-call | tf_op jit(solution)/shard_map/pallas_call | solution.py:687
  22.1 2.5 %collective-permute-start.8 = (bf16[128,384]{1,0:T(8,128)(2,1)S(1)}, bf16[128,384]{1,0:T(8,128)(2,1)S(1)}, u32[]{:S(2)}, u32[]{:S(2)}) collective-permute-start(bf16[128,384]{1,0:T(8,128)(2,1)S(1)} %shard_map.122.refs_0_), channel_id=1, source_target_pairs={{32,0},{40,8},{48,16},{56,24},{64,32},{72,40},{80,48},{88,56},{96,... | collective-permute-start | bytes 294920 | tf_op jit(solution)/shard_map/ppermute | solution.py:486
  24.6 1.3 %collective-permute-start.5 = (bf16[128,384]{1,0:T(8,128)(2,1)S(1)}, bf16[128,384]{1,0:T(8,128)(2,1)S(1)}, u32[]{:S(2)}, u32[]{:S(2)}) collective-permute-start(bf16[128,384]{1,0:T(8,128)(2,1)S(1)} %shard_map.122.refs_0_), channel_id=1, source_target_pairs={{96,0},{104,8},{112,16},{120,24},{0,32},{8,40},{16,48},{24,56},{32... | collective-permute-start | bytes 294920 | tf_op jit(solution)/shard_map/ppermute | solution.py:486
  25.8 1.7 %collective-permute-start.6 = (f32[3,1,512]{2,1,0:T(1,128)S(1)}, f32[3,1,512]{2,1,0:T(1,128)S(1)}, u32[]{:S(2)}, u32[]{:S(2)}) collective-permute-start(f32[3,1,512]{2,1,0:T(1,128)S(1)} %bitcast.23), channel_id=1, source_target_pairs={{1,0},{0,1},{3,2},{2,3},{5,4},{4,5},{7,6},{6,7},{9,8},{8,9},{11,10... | collective-permute-start | bytes 18440 | tf_op jit(solution)/shard_map/ppermute | solution.py:486
  27.6 1.9 %shard_map.123 = (f32[512,1024]{1,0:T(8,128)S(1)}, bf16[512,512]{1,0:T(8,128)(2,1)S(1)}) custom-call(bf16[512,768]{1,0:T(8,128)(2,1)S(1)} %get-tuple-element.80.weight_turned, bf16[512,2048]{1,0:T(8,128)(2,1)S(1)} %get-tuple-element.81.own_waves.waves, bf16[256,2048]{1,0:T(8,128)(2,1)S(1)} %get-tuple-element.78.ghost_waves.waves, ...), custom_call_target="tpu_custom_call" | custom-call | tf_op jit(solution)/shard_map/pallas_call | solution.py:694
  29.5 1.3 %collective-permute-done.7.refs_2_ = bf16[128,384]{1,0:T(8,128)(2,1)S(1)} collective-permute-done((bf16[128,384]{1,0:T(8,128)(2,1)S(1)}, bf16[128,384]{1,0:T(8,128)(2,1)S(1)}, u32[]{:S(2)}, u32[]{:S(2)}) %collective-permute-start.7) | collective-permute-done | bytes 98336 | tf_op jit(solution)/shard_map/ppermute | solution.py:486
  30.8 0.7 collective-permute-done.5.refs_1_
  31.7 1.6 %collective-permute-start.12 = (f32[3,1,512]{2,1,0:T(1,128)S(1)}, f32[3,1,512]{2,1,0:T(1,128)S(1)}, u32[]{:S(2)}, u32[]{:S(2)}) collective-permute-start(f32[3,1,512]{2,1,0:T(1,128)S(1)} %bitcast.24), channel_id=1, source_target_pairs={{7,0},{2,1},{1,2},{4,3},{3,4},{6,5},{5,6},{0,7},{15,8},{10,9},{9,1... | collective-permute-start | bytes 18440 | tf_op jit(solution)/shard_map/ppermute | solution.py:486
  33.6 2.8 %shard_map.125 = (f32[512,512]{1,0:T(8,128)S(1)}, bf16[512,2048]{1,0:T(8,128)(2,1)S(1)}, f32[3,512]{1,0:T(4,128)S(1)}, f32[3,128]{1,0:T(4,128)S(1)}, f32[3,128]{1,0:T(4,128)S(1)}) custom-call(bf16[512,512]{1,0:T(8,128)(2,1)S(1)} %get-tuple-element.83.low, bf16[512,512]{1,0:T(8,128)(2,1)S(1)} %shard_map.124.half_ref, ...), custom_call_target="tpu_custom_call" | custom-call | tf_op jit(solution)/shard_map/pallas_call | solution.py:706
  36.6 1.6 %collective-permute-start.11 = (f32[3,128]{1,0:T(4,128)S(1)}, f32[3,128]{1,0:T(4,128)S(1)}, u32[]{:S(2)}, u32[]{:S(2)}) collective-permute-start(f32[3,128]{1,0:T(4,128)S(1)} %get-tuple-element.93), channel_id=1, source_target_pairs={{120,0},{16,8},{8,16},{32,24},{24,32},{48,40},{40,48},{64,56},{56,... | collective-permute-start | bytes 4616 | tf_op jit(solution)/shard_map/ppermute | solution.py:486
  38.2 3.5 %shard_map.126.force_ref = f32[3,512]{1,0:T(4,128)S(1)} custom-call(f32[512,512]{1,0:T(8,128)S(1)} %get-tuple-element.88.grad, bf16[512,2048]{1,0:T(8,128)(2,1)S(1)} %get-tuple-element.89.spread, f32[512,1024]{1,0:T(8,128)S(1)} %get-tuple-element.90.sines, bf16[512,2048]{1,0:T(8,128)(2,1)S(1)} %get-tuple-element.81.own_waves.waves, ...), custom_call_target="tpu_custom_call" | custom-call | tf_op jit(solution)/shard_map/pallas_call | solution.py:720
  41.8 0.9 %shard_map.127 = (f32[3,1,512]{2,1,0:T(1,128)S(1)}, f32[3,1,512]{2,1,0:T(1,128)S(1)}, f32[4,128]{1,0:T(4,128)S(1)}, f32[4,128]{1,0:T(4,128)S(1)}) custom-call(f32[3,512]{1,0:T(4,128)S(1)} %shard_map.126.force_ref, f32[3,128]{1,0:T(4,128)S(1)} %collective-permute-done.10.near_back_ref, f32[3,128]{1,0:T(4,128)S(1)} %collective-permute-done.11.far_back_ref, ...), custom_call_target="tpu_custom_call" | custom-call | tf_op jit(solution)/shard_map/pallas_call | solution.py:724
  42.8 2.5 %collective-permute-start.14 = (f32[4,128]{1,0:T(4,128)S(1)}, f32[4,128]{1,0:T(4,128)S(1)}, u32[]{:S(2)}, u32[]{:S(2)}) collective-permute-start(f32[4,128]{1,0:T(4,128)S(1)} %get-tuple-element.97), channel_id=1, source_target_pairs={{120,0},{16,8},{8,16},{32,24},{24,32},{48,40},{40,48},{64,56},{56,... | collective-permute-start | bytes 6152 | tf_op jit(solution)/shard_map/ppermute | solution.py:486
  45.3 2.9 %shard_map.128 = (f32[512,128]{1,0:T(8,128)S(1)}, bf16[512,2048]{1,0:T(8,128)(2,1)S(1)}, f32[512,2048]{1,0:T(8,128)S(1)}) custom-call(f32[3,1,512]{2,1,0:T(1,128)S(1)} %get-tuple-element.113.position_ref, s32[1,512]{1,0:T(1,128)S(1)} %bitcast.31, f32[3,2,512]{2,1,0:T(2,128)S(1)} %bitcast.16, f32[2,512]{1,0:T(2,128)S(1)} %copy-done.6), custom_call_target="tpu_custom_call" | custom-call | tf_op jit(solution)/shard_map/pallas_call | solution.py:680
  48.2 1.8 %collective-permute-start.17 = (f32[3,1,512]{2,1,0:T(1,128)S(1)}, f32[3,1,512]{2,1,0:T(1,128)S(1)}, u32[]{:S(2)}, u32[]{:S(2)}) collective-permute-start(f32[3,1,512]{2,1,0:T(1,128)S(1)} %get-tuple-element.113.position_ref), channel_id=1, source_target_pairs={{7,0},{2,1},{1,2},{4,3},{3,4},{6,5},{5,6},{0,7},{15,8},{10,9},{9,1... | collective-permute-start | bytes 18440 | tf_op jit(solution)/shard_map/ppermute | solution.py:486
  50.0 3.2 %shard_map.129 = (f32[256,128]{1,0:T(8,128)S(1)}, f32[768,512]{1,0:T(8,128)S(1)}, bf16[256,2048]{1,0:T(8,128)(2,1)S(1)}, f32[512,1024]{1,0:T(8,128)S(1)}, bf16[512,512]{1,0:T(8,128)(2,1)S(1)}) custom-call(f32[3,1,512]{2,1,0:T(1,128)S(1)} %get-tuple-element.113.position_ref, f32[4,128]{1,0:T(4,128)S(1)} %collective-permute-done.13.near_ref, ...), custom_call_target="tpu_custom_call" | custom-call | tf_op jit(solution)/shard_map/pallas_call | solution.py:702
  53.2 5.3 %collective-permute-start.18 = (f32[3,1,512]{2,1,0:T(1,128)S(1)}, f32[3,1,512]{2,1,0:T(1,128)S(1)}, u32[]{:S(2)}, u32[]{:S(2)}) collective-permute-start(f32[3,1,512]{2,1,0:T(1,128)S(1)} %get-tuple-element.113.position_ref), channel_id=1, source_target_pairs={{1,0},{0,1},{3,2},{2,3},{5,4},{4,5},{7,6},{6,7},{9,8},{8,9},{11,10... | collective-permute-start | bytes 18440 | tf_op jit(solution)/shard_map/ppermute | solution.py:486
  58.5 2.8 %shard_map.130 = (f32[512,512]{1,0:T(8,128)S(1)}, bf16[512,2048]{1,0:T(8,128)(2,1)S(1)}, f32[3,512]{1,0:T(4,128)S(1)}, f32[3,128]{1,0:T(4,128)S(1)}, f32[3,128]{1,0:T(4,128)S(1)}) custom-call(bf16[512,512]{1,0:T(8,128)(2,1)S(1)} %get-tuple-element.101.low, bf16[512,512]{1,0:T(8,128)(2,1)S(1)} %shard_map.124.half_ref, ...), custom_call_target="tpu_custom_call" | custom-call | tf_op jit(solution)/shard_map/pallas_call | solution.py:706
  61.4 1.0 %collective-permute-start.16 = (f32[3,128]{1,0:T(4,128)S(1)}, f32[3,128]{1,0:T(4,128)S(1)}, u32[]{:S(2)}, u32[]{:S(2)}) collective-permute-start(f32[3,128]{1,0:T(4,128)S(1)} %get-tuple-element.110), channel_id=1, source_target_pairs={{120,0},{16,8},{8,16},{32,24},{24,32},{48,40},{40,48},{64,56},{56,... | collective-permute-start | bytes 4616 | tf_op jit(solution)/shard_map/ppermute | solution.py:486
  62.4 3.5 %shard_map.131.force_ref = f32[3,512]{1,0:T(4,128)S(1)} custom-call(f32[512,512]{1,0:T(8,128)S(1)} %get-tuple-element.105.grad, bf16[512,2048]{1,0:T(8,128)(2,1)S(1)} %get-tuple-element.106.spread, f32[512,1024]{1,0:T(8,128)S(1)} %get-tuple-element.107.sines, bf16[512,2048]{1,0:T(8,128)(2,1)S(1)} %get-tuple-element.99.own_waves.waves, ...), custom_call_target="tpu_custom_call" | custom-call | tf_op jit(solution)/shard_map/pallas_call | solution.py:720
  65.9 1.0 %collective-permute-done.16.far_back_ref = f32[3,128]{1,0:T(4,128)S(1)} collective-permute-done((f32[3,128]{1,0:T(4,128)S(1)}, f32[3,128]{1,0:T(4,128)S(1)}, u32[]{:S(2)}, u32[]{:S(2)}) %collective-permute-start.16) | collective-permute-done | bytes 1568 | tf_op jit(solution)/shard_map/ppermute | solution.py:486
  66.9 1.0 %shard_map.132 = (f32[3,1,512]{2,1,0:T(1,128)}, f32[3,1,512]{2,1,0:T(1,128)}) custom-call(f32[3,512]{1,0:T(4,128)S(1)} %shard_map.131.force_ref, f32[3,128]{1,0:T(4,128)S(1)} %collective-permute-done.15.near_back_ref, f32[3,128]{1,0:T(4,128)S(1)} %collective-permute-done.16.far_back_ref, s32[2,128]{1,0:T(2,128)S(1)} %copy-done.7, ...), custom_call_target="tpu_custom_call" | custom-call | tf_op jit(solution)/shard_map/pallas_call | solution.py:724
  (48 shorter events, 3.7 us)
Async XLA Ops:
  0.6 1.0 %copy-start = (bf16[2,250,512]{2,0,1:T(2,128)(2,1)S(1)}, bf16[2,250,512]{2,0,1:T(2,128)(2,1)}, u32[]{:S(2)}) copy-start(bf16[2,250,512]{2,0,1:T(2,128)(2,1)} %param.18) | copy-start | bytes 1536004
  0.6 5.9 %copy-start.3 = (f32[1,3,512]{2,0,1:T(1,128)S(1)}, f32[1,3,512]{2,0,1:T(1,128)}, u32[]{:S(2)}) copy-start(f32[1,3,512]{2,0,1:T(1,128)} %param.10) | copy-start | bytes 18436
  0.7 5.9 %copy-start.4 = (s32[512]{0:T(512)S(1)}, s32[512]{0:T(512)}, u32[]{:S(2)}) copy-start(s32[512]{0:T(512)} %param.12) | copy-start | bytes 6148
  0.7 5.9 %copy-start.7 = (s32[2,128]{1,0:T(2,128)S(1)}, s32[2,128]{1,0:T(2,128)}, u32[]{:S(2)}) copy-start(s32[2,128]{1,0:T(2,128)} %lists_ref.5) | copy-start | bytes 3076
  0.7 9.2 %copy-start.5 = (s32[512]{0:T(512)S(1)}, s32[512]{0:T(512)}, u32[]{:S(2)}) copy-start(s32[512]{0:T(512)} %param.14) | copy-start | bytes 6148
  0.7 9.2 %copy-start.2 = (s32[32,512]{1,0:T(8,128)S(1)}, s32[32,512]{1,0:T(8,128)}, u32[]{:S(2)}) copy-start(s32[32,512]{1,0:T(8,128)} %neighbours_ref.4) | copy-start | bytes 196612
  0.7 12.1 %copy-start.1 = (f32[2,3,512]{2,0,1:T(2,128)S(1)}, f32[2,3,512]{2,0,1:T(2,128)}, u32[]{:S(2)}) copy-start(f32[2,3,512]{2,0,1:T(2,128)} %param.16) | copy-start | bytes 36868
  0.7 12.1 %copy-start.6 = (f32[2,512]{1,0:T(2,128)S(1)}, f32[2,512]{1,0:T(2,128)}, u32[]{:S(2)}) copy-start(f32[2,512]{1,0:T(2,128)} %shift_ref.3) | copy-start | bytes 12292
  3.4 8.8 %collective-permute-start = (bf16[128,384]{1,0:T(8,128)(2,1)S(1)}, bf16[128,384]{1,0:T(8,128)(2,1)S(1)}, u32[]{:S(2)}, u32[]{:S(2)}) collective-permute-start(bf16[128,384]{1,0:T(8,128)(2,1)S(1)} %get-tuple-element.60), channel_id=1, source_target_pairs={{20,0},{21,1},{22,2},{23,3},{16,4},{17,5},{18,6},{19,7},{28,8},{29... | collective-permute-start | bytes 294920 | tf_op jit(solution)/shard_map/ppermute | solution.py:500
  7.0 5.2 %collective-permute-start.1 = (f32[4,128]{1,0:T(4,128)S(1)}, f32[4,128]{1,0:T(4,128)S(1)}, u32[]{:S(2)}, u32[]{:S(2)}) collective-permute-start(f32[4,128]{1,0:T(4,128)S(1)} %get-tuple-element.62), channel_id=1, source_target_pairs={{120,0},{16,8},{8,16},{32,24},{24,32},{48,40},{40,48},{64,56},{56,... | collective-permute-start | bytes 6152 | tf_op jit(solution)/shard_map/ppermute | solution.py:486
  9.8 2.4 %collective-permute-start.2 = (f32[4,128]{1,0:T(4,128)S(1)}, f32[4,128]{1,0:T(4,128)S(1)}, u32[]{:S(2)}, u32[]{:S(2)}) collective-permute-start(f32[4,128]{1,0:T(4,128)S(1)} %get-tuple-element.64), channel_id=1, source_target_pairs={{8,0},{0,8},{24,16},{16,24},{40,32},{32,40},{56,48},{48,56},{72,64... | collective-permute-start | bytes 6152 | tf_op jit(solution)/shard_map/ppermute | solution.py:486
  12.2 5.1 %collective-permute-start.3 = (bf16[128,384]{1,0:T(8,128)(2,1)S(1)}, bf16[128,384]{1,0:T(8,128)(2,1)S(1)}, u32[]{:S(2)}, u32[]{:S(2)}) collective-permute-start(bf16[128,384]{1,0:T(8,128)(2,1)S(1)} %get-tuple-element.67), channel_id=1, source_target_pairs={{1,0},{0,1},{3,2},{2,3},{5,4},{4,5},{7,6},{6,7},{9,8},{8,9},{11,10... | collective-permute-start | bytes 294920 | tf_op jit(solution)/shard_map/ppermute | solution.py:486
  17.4 4.7 %collective-permute-start.4 = (bf16[128,384]{1,0:T(8,128)(2,1)S(1)}, bf16[128,384]{1,0:T(8,128)(2,1)S(1)}, u32[]{:S(2)}, u32[]{:S(2)}) collective-permute-start(bf16[128,384]{1,0:T(8,128)(2,1)S(1)} %get-tuple-element.71), channel_id=1, source_target_pairs={{3,0},{2,1},{1,2},{0,3},{7,4},{6,5},{5,6},{4,7},{11,8},{10,9},{9,1... | collective-permute-start | bytes 294920 | tf_op jit(solution)/shard_map/ppermute | solution.py:486
  22.1 7.4 %collective-permute-start.8 = (bf16[128,384]{1,0:T(8,128)(2,1)S(1)}, bf16[128,384]{1,0:T(8,128)(2,1)S(1)}, u32[]{:S(2)}, u32[]{:S(2)}) collective-permute-start(bf16[128,384]{1,0:T(8,128)(2,1)S(1)} %shard_map.122.refs_0_), channel_id=1, source_target_pairs={{32,0},{40,8},{48,16},{56,24},{64,32},{72,40},{80,48},{88,56},{96,... | collective-permute-start | bytes 294920 | tf_op jit(solution)/shard_map/ppermute | solution.py:486
  24.6 6.2 %collective-permute-start.7 = (bf16[128,384]{1,0:T(8,128)(2,1)S(1)}, bf16[128,384]{1,0:T(8,128)(2,1)S(1)}, u32[]{:S(2)}, u32[]{:S(2)}) collective-permute-start(bf16[128,384]{1,0:T(8,128)(2,1)S(1)} %shard_map.122.refs_0_), channel_id=1, source_target_pairs={{64,0},{72,8},{80,16},{88,24},{96,32},{104,40},{112,48},{120,56},{... | collective-permute-start | bytes 294920 | tf_op jit(solution)/shard_map/ppermute | solution.py:486
  24.6 6.9 %collective-permute-start.5 = (bf16[128,384]{1,0:T(8,128)(2,1)S(1)}, bf16[128,384]{1,0:T(8,128)(2,1)S(1)}, u32[]{:S(2)}, u32[]{:S(2)}) collective-permute-start(bf16[128,384]{1,0:T(8,128)(2,1)S(1)} %shard_map.122.refs_0_), channel_id=1, source_target_pairs={{96,0},{104,8},{112,16},{120,24},{0,32},{8,40},{16,48},{24,56},{32... | collective-permute-start | bytes 294920 | tf_op jit(solution)/shard_map/ppermute | solution.py:486
  25.8 3.7 %collective-permute-start.6 = (f32[3,1,512]{2,1,0:T(1,128)S(1)}, f32[3,1,512]{2,1,0:T(1,128)S(1)}, u32[]{:S(2)}, u32[]{:S(2)}) collective-permute-start(f32[3,1,512]{2,1,0:T(1,128)S(1)} %bitcast.23), channel_id=1, source_target_pairs={{1,0},{0,1},{3,2},{2,3},{5,4},{4,5},{7,6},{6,7},{9,8},{8,9},{11,10... | collective-permute-start | bytes 18440 | tf_op jit(solution)/shard_map/ppermute | solution.py:486
  31.6 2.0 %collective-permute-start.9 = (bf16[512,512]{1,0:T(8,128)(2,1)S(1)}, bf16[512,512]{1,0:T(8,128)(2,1)S(1)}, u32[]{:S(2)}, u32[]{:S(2)}) collective-permute-start(bf16[512,512]{1,0:T(8,128)(2,1)S(1)} %shard_map.124.half_ref), channel_id=1, source_target_pairs={{8,0},{0,8},{24,16},{16,24},{40,32},{32,40},{56,48},{48,56},{72,64... | collective-permute-start | bytes 1572872 | tf_op jit(solution)/shard_map/ppermute | solution.py:486
  31.7 10.0 %collective-permute-start.12 = (f32[3,1,512]{2,1,0:T(1,128)S(1)}, f32[3,1,512]{2,1,0:T(1,128)S(1)}, u32[]{:S(2)}, u32[]{:S(2)}) collective-permute-start(f32[3,1,512]{2,1,0:T(1,128)S(1)} %bitcast.24), channel_id=1, source_target_pairs={{7,0},{2,1},{1,2},{4,3},{3,4},{6,5},{5,6},{0,7},{15,8},{10,9},{9,1... | collective-permute-start | bytes 18440 | tf_op jit(solution)/shard_map/ppermute | solution.py:486
  36.4 5.4 %collective-permute-start.10 = (f32[3,128]{1,0:T(4,128)S(1)}, f32[3,128]{1,0:T(4,128)S(1)}, u32[]{:S(2)}, u32[]{:S(2)}) collective-permute-start(f32[3,128]{1,0:T(4,128)S(1)} %get-tuple-element.92), channel_id=1, source_target_pairs={{8,0},{0,8},{24,16},{16,24},{40,32},{32,40},{56,48},{48,56},{72,64... | collective-permute-start | bytes 4616 | tf_op jit(solution)/shard_map/ppermute | solution.py:486
  36.6 5.2 %collective-permute-start.11 = (f32[3,128]{1,0:T(4,128)S(1)}, f32[3,128]{1,0:T(4,128)S(1)}, u32[]{:S(2)}, u32[]{:S(2)}) collective-permute-start(f32[3,128]{1,0:T(4,128)S(1)} %get-tuple-element.93), channel_id=1, source_target_pairs={{120,0},{16,8},{8,16},{32,24},{24,32},{48,40},{40,48},{64,56},{56,... | collective-permute-start | bytes 4616 | tf_op jit(solution)/shard_map/ppermute | solution.py:486
  38.2 3.5 %copy-start.8 = (f32[1,3,512]{2,0,1:T(1,128)S(1)}, f32[1,3,512]{2,0,1:T(1,128)}, u32[]{:S(2)}) copy-start(f32[1,3,512]{2,0,1:T(1,128)} %param.11) | copy-start | bytes 18436
  42.7 5.5 %collective-permute-start.13 = (f32[4,128]{1,0:T(4,128)S(1)}, f32[4,128]{1,0:T(4,128)S(1)}, u32[]{:S(2)}, u32[]{:S(2)}) collective-permute-start(f32[4,128]{1,0:T(4,128)S(1)} %get-tuple-element.96), channel_id=1, source_target_pairs={{8,0},{0,8},{24,16},{16,24},{40,32},{32,40},{56,48},{48,56},{72,64... | collective-permute-start | bytes 6152 | tf_op jit(solution)/shard_map/ppermute | solution.py:486
  42.8 5.4 %collective-permute-start.14 = (f32[4,128]{1,0:T(4,128)S(1)}, f32[4,128]{1,0:T(4,128)S(1)}, u32[]{:S(2)}, u32[]{:S(2)}) collective-permute-start(f32[4,128]{1,0:T(4,128)S(1)} %get-tuple-element.97), channel_id=1, source_target_pairs={{120,0},{16,8},{8,16},{32,24},{24,32},{48,40},{40,48},{64,56},{56,... | collective-permute-start | bytes 6152 | tf_op jit(solution)/shard_map/ppermute | solution.py:486
  48.2 5.0 %collective-permute-start.17 = (f32[3,1,512]{2,1,0:T(1,128)S(1)}, f32[3,1,512]{2,1,0:T(1,128)S(1)}, u32[]{:S(2)}, u32[]{:S(2)}) collective-permute-start(f32[3,1,512]{2,1,0:T(1,128)S(1)} %get-tuple-element.113.position_ref), channel_id=1, source_target_pairs={{7,0},{2,1},{1,2},{4,3},{3,4},{6,5},{5,6},{0,7},{15,8},{10,9},{9,1... | collective-permute-start | bytes 18440 | tf_op jit(solution)/shard_map/ppermute | solution.py:486
  53.2 13.6 %collective-permute-start.18 = (f32[3,1,512]{2,1,0:T(1,128)S(1)}, f32[3,1,512]{2,1,0:T(1,128)S(1)}, u32[]{:S(2)}, u32[]{:S(2)}) collective-permute-start(f32[3,1,512]{2,1,0:T(1,128)S(1)} %get-tuple-element.113.position_ref), channel_id=1, source_target_pairs={{1,0},{0,1},{3,2},{2,3},{5,4},{4,5},{7,6},{6,7},{9,8},{8,9},{11,10... | collective-permute-start | bytes 18440 | tf_op jit(solution)/shard_map/ppermute | solution.py:486
  61.3 4.6 %collective-permute-start.15 = (f32[3,128]{1,0:T(4,128)S(1)}, f32[3,128]{1,0:T(4,128)S(1)}, u32[]{:S(2)}, u32[]{:S(2)}) collective-permute-start(f32[3,128]{1,0:T(4,128)S(1)} %get-tuple-element.109), channel_id=1, source_target_pairs={{8,0},{0,8},{24,16},{16,24},{40,32},{32,40},{56,48},{48,56},{72,64... | collective-permute-start | bytes 4616 | tf_op jit(solution)/shard_map/ppermute | solution.py:486
  61.4 5.5 %collective-permute-start.16 = (f32[3,128]{1,0:T(4,128)S(1)}, f32[3,128]{1,0:T(4,128)S(1)}, u32[]{:S(2)}, u32[]{:S(2)}) collective-permute-start(f32[3,128]{1,0:T(4,128)S(1)} %get-tuple-element.110), channel_id=1, source_target_pairs={{120,0},{16,8},{8,16},{32,24},{24,32},{48,40},{40,48},{64,56},{56,... | collective-permute-start | bytes 4616 | tf_op jit(solution)/shard_map/ppermute | solution.py:486

commit v7 on v6

--- a/solution.py
+++ b/solution.py
@@ -698,11 +698,11 @@
             other_half = near_pair(half)
             other_bead = odd_bead(after(position, half))
         else:
-            other_bead = odd_bead(after(position, cols, from_far, from_near))
+            one_bead = even_bead(after(position, cols, from_far, from_near))
             ghost_cols, weight, ghost_waves, sines, low = weigh_describe_call(
                 position, from_near, from_far, cols, projection, waves, turned, *number
             )
-            one_bead = even_bead(after(position, low, other_bead))
+            other_bead = odd_bead(after(position, low))
         grad, spread, centre, near_force, far_force = ghost_force_call(
             low,
             half,

time: 68 us -> 66.4 us (0.976)
  the two profiles are of different devices: /device:TPU:2 before, /device:TPU:6 now
where the time goes in v7:
time: 66.4 us; the launch traced here: 66.1 us
  Pallas kernels  31.1 us (47%)
  starting transfers between devices  21.7 us (33%)
  waiting for transfers between devices  9.76 us (15%)
  local copies, waits for them, and re-layouts  1.55 us (2%)
  between operations  0.94 us (1%)
  other arithmetic  0.69 us (1%)
    ppermute x18, starting transfers between devices, routed(): lax.ppermute(block, axis, [(source(i), i) for i in range(lax.axis_size(ax...  18.6 us
    ppermute x18, waiting for transfers between devices, routed(): lax.ppermute(block, axis, [(source(i), i) for i in range(lax.axis_size(ax...  9.76 us
    pallas_call x2, Pallas kernels, shards(): own_force_call(grad, spread, sines, waves, weight, cols, position, centre...  7.05 us
    pallas_call x2, Pallas kernels, shards(): cols, waves, turned = own_call(start, species, projection, phase_shift)  5.72 us
    pallas_call x2, Pallas kernels, shards(): ghost_force_call(low, half, other_half, cols, turned, weight, ghost_waves...  5.6 us
    pallas_call x3, Pallas kernels, count(): call(functools.partial(count_kernel, part), shape((ghosts, own), F32), [p...  3.22 us
    pallas_call x1, Pallas kernels, shards(): weigh_describe_call(position, from_near, from_far, cols, projection, wave...  3.19 us
    ppermute x1, starting transfers between devices, across(): return lax.ppermute(block, ('dom', 'bead'), route)  3.1 us
  transfers between devices with their start and end apart: 19, of which 9 were waited for; matrix products, arithmetic and copies ran while one was open for 0% of the time, Pallas kernels for 44%

profile of v7, /device:TPU:6, one launch (start us, length us, event | category | flops | bytes accessed | tf_op | source)
XLA Modules:
  0.0 66.1 jit_solution(17155060891081516591)
XLA Ops:
  0.7 0.9 %copy-done = bf16[2,250,512]{2,0,1:T(2,128)(2,1)S(1)} copy-done((bf16[2,250,512]{2,0,1:T(2,128)(2,1)S(1)}, bf16[2,250,512]{2,0,1:T(2,128)(2,1)}, u32[]{:S(2)}) %copy-start) | copy-done | bytes 512024
  2.3 0.7 %convert_multiply_fusion = f32[1,250]{1,0:T(1,128)S(1)} fusion(bf16[2,250]{1,0:T(2,128)(2,1)} %param.19, s32[]{:T(128)S(6)} %select_n.21), kind=kLoop, calls=%fused_computation.6 | loop fusion | flops 500 | bytes 1504 | tf_op jit(solution)/shard_map/mul | solution.py:522
  3.4 3.1 %collective-permute-start = (bf16[128,384]{1,0:T(8,128)(2,1)S(1)}, bf16[128,384]{1,0:T(8,128)(2,1)S(1)}, u32[]{:S(2)}, u32[]{:S(2)}) collective-permute-start(bf16[128,384]{1,0:T(8,128)(2,1)S(1)} %get-tuple-element.60), channel_id=1, source_target_pairs={{20,0},{21,1},{22,2},{23,3},{16,4},{17,5},{18,6},{19,7},{28,8},{29... | collective-permute-start | bytes 294920 | tf_op jit(solution)/shard_map/ppermute | solution.py:500
  7.0 2.9 %collective-permute-start.1 = (f32[4,128]{1,0:T(4,128)S(1)}, f32[4,128]{1,0:T(4,128)S(1)}, u32[]{:S(2)}, u32[]{:S(2)}) collective-permute-start(f32[4,128]{1,0:T(4,128)S(1)} %get-tuple-element.62), channel_id=1, source_target_pairs={{120,0},{16,8},{8,16},{32,24},{24,32},{48,40},{40,48},{64,56},{56,... | collective-permute-start | bytes 6152 | tf_op jit(solution)/shard_map/ppermute | solution.py:486
  9.8 1.1 %shard_map.115.rest_0_ = f32[256,512]{1,0:T(8,128)S(1)} custom-call(s32[32,512]{1,0:T(8,128)S(1)} %copy-done.2, s32[1,512]{1,0:T(1,128)S(1)} %bitcast.33), custom_call_target="tpu_custom_call" | custom-call | tf_op jit(solution)/shard_map/pallas_call | solution.py:586
  10.9 1.1 %shard_map.116.rest_1_ = f32[256,512]{1,0:T(8,128)S(1)} custom-call(s32[32,512]{1,0:T(8,128)S(1)} %copy-done.2, s32[1,512]{1,0:T(1,128)S(1)} %bitcast.34), custom_call_target="tpu_custom_call" | custom-call | tf_op jit(solution)/shard_map/pallas_call | solution.py:586
  12.2 0.9 %collective-permute-start.3 = (bf16[128,384]{1,0:T(8,128)(2,1)S(1)}, bf16[128,384]{1,0:T(8,128)(2,1)S(1)}, u32[]{:S(2)}, u32[]{:S(2)}) collective-permute-start(bf16[128,384]{1,0:T(8,128)(2,1)S(1)} %get-tuple-element.67), channel_id=1, source_target_pairs={{1,0},{0,1},{3,2},{2,3},{5,4},{4,5},{7,6},{6,7},{9,8},{8,9},{11,10... | collective-permute-start | bytes 294920 | tf_op jit(solution)/shard_map/ppermute | solution.py:486
  13.1 2.9 %shard_map.118 = (f32[512,128]{1,0:T(8,128)S(1)}, bf16[512,2048]{1,0:T(8,128)(2,1)S(1)}, f32[512,2048]{1,0:T(8,128)S(1)}) custom-call(f32[3,1,512]{2,1,0:T(1,128)S(1)} %bitcast.21, s32[1,512]{1,0:T(1,128)S(1)} %bitcast.29, f32[3,2,512]{2,1,0:T(2,128)S(1)} %bitcast.12, f32[2,512]{1,0:T(2,128)S(1)} %copy-done.6), custom_call_target="tpu_custom_call" | custom-call | tf_op jit(solution)/shard_map/pallas_call | solution.py:680
  16.0 1.3 %collective-permute-done.3.other_ref = bf16[128,384]{1,0:T(8,128)(2,1)S(1)} collective-permute-done((bf16[128,384]{1,0:T(8,128)(2,1)S(1)}, bf16[128,384]{1,0:T(8,128)(2,1)S(1)}, u32[]{:S(2)}, u32[]{:S(2)}) %collective-permute-start.3) | collective-permute-done | bytes 98336 | tf_op jit(solution)/shard_map/ppermute | solution.py:486
  17.9 1.1 %shard_map.120.rest_2_ = f32[256,512]{1,0:T(8,128)S(1)} custom-call(s32[32,512]{1,0:T(8,128)S(1)} %copy-done.2, s32[1,512]{1,0:T(1,128)S(1)} %bitcast.35), custom_call_target="tpu_custom_call" | custom-call | tf_op jit(solution)/shard_map/pallas_call | solution.py:586
  19.0 1.7 %shard_map.121 = (f32[256,128]{1,0:T(8,128)S(1)}, f32[768,512]{1,0:T(8,128)S(1)}, bf16[512,768]{1,0:T(8,128)(2,1)S(1)}, bf16[256,2048]{1,0:T(8,128)(2,1)S(1)}) custom-call(f32[3,1,512]{2,1,0:T(1,128)S(1)} %bitcast.22, f32[4,128]{1,0:T(4,128)S(1)} %collective-permute-done.2.near_ref, f32[4,128]{1,0:T(4,128)S(1)} %collective-permute-done.1.far_ref, ...), custom_call_target="tpu_custom_call" | custom-call | tf_op jit(solution)/shard_map/pallas_call | solution.py:687
  20.7 2.5 %collective-permute-done.4.other_ref = bf16[128,384]{1,0:T(8,128)(2,1)S(1)} collective-permute-done((bf16[128,384]{1,0:T(8,128)(2,1)S(1)}, bf16[128,384]{1,0:T(8,128)(2,1)S(1)}, u32[]{:S(2)}, u32[]{:S(2)}) %collective-permute-start.4) | collective-permute-done | bytes 98336 | tf_op jit(solution)/shard_map/ppermute | solution.py:486
  23.3 2.5 %collective-permute-start.8 = (bf16[128,384]{1,0:T(8,128)(2,1)S(1)}, bf16[128,384]{1,0:T(8,128)(2,1)S(1)}, u32[]{:S(2)}, u32[]{:S(2)}) collective-permute-start(bf16[128,384]{1,0:T(8,128)(2,1)S(1)} %shard_map.122.refs_0_), channel_id=1, source_target_pairs={{32,0},{40,8},{48,16},{56,24},{64,32},{72,40},{80,48},{88,56},{96,... | collective-permute-start | bytes 294920 | tf_op jit(solution)/shard_map/ppermute | solution.py:486
  25.8 1.3 %collective-permute-start.5 = (bf16[128,384]{1,0:T(8,128)(2,1)S(1)}, bf16[128,384]{1,0:T(8,128)(2,1)S(1)}, u32[]{:S(2)}, u32[]{:S(2)}) collective-permute-start(bf16[128,384]{1,0:T(8,128)(2,1)S(1)} %shard_map.122.refs_0_), channel_id=1, source_target_pairs={{96,0},{104,8},{112,16},{120,24},{0,32},{8,40},{16,48},{24,56},{32... | collective-permute-start | bytes 294920 | tf_op jit(solution)/shard_map/ppermute | solution.py:486
  27.1 1.9 %shard_map.123 = (f32[512,1024]{1,0:T(8,128)S(1)}, bf16[512,512]{1,0:T(8,128)(2,1)S(1)}) custom-call(bf16[512,768]{1,0:T(8,128)(2,1)S(1)} %get-tuple-element.80.weight_turned, bf16[512,2048]{1,0:T(8,128)(2,1)S(1)} %get-tuple-element.81.own_waves.waves, bf16[256,2048]{1,0:T(8,128)(2,1)S(1)} %get-tuple-element.78.ghost_waves.waves, ...), custom_call_target="tpu_custom_call" | custom-call | tf_op jit(solution)/shard_map/pallas_call | solution.py:694
  29.0 1.7 %collective-permute-done.6.other_bead_ref = f32[3,1,512]{2,1,0:T(1,128)S(1)} collective-permute-done((f32[3,1,512]{2,1,0:T(1,128)S(1)}, f32[3,1,512]{2,1,0:T(1,128)S(1)}, u32[]{:S(2)}, u32[]{:S(2)}) %collective-permute-start.6) | collective-permute-done | bytes 6176 | tf_op jit(solution)/shard_map/ppermute | solution.py:486
  30.7 1.3 %collective-permute-done.7.refs_2_ = bf16[128,384]{1,0:T(8,128)(2,1)S(1)} collective-permute-done((bf16[128,384]{1,0:T(8,128)(2,1)S(1)}, bf16[128,384]{1,0:T(8,128)(2,1)S(1)}, u32[]{:S(2)}, u32[]{:S(2)}) %collective-permute-start.7) | collective-permute-done | bytes 98336 | tf_op jit(solution)/shard_map/ppermute | solution.py:486
  32.0 0.7 collective-permute-done.5.refs_1_
  32.9 0.7 %collective-permute-start.12 = (f32[3,1,512]{2,1,0:T(1,128)S(1)}, f32[3,1,512]{2,1,0:T(1,128)S(1)}, u32[]{:S(2)}, u32[]{:S(2)}) collective-permute-start(f32[3,1,512]{2,1,0:T(1,128)S(1)} %bitcast.24), channel_id=1, source_target_pairs={{7,0},{2,1},{1,2},{4,3},{3,4},{6,5},{5,6},{0,7},{15,8},{10,9},{9,1... | collective-permute-start | bytes 18440 | tf_op jit(solution)/shard_map/ppermute | solution.py:486
  33.6 1.2 %collective-permute-done.9.other_ref = bf16[512,512]{1,0:T(8,128)(2,1)S(1)} collective-permute-done((bf16[512,512]{1,0:T(8,128)(2,1)S(1)}, bf16[512,512]{1,0:T(8,128)(2,1)S(1)}, u32[]{:S(2)}, u32[]{:S(2)}) %collective-permute-start.9) | collective-permute-done | bytes 524320 | tf_op jit(solution)/shard_map/ppermute | solution.py:486
  34.8 2.8 %shard_map.125 = (f32[512,512]{1,0:T(8,128)S(1)}, bf16[512,2048]{1,0:T(8,128)(2,1)S(1)}, f32[3,512]{1,0:T(4,128)S(1)}, f32[3,128]{1,0:T(4,128)S(1)}, f32[3,128]{1,0:T(4,128)S(1)}) custom-call(bf16[512,512]{1,0:T(8,128)(2,1)S(1)} %get-tuple-element.83.low, bf16[512,512]{1,0:T(8,128)(2,1)S(1)} %shard_map.124.half_ref, ...), custom_call_target="tpu_custom_call" | custom-call | tf_op jit(solution)/shard_map/pallas_call | solution.py:706
  37.8 1.2 %collective-permute-start.11 = (f32[3,128]{1,0:T(4,128)S(1)}, f32[3,128]{1,0:T(4,128)S(1)}, u32[]{:S(2)}, u32[]{:S(2)}) collective-permute-start(f32[3,128]{1,0:T(4,128)S(1)} %get-tuple-element.93), channel_id=1, source_target_pairs={{120,0},{16,8},{8,16},{32,24},{24,32},{48,40},{40,48},{64,56},{56,... | collective-permute-start | bytes 4616 | tf_op jit(solution)/shard_map/ppermute | solution.py:486
  39.0 3.5 %shard_map.126.force_ref = f32[3,512]{1,0:T(4,128)S(1)} custom-call(f32[512,512]{1,0:T(8,128)S(1)} %get-tuple-element.88.grad, bf16[512,2048]{1,0:T(8,128)(2,1)S(1)} %get-tuple-element.89.spread, f32[512,1024]{1,0:T(8,128)S(1)} %get-tuple-element.90.sines, bf16[512,2048]{1,0:T(8,128)(2,1)S(1)} %get-tuple-element.81.own_waves.waves, ...), custom_call_target="tpu_custom_call" | custom-call | tf_op jit(solution)/shard_map/pallas_call | solution.py:720
  42.9 0.9 %shard_map.127 = (f32[3,1,512]{2,1,0:T(1,128)S(1)}, f32[3,1,512]{2,1,0:T(1,128)S(1)}, f32[4,128]{1,0:T(4,128)S(1)}, f32[4,128]{1,0:T(4,128)S(1)}) custom-call(f32[3,512]{1,0:T(4,128)S(1)} %shard_map.126.force_ref, f32[3,128]{1,0:T(4,128)S(1)} %collective-permute-done.10.near_back_ref, f32[3,128]{1,0:T(4,128)S(1)} %collective-permute-done.11.far_back_ref, ...), custom_call_target="tpu_custom_call" | custom-call | tf_op jit(solution)/shard_map/pallas_call | solution.py:724
  43.9 2.6 %collective-permute-start.14 = (f32[4,128]{1,0:T(4,128)S(1)}, f32[4,128]{1,0:T(4,128)S(1)}, u32[]{:S(2)}, u32[]{:S(2)}) collective-permute-start(f32[4,128]{1,0:T(4,128)S(1)} %get-tuple-element.97), channel_id=1, source_target_pairs={{120,0},{16,8},{8,16},{32,24},{24,32},{48,40},{40,48},{64,56},{56,... | collective-permute-start | bytes 6152 | tf_op jit(solution)/shard_map/ppermute | solution.py:486
  46.5 2.9 %shard_map.128 = (f32[512,128]{1,0:T(8,128)S(1)}, bf16[512,2048]{1,0:T(8,128)(2,1)S(1)}, f32[512,2048]{1,0:T(8,128)S(1)}) custom-call(f32[3,1,512]{2,1,0:T(1,128)S(1)} %get-tuple-element.113.position_ref, s32[1,512]{1,0:T(1,128)S(1)} %bitcast.31, f32[3,2,512]{2,1,0:T(2,128)S(1)} %bitcast.16, f32[2,512]{1,0:T(2,128)S(1)} %copy-done.6), custom_call_target="tpu_custom_call" | custom-call | tf_op jit(solution)/shard_map/pallas_call | solution.py:680
  49.5 3.2 %shard_map.129 = (f32[256,128]{1,0:T(8,128)S(1)}, f32[768,512]{1,0:T(8,128)S(1)}, bf16[256,2048]{1,0:T(8,128)(2,1)S(1)}, f32[512,1024]{1,0:T(8,128)S(1)}, bf16[512,512]{1,0:T(8,128)(2,1)S(1)}) custom-call(f32[3,1,512]{2,1,0:T(1,128)S(1)} %get-tuple-element.113.position_ref, f32[4,128]{1,0:T(4,128)S(1)} %collective-permute-done.13.near_ref, ...), custom_call_target="tpu_custom_call" | custom-call | tf_op jit(solution)/shard_map/pallas_call | solution.py:702
  52.7 4.0 %collective-permute-start.17 = (f32[3,1,512]{2,1,0:T(1,128)S(1)}, f32[3,1,512]{2,1,0:T(1,128)S(1)}, u32[]{:S(2)}, u32[]{:S(2)}) collective-permute-start(f32[3,1,512]{2,1,0:T(1,128)S(1)} %get-tuple-element.113.position_ref), channel_id=1, source_target_pairs={{7,0},{2,1},{1,2},{4,3},{3,4},{6,5},{5,6},{0,7},{15,8},{10,9},{9,1... | collective-permute-start | bytes 18440 | tf_op jit(solution)/shard_map/ppermute | solution.py:486
  56.7 2.8 %shard_map.130 = (f32[512,512]{1,0:T(8,128)S(1)}, bf16[512,2048]{1,0:T(8,128)(2,1)S(1)}, f32[3,512]{1,0:T(4,128)S(1)}, f32[3,128]{1,0:T(4,128)S(1)}, f32[3,128]{1,0:T(4,128)S(1)}) custom-call(bf16[512,512]{1,0:T(8,128)(2,1)S(1)} %get-tuple-element.101.low, bf16[512,512]{1,0:T(8,128)(2,1)S(1)} %shard_map.124.half_ref, ...), custom_call_target="tpu_custom_call" | custom-call | tf_op jit(solution)/shard_map/pallas_call | solution.py:706
  59.6 1.5 %collective-permute-start.16 = (f32[3,128]{1,0:T(4,128)S(1)}, f32[3,128]{1,0:T(4,128)S(1)}, u32[]{:S(2)}, u32[]{:S(2)}) collective-permute-start(f32[3,128]{1,0:T(4,128)S(1)} %get-tuple-element.110), channel_id=1, source_target_pairs={{120,0},{16,8},{8,16},{32,24},{24,32},{48,40},{40,48},{64,56},{56,... | collective-permute-start | bytes 4616 | tf_op jit(solution)/shard_map/ppermute | solution.py:486
  61.1 3.5 %shard_map.131.force_ref = f32[3,512]{1,0:T(4,128)S(1)} custom-call(f32[512,512]{1,0:T(8,128)S(1)} %get-tuple-element.105.grad, bf16[512,2048]{1,0:T(8,128)(2,1)S(1)} %get-tuple-element.106.spread, f32[512,1024]{1,0:T(8,128)S(1)} %get-tuple-element.107.sines, bf16[512,2048]{1,0:T(8,128)(2,1)S(1)} %get-tuple-element.99.own_waves.waves, ...), custom_call_target="tpu_custom_call" | custom-call | tf_op jit(solution)/shard_map/pallas_call | solution.py:720
  65.1 1.0 %shard_map.132 = (f32[3,1,512]{2,1,0:T(1,128)}, f32[3,1,512]{2,1,0:T(1,128)}) custom-call(f32[3,512]{1,0:T(4,128)S(1)} %shard_map.131.force_ref, f32[3,128]{1,0:T(4,128)S(1)} %collective-permute-done.15.near_back_ref, f32[3,128]{1,0:T(4,128)S(1)} %collective-permute-done.16.far_back_ref, s32[2,128]{1,0:T(2,128)S(1)} %copy-done.7, ...), custom_call_target="tpu_custom_call" | custom-call | tf_op jit(solution)/shard_map/pallas_call | solution.py:724
  (48 shorter events, 3.9 us)
Async XLA Ops:
  0.6 1.0 %copy-start = (bf16[2,250,512]{2,0,1:T(2,128)(2,1)S(1)}, bf16[2,250,512]{2,0,1:T(2,128)(2,1)}, u32[]{:S(2)}) copy-start(bf16[2,250,512]{2,0,1:T(2,128)(2,1)} %param.18) | copy-start | bytes 1536004
  0.6 5.9 %copy-start.3 = (f32[1,3,512]{2,0,1:T(1,128)S(1)}, f32[1,3,512]{2,0,1:T(1,128)}, u32[]{:S(2)}) copy-start(f32[1,3,512]{2,0,1:T(1,128)} %param.10) | copy-start | bytes 18436
  0.7 5.9 %copy-start.4 = (s32[512]{0:T(512)S(1)}, s32[512]{0:T(512)}, u32[]{:S(2)}) copy-start(s32[512]{0:T(512)} %param.12) | copy-start | bytes 6148
  0.7 5.9 %copy-start.7 = (s32[2,128]{1,0:T(2,128)S(1)}, s32[2,128]{1,0:T(2,128)}, u32[]{:S(2)}) copy-start(s32[2,128]{1,0:T(2,128)} %lists_ref.5) | copy-start | bytes 3076
  0.7 9.2 %copy-start.5 = (s32[512]{0:T(512)S(1)}, s32[512]{0:T(512)}, u32[]{:S(2)}) copy-start(s32[512]{0:T(512)} %param.14) | copy-start | bytes 6148
  0.7 9.2 %copy-start.2 = (s32[32,512]{1,0:T(8,128)S(1)}, s32[32,512]{1,0:T(8,128)}, u32[]{:S(2)}) copy-start(s32[32,512]{1,0:T(8,128)} %neighbours_ref.4) | copy-start | bytes 196612
  0.7 12.4 %copy-start.1 = (f32[2,3,512]{2,0,1:T(2,128)S(1)}, f32[2,3,512]{2,0,1:T(2,128)}, u32[]{:S(2)}) copy-start(f32[2,3,512]{2,0,1:T(2,128)} %param.16) | copy-start | bytes 36868
  0.7 12.4 %copy-start.6 = (f32[2,512]{1,0:T(2,128)S(1)}, f32[2,512]{1,0:T(2,128)}, u32[]{:S(2)}) copy-start(f32[2,512]{1,0:T(2,128)} %shift_ref.3) | copy-start | bytes 12292
  3.4 8.8 %collective-permute-start = (bf16[128,384]{1,0:T(8,128)(2,1)S(1)}, bf16[128,384]{1,0:T(8,128)(2,1)S(1)}, u32[]{:S(2)}, u32[]{:S(2)}) collective-permute-start(bf16[128,384]{1,0:T(8,128)(2,1)S(1)} %get-tuple-element.60), channel_id=1, source_target_pairs={{20,0},{21,1},{22,2},{23,3},{16,4},{17,5},{18,6},{19,7},{28,8},{29... | collective-permute-start | bytes 294920 | tf_op jit(solution)/shard_map/ppermute | solution.py:500
  7.0 5.2 %collective-permute-start.1 = (f32[4,128]{1,0:T(4,128)S(1)}, f32[4,128]{1,0:T(4,128)S(1)}, u32[]{:S(2)}, u32[]{:S(2)}) collective-permute-start(f32[4,128]{1,0:T(4,128)S(1)} %get-tuple-element.62), channel_id=1, source_target_pairs={{120,0},{16,8},{8,16},{32,24},{24,32},{48,40},{40,48},{64,56},{56,... | collective-permute-start | bytes 6152 | tf_op jit(solution)/shard_map/ppermute | solution.py:486
  9.8 2.4 %collective-permute-start.2 = (f32[4,128]{1,0:T(4,128)S(1)}, f32[4,128]{1,0:T(4,128)S(1)}, u32[]{:S(2)}, u32[]{:S(2)}) collective-permute-start(f32[4,128]{1,0:T(4,128)S(1)} %get-tuple-element.64), channel_id=1, source_target_pairs={{8,0},{0,8},{24,16},{16,24},{40,32},{32,40},{56,48},{48,56},{72,64... | collective-permute-start | bytes 6152 | tf_op jit(solution)/shard_map/ppermute | solution.py:486
  12.2 5.1 %collective-permute-start.3 = (bf16[128,384]{1,0:T(8,128)(2,1)S(1)}, bf16[128,384]{1,0:T(8,128)(2,1)S(1)}, u32[]{:S(2)}, u32[]{:S(2)}) collective-permute-start(bf16[128,384]{1,0:T(8,128)(2,1)S(1)} %get-tuple-element.67), channel_id=1, source_target_pairs={{1,0},{0,1},{3,2},{2,3},{5,4},{4,5},{7,6},{6,7},{9,8},{8,9},{11,10... | collective-permute-start | bytes 294920 | tf_op jit(solution)/shard_map/ppermute | solution.py:486
  17.4 5.9 %collective-permute-start.4 = (bf16[128,384]{1,0:T(8,128)(2,1)S(1)}, bf16[128,384]{1,0:T(8,128)(2,1)S(1)}, u32[]{:S(2)}, u32[]{:S(2)}) collective-permute-start(bf16[128,384]{1,0:T(8,128)(2,1)S(1)} %get-tuple-element.71), channel_id=1, source_target_pairs={{3,0},{2,1},{1,2},{0,3},{7,4},{6,5},{5,6},{4,7},{11,8},{10,9},{9,1... | collective-permute-start | bytes 294920 | tf_op jit(solution)/shard_map/ppermute | solution.py:486
  23.3 7.4 %collective-permute-start.8 = (bf16[128,384]{1,0:T(8,128)(2,1)S(1)}, bf16[128,384]{1,0:T(8,128)(2,1)S(1)}, u32[]{:S(2)}, u32[]{:S(2)}) collective-permute-start(bf16[128,384]{1,0:T(8,128)(2,1)S(1)} %shard_map.122.refs_0_), channel_id=1, source_target_pairs={{32,0},{40,8},{48,16},{56,24},{64,32},{72,40},{80,48},{88,56},{96,... | collective-permute-start | bytes 294920 | tf_op jit(solution)/shard_map/ppermute | solution.py:486
  25.8 6.2 %collective-permute-start.7 = (bf16[128,384]{1,0:T(8,128)(2,1)S(1)}, bf16[128,384]{1,0:T(8,128)(2,1)S(1)}, u32[]{:S(2)}, u32[]{:S(2)}) collective-permute-start(bf16[128,384]{1,0:T(8,128)(2,1)S(1)} %shard_map.122.refs_0_), channel_id=1, source_target_pairs={{64,0},{72,8},{80,16},{88,24},{96,32},{104,40},{112,48},{120,56},{... | collective-permute-start | bytes 294920 | tf_op jit(solution)/shard_map/ppermute | solution.py:486
  25.8 6.9 %collective-permute-start.5 = (bf16[128,384]{1,0:T(8,128)(2,1)S(1)}, bf16[128,384]{1,0:T(8,128)(2,1)S(1)}, u32[]{:S(2)}, u32[]{:S(2)}) collective-permute-start(bf16[128,384]{1,0:T(8,128)(2,1)S(1)} %shard_map.122.refs_0_), channel_id=1, source_target_pairs={{96,0},{104,8},{112,16},{120,24},{0,32},{8,40},{16,48},{24,56},{32... | collective-permute-start | bytes 294920 | tf_op jit(solution)/shard_map/ppermute | solution.py:486
  27.0 3.6 %collective-permute-start.6 = (f32[3,1,512]{2,1,0:T(1,128)S(1)}, f32[3,1,512]{2,1,0:T(1,128)S(1)}, u32[]{:S(2)}, u32[]{:S(2)}) collective-permute-start(f32[3,1,512]{2,1,0:T(1,128)S(1)} %bitcast.23), channel_id=1, source_target_pairs={{1,0},{0,1},{3,2},{2,3},{5,4},{4,5},{7,6},{6,7},{9,8},{8,9},{11,10... | collective-permute-start | bytes 18440 | tf_op jit(solution)/shard_map/ppermute | solution.py:486
  32.8 2.0 %collective-permute-start.9 = (bf16[512,512]{1,0:T(8,128)(2,1)S(1)}, bf16[512,512]{1,0:T(8,128)(2,1)S(1)}, u32[]{:S(2)}, u32[]{:S(2)}) collective-permute-start(bf16[512,512]{1,0:T(8,128)(2,1)S(1)} %shard_map.124.half_ref), channel_id=1, source_target_pairs={{8,0},{0,8},{24,16},{16,24},{40,32},{32,40},{56,48},{48,56},{72,64... | collective-permute-start | bytes 1572872 | tf_op jit(solution)/shard_map/ppermute | solution.py:486
  32.9 9.6 %collective-permute-start.12 = (f32[3,1,512]{2,1,0:T(1,128)S(1)}, f32[3,1,512]{2,1,0:T(1,128)S(1)}, u32[]{:S(2)}, u32[]{:S(2)}) collective-permute-start(f32[3,1,512]{2,1,0:T(1,128)S(1)} %bitcast.24), channel_id=1, source_target_pairs={{7,0},{2,1},{1,2},{4,3},{3,4},{6,5},{5,6},{0,7},{15,8},{10,9},{9,1... | collective-permute-start | bytes 18440 | tf_op jit(solution)/shard_map/ppermute | solution.py:486
  37.6 5.0 %collective-permute-start.10 = (f32[3,128]{1,0:T(4,128)S(1)}, f32[3,128]{1,0:T(4,128)S(1)}, u32[]{:S(2)}, u32[]{:S(2)}) collective-permute-start(f32[3,128]{1,0:T(4,128)S(1)} %get-tuple-element.92), channel_id=1, source_target_pairs={{8,0},{0,8},{24,16},{16,24},{40,32},{32,40},{56,48},{48,56},{72,64... | collective-permute-start | bytes 4616 | tf_op jit(solution)/shard_map/ppermute | solution.py:486
  37.8 5.1 %collective-permute-start.11 = (f32[3,128]{1,0:T(4,128)S(1)}, f32[3,128]{1,0:T(4,128)S(1)}, u32[]{:S(2)}, u32[]{:S(2)}) collective-permute-start(f32[3,128]{1,0:T(4,128)S(1)} %get-tuple-element.93), channel_id=1, source_target_pairs={{120,0},{16,8},{8,16},{32,24},{24,32},{48,40},{40,48},{64,56},{56,... | collective-permute-start | bytes 4616 | tf_op jit(solution)/shard_map/ppermute | solution.py:486
  39.0 3.9 %copy-start.8 = (f32[1,3,512]{2,0,1:T(1,128)S(1)}, f32[1,3,512]{2,0,1:T(1,128)}, u32[]{:S(2)}) copy-start(f32[1,3,512]{2,0,1:T(1,128)} %param.11) | copy-start | bytes 18436
  43.8 5.6 %collective-permute-start.13 = (f32[4,128]{1,0:T(4,128)S(1)}, f32[4,128]{1,0:T(4,128)S(1)}, u32[]{:S(2)}, u32[]{:S(2)}) collective-permute-start(f32[4,128]{1,0:T(4,128)S(1)} %get-tuple-element.96), channel_id=1, source_target_pairs={{8,0},{0,8},{24,16},{16,24},{40,32},{32,40},{56,48},{48,56},{72,64... | collective-permute-start | bytes 6152 | tf_op jit(solution)/shard_map/ppermute | solution.py:486
  43.9 5.5 %collective-permute-start.14 = (f32[4,128]{1,0:T(4,128)S(1)}, f32[4,128]{1,0:T(4,128)S(1)}, u32[]{:S(2)}, u32[]{:S(2)}) collective-permute-start(f32[4,128]{1,0:T(4,128)S(1)} %get-tuple-element.97), channel_id=1, source_target_pairs={{120,0},{16,8},{8,16},{32,24},{24,32},{48,40},{40,48},{64,56},{56,... | collective-permute-start | bytes 6152 | tf_op jit(solution)/shard_map/ppermute | solution.py:486
  49.4 15.7 %collective-permute-start.18 = (f32[3,1,512]{2,1,0:T(1,128)S(1)}, f32[3,1,512]{2,1,0:T(1,128)S(1)}, u32[]{:S(2)}, u32[]{:S(2)}) collective-permute-start(f32[3,1,512]{2,1,0:T(1,128)S(1)} %get-tuple-element.113.position_ref), channel_id=1, source_target_pairs={{1,0},{0,1},{3,2},{2,3},{5,4},{4,5},{7,6},{6,7},{9,8},{8,9},{11,10... | collective-permute-start | bytes 18440 | tf_op jit(solution)/shard_map/ppermute | solution.py:486
  52.7 12.4 %collective-permute-start.17 = (f32[3,1,512]{2,1,0:T(1,128)S(1)}, f32[3,1,512]{2,1,0:T(1,128)S(1)}, u32[]{:S(2)}, u32[]{:S(2)}) collective-permute-start(f32[3,1,512]{2,1,0:T(1,128)S(1)} %get-tuple-element.113.position_ref), channel_id=1, source_target_pairs={{7,0},{2,1},{1,2},{4,3},{3,4},{6,5},{5,6},{0,7},{15,8},{10,9},{9,1... | collective-permute-start | bytes 18440 | tf_op jit(solution)/shard_map/ppermute | solution.py:486
  59.5 5.1 %collective-permute-start.15 = (f32[3,128]{1,0:T(4,128)S(1)}, f32[3,128]{1,0:T(4,128)S(1)}, u32[]{:S(2)}, u32[]{:S(2)}) collective-permute-start(f32[3,128]{1,0:T(4,128)S(1)} %get-tuple-element.109), channel_id=1, source_target_pairs={{8,0},{0,8},{24,16},{16,24},{40,32},{32,40},{56,48},{48,56},{72,64... | collective-permute-start | bytes 4616 | tf_op jit(solution)/shard_map/ppermute | solution.py:486
  59.6 5.5 %collective-permute-start.16 = (f32[3,128]{1,0:T(4,128)S(1)}, f32[3,128]{1,0:T(4,128)S(1)}, u32[]{:S(2)}, u32[]{:S(2)}) collective-permute-start(f32[3,128]{1,0:T(4,128)S(1)} %get-tuple-element.110), channel_id=1, source_target_pairs={{120,0},{16,8},{8,16},{32,24},{24,32},{48,40},{40,48},{64,56},{56,... | collective-permute-start | bytes 4616 | tf_op jit(solution)/shard_map/ppermute | solution.py:486
